TPU v7x, 512 devices: a whole 4x8x8 slice. The times are simulated.
512 devices in a mesh: depth: 8 (over y), lat: 16 (over z_lo, x, core), tx: 4 (over z_hi).
Axes of the slice: x: 4, y: 8, z: 8 (z_hi: 4, z_lo: 2; z = z_hi * 2 + z_lo), core: 2. Of those that a mesh axis runs over, the one named last changes fastest.
Arguments:
- conductivity: float32 [16, 128, 512], P('depth', 'lat'), may hold values from 0.1 to 10
- field_guess: float32 [4, 2, 2, 3, 16, 128, 512], P('tx', None, None, None, 'depth', 'lat'), may hold values from -56 to 56, as said below
- tx_cell: int32 [4], P('tx'), may hold values from 0 to 1048575
- rx_cell: int32 [4, 64], P('tx'), may hold values from 0 to 1048575
- rx_weight: float32 [4, 64, 2], P('tx'), may hold values from -16 to 16
Outputs:
- fields: float32 [4, 2, 2, 3, 16, 128, 512], P('tx', None, None, None, 'depth', 'lat')
- gradient: float32 [16, 128, 512], P('depth', 'lat', 'tx')
Inputs may be any that keep to these rules, and one draw needn't show every extreme that they name: `tx_cell`: a cell number (z * 128 + x) * 512 + y. `rx_cell`: cell numbers (z * 128 + x) * 512 + y; two receivers may share a cell. `field_guess`: a starting field.
All inputs are finite; a program needn't handle non-finite values.
Results may differ from a plain program's by a relative error of at most 0.0001.
Values sent between devices are 32-bit elements; how exact they have to be, the bound alone decides.
No kernel may reach another device: no remote copies, remote signals or barrier semaphores. Data moves between devices by JAX's collectives and lax.ppermute only.
A program may use at most 64 MiB of HBM per device.

v0:
```python
import jax
import jax.numpy as jnp
from jax import lax
from jax.sharding import PartitionSpec as P

ITERS = 2


source_amplitude = 20.0


def with_halo(cells, sides, width):
    for axis, dim in sides:
        count = lax.axis_size(axis)
        ends = count - 1
        head = lax.slice_in_dim(cells, 0, width, axis=dim)
        tail = lax.slice_in_dim(cells, cells.shape[dim] - width, cells.shape[dim], axis=dim)
        cells = jnp.concatenate(
            [
                lax.ppermute(tail, axis, [(i, (i + 1) % count) for i in range(ends)]),
                cells,
                lax.ppermute(head, axis, [((i + 1) % count, i) for i in range(ends)]),
            ],
            axis=dim,
        )
    return cells


def step_ahead(values, plane, along_axis):
    length = values.shape[along_axis]
    return (
        jnp.concatenate(
            [lax.slice_in_dim(values, 1, length, axis=along_axis), plane], axis=along_axis
        )
        - values
    )


def step_behind(values, plane, along_axis):
    length = values.shape[along_axis]
    return values - jnp.concatenate(
        [plane, lax.slice_in_dim(values, 0, length - 1, axis=along_axis)], axis=along_axis
    )


def curl_pair(electric, depth_plane, lat_plane, difference):

    def along(component, direction_axis):
        values = electric[:, :, component]
        if direction_axis == 2:
            plane = depth_plane[:, :, component]
        elif direction_axis == 3:
            plane = lat_plane[:, :, component]
        else:
            plane = jnp.zeros_like(values[..., :1])
        return difference(values, plane, direction_axis)

    out_depth = along(2, 3) - along(1, 4)
    out_lat = along(0, 4) - along(2, 2)
    out_span = along(1, 2) - along(0, 3)
    return jnp.stack([out_depth, out_lat, out_span], axis=2)


def inner_local(left_side, right_side):
    real_part = jnp.sum(
        left_side[:, 0] * right_side[:, 0] + left_side[:, 1] * right_side[:, 1], axis=(1, 2, 3, 4)
    )
    imag_part = jnp.sum(
        left_side[:, 0] * right_side[:, 1] - left_side[:, 1] * right_side[:, 0], axis=(1, 2, 3, 4)
    )
    return (real_part, imag_part)


def complex_product(first_pair, second_pair):
    return (
        first_pair[0] * second_pair[0] - first_pair[1] * second_pair[1],
        first_pair[0] * second_pair[1] + first_pair[1] * second_pair[0],
    )


def complex_quotient(first_pair, second_pair):
    denominator = second_pair[0] * second_pair[0] + second_pair[1] * second_pair[1]
    return (
        (first_pair[0] * second_pair[0] + first_pair[1] * second_pair[1]) / denominator,
        (first_pair[1] * second_pair[0] - first_pair[0] * second_pair[1]) / denominator,
    )


def scale_field(factor, electric):
    real_factor = factor[0].reshape(-1, 1, 1, 1, 1)
    imag_factor = factor[1].reshape(-1, 1, 1, 1, 1)
    real_part = real_factor * electric[:, 0] - imag_factor * electric[:, 1]
    imag_part = real_factor * electric[:, 1] + imag_factor * electric[:, 0]
    return jnp.stack([real_part, imag_part], axis=1)


def local(conductivity, field_guess, tx_cell, rx_cell, rx_weight):
    depth_cells, lat_cells, width = conductivity.shape
    depth_index = lax.axis_index("depth")
    lat_index = lax.axis_index("lat")
    total_lat = lat_cells * lax.axis_size("lat")
    depth_keep = (depth_index > 0).astype(jnp.float32)
    lat_keep = (lat_index > 0).astype(jnp.float32)
    local_total = depth_cells * lat_cells * width

    def apply_operator(electric):
        padded = with_halo(electric, (("depth", 3), ("lat", 4)), 1)
        inner_block = padded[:, :, :, : depth_cells + 1, : lat_cells + 1]
        depth_ahead = padded[:, :, :, depth_cells + 1 :, : lat_cells + 1]
        lat_ahead = padded[:, :, :, : depth_cells + 1, lat_cells + 1 :]
        magnetic = curl_pair(inner_block, depth_ahead, lat_ahead, step_ahead)
        depth_behind = magnetic[:, :, :, :1, 1:] * depth_keep
        lat_behind = magnetic[:, :, :, 1:, :1] * lat_keep
        curled = curl_pair(magnetic[:, :, :, 1:, 1:], depth_behind, lat_behind, step_behind)
        real_part = curled[:, 0] - conductivity * electric[:, 1]
        imag_part = curled[:, 1] + conductivity * electric[:, 0]
        return jnp.stack([real_part, imag_part], axis=1)

    def place(cell_ids, amounts):
        depth_pos = cell_ids // (total_lat * width)
        lat_pos = cell_ids // width % total_lat
        span_pos = cell_ids % width
        local_depth = depth_pos - depth_index * depth_cells
        local_lat = lat_pos - lat_index * lat_cells
        inside = (
            (local_depth >= 0)
            & (local_depth < depth_cells)
            & (local_lat >= 0)
            & (local_lat < lat_cells)
        )
        local_flat = jnp.where(
            inside, (local_depth * lat_cells + local_lat) * width + span_pos, local_total
        )
        plane = jnp.zeros((local_total,), jnp.float32).at[local_flat].add(amounts, mode="drop")
        return plane.reshape(depth_cells, lat_cells, width)

    blank_plane = jnp.zeros((depth_cells, lat_cells, width), jnp.float32)
    tx_plane = place(tx_cell, jnp.full((1,), -source_amplitude, jnp.float32))
    rx_real = place(rx_cell[0], rx_weight[0, :, 0])
    rx_imag = place(rx_cell[0], rx_weight[0, :, 1])
    tx_side = jnp.stack(
        [
            jnp.stack([blank_plane, blank_plane, blank_plane]),
            jnp.stack([tx_plane, blank_plane, blank_plane]),
        ]
    )
    rx_side = jnp.stack(
        [
            jnp.stack([rx_real, blank_plane, blank_plane]),
            jnp.stack([rx_imag, blank_plane, blank_plane]),
        ]
    )
    start_field = field_guess[0]
    solution = start_field
    residual = jnp.stack([tx_side, rx_side]) - apply_operator(start_field)
    shadow = residual
    direction = residual
    start_pair = inner_local(shadow, residual)
    shadow_dot = lax.psum((start_pair[0], start_pair[1]), ("depth", "lat"))
    for iteration in range(ITERS):
        applied = apply_operator(direction)
        curve_pair = inner_local(shadow, applied)
        curve_sum = lax.psum((curve_pair[0], curve_pair[1]), ("depth", "lat"))
        step_length = complex_quotient(shadow_dot, curve_sum)
        halfway = residual - scale_field(step_length, applied)
        second = apply_operator(halfway)
        cross_pair = inner_local(second, halfway)
        energy = jnp.sum(second * second, axis=(1, 2, 3, 4, 5))
        cross_real, cross_imag, energy_sum = lax.psum(
            (cross_pair[0], cross_pair[1], energy), ("depth", "lat")
        )
        relax_weight = (cross_real / energy_sum, cross_imag / energy_sum)
        solution = (
            solution + scale_field(step_length, direction) + scale_field(relax_weight, halfway)
        )
        residual = halfway - scale_field(relax_weight, second)
        if iteration + 1 < ITERS:
            next_pair = inner_local(shadow, residual)
            new_dot = lax.psum((next_pair[0], next_pair[1]), ("depth", "lat"))
            mixing = complex_product(
                complex_quotient(new_dot, shadow_dot), complex_quotient(step_length, relax_weight)
            )
            direction = residual + scale_field(
                mixing, direction - scale_field(relax_weight, applied)
            )
            shadow_dot = new_dot
    solutions = [solution]
    fields = jnp.stack(solutions)
    term = jnp.sum(
        fields[:, 0, 0] * fields[:, 1, 0] - fields[:, 0, 1] * fields[:, 1, 1], axis=(0, 1)
    )
    gradient = lax.psum_scatter(term, "tx", scatter_dimension=2, tiled=True)
    return (fields, gradient)


def solution(mesh):
    return jax.shard_map(
        local,
        mesh=mesh,
        in_specs=(
            P("depth", "lat", None),
            P("tx", None, None, None, "depth", "lat", None),
            P("tx"),
            P("tx", None),
            P("tx", None, None),
        ),
        out_specs=(P("tx", None, None, None, "depth", "lat", None), P("depth", "lat", "tx")),
        check_vma=False,
    )
```

profile of v0, /device:TPU:6, one launch (start us, length us, event | category | flops | bytes accessed | tf_op | source)
XLA Modules:
  0.0 1536.5 jit_solution(4327882843322564249)
XLA Ops:
  8.6 3.5 collective-permute-start
  16.2 4.1 collective-permute-done.1
  20.7 1.9 collective-permute-start.2
  26.0 3.6 collective-permute-start.3
  35.3 3.5 collective-permute-start.4
  41.9 5.0 collective-permute-done.5
  47.3 5.4 collective-permute-start.6
  52.7 1.9 collective-permute-start.7
  59.9 259.2 %all-reduce.28 = (f32[2]{0:T(128)S(1)}, f32[2]{0:T(128)S(1)}, f32[2]{0:T(128)S(1)}, f32[2]{0:T(128)S(1)}) all-reduce(f32[2]{0:T(128)S(1)} %get-tuple-element.35, f32[2]{0:T(128)S(1)} %get-tuple-element.29, f32[2]{0:T(128)S(1)} %get-tuple-element.34, f32[2]{0:T(128)S(1)} %get-tuple-element.28), channel_id=1, replica_groups=mesh['depth'=8,'lat'=16,'tx'=4] {'depth','lat'}, use_global_device_ids=true, to_apply=%region_3.4 | all-reduce | flops 8 | bytes 64 | tf_op jit(solution)/shard_map/psum | solution.py:159
  325.4 4.2 collective-permute-done.9
  329.7 1.9 collective-permute-start.10
  331.6 3.6 collective-permute-start.11
  340.0 272.7 %all-reduce.27 = (f32[2]{0:T(128)S(1)}, f32[2]{0:T(128)S(1)}, f32[2]{0:T(128)S(1)}) all-reduce(f32[2]{0:T(128)S(1)} %get-tuple-element.27, f32[2]{0:T(128)S(1)} %fusion.8, f32[2]{0:T(128)S(1)} %get-tuple-element.26), channel_id=1, replica_groups=mesh['depth'=8,'lat'=16,'tx'=4] {'depth','lat'}, use_global_device_ids=true, to_apply=%region_15.16 | all-reduce | flops 6 | bytes 48 | tf_op jit(solution)/shard_map/psum | solution.py:169
  614.1 275.6 %all-reduce.26 = (f32[2]{0:T(128)S(1)}, f32[2]{0:T(128)S(1)}) all-reduce(f32[2]{0:T(128)S(1)} %get-tuple-element.33, f32[2]{0:T(128)S(1)} %get-tuple-element.32), channel_id=1, replica_groups=mesh['depth'=8,'lat'=16,'tx'=4] {'depth','lat'}, use_global_device_ids=true, to_apply=%region_17.18 | all-reduce | flops 4 | bytes 32 | tf_op jit(solution)/shard_map/psum | solution.py:179
  892.5 3.1 collective-permute-done.12
  895.7 4.1 collective-permute-done.13
  899.9 1.9 collective-permute-start.14
  901.9 7.0 collective-permute-start.15
  912.9 271.3 %all-reduce.25 = (f32[2]{0:T(128)S(1)}, f32[2]{0:T(128)S(1)}) all-reduce(f32[2]{0:T(128)S(1)} %get-tuple-element.25, f32[2]{0:T(128)S(1)} %get-tuple-element.24), channel_id=1, replica_groups=mesh['depth'=8,'lat'=16,'tx'=4] {'depth','lat'}, use_global_device_ids=true, to_apply=%region_23.24 | all-reduce | flops 4 | bytes 32 | tf_op jit(solution)/shard_map/psum | solution.py:163
  1189.5 4.3 collective-permute-done.17
  1193.9 1.9 collective-permute-start.18
  1195.9 4.6 collective-permute-start.19
  1205.4 272.2 %all-reduce.24 = (f32[2]{0:T(128)S(1)}, f32[2]{0:T(128)S(1)}, f32[2]{0:T(128)S(1)}) all-reduce(f32[2]{0:T(128)S(1)} %get-tuple-element.31, f32[2]{0:T(128)S(1)} %fusion.14, f32[2]{0:T(128)S(1)} %get-tuple-element.30), channel_id=1, replica_groups=mesh['depth'=8,'lat'=16,'tx'=4] {'depth','lat'}, use_global_device_ids=true, to_apply=%region_25.26 | all-reduce | flops 6 | bytes 48 | tf_op jit(solution)/shard_map/psum | solution.py:169
  1479.5 50.1 %reduce-scatter.2.cloned.1.call-done = f32[2,8,128]{2,1,0:T(8,128)} async-done(((f32[2,8,512]{2,1,0:T(8,128)}), f32[2,8,128]{2,1,0:T(8,128)}) %reduce-scatter.2.cloned.1.call-update) | async-done | bytes 8208 | tf_op jit(solution)/shard_map/reduce_scatter | solution.py:192
  (272 shorter events, 52.9 us)
Async XLA Ops:
  7.2 1522.5 %reduce-scatter.2.cloned.1.call-start = ((), (), s32[]{:S(2)}) async-start(), calls=%async_computation.1 | async-start | bytes 40960 | tf_op jit(solution)/shard_map/reduce_scatter | solution.py:192
  8.6 7.6 collective-permute-start
  12.1 8.3 collective-permute-start.1
  20.7 8.9 collective-permute-start.2
  26.0 5.8 collective-permute-start.3
  35.3 6.7 collective-permute-start.4
  38.8 8.2 collective-permute-start.5
  47.3 7.3 collective-permute-start.6
  52.7 4.5 collective-permute-start.7
  320.6 4.5 collective-permute-start.8
  322.1 7.6 collective-permute-start.9
  329.7 5.9 collective-permute-start.10
  331.6 5.8 collective-permute-start.11
  889.9 5.7 collective-permute-start.12
  891.2 8.6 collective-permute-start.13
  899.9 9.3 collective-permute-start.14
  901.9 9.2 collective-permute-start.15
  1184.7 4.5 collective-permute-start.16
  1186.3 7.6 collective-permute-start.17
  1193.9 6.6 collective-permute-start.18
  1195.9 6.6 collective-permute-start.19
  1205.0 272.8 %copy-start.1 = (f32[1,2,2,3,2,8,512]{6,5,4,3,2,1,0:T(8,128)S(1)}, f32[1,2,2,3,2,8,512]{6,5,4,3,2,1,0:T(8,128)}, u32[]{:S(2)}) copy-start(f32[1,2,2,3,2,8,512]{6,5,4,3,2,1,0:T(8,128)} %param.8) | copy-start | bytes 1179652
  1205.1 272.8 %copy-start.2 = (f32[1,2,1,3,2,8,512]{6,5,1,4,3,2,0:T(8,128)S(1)}, f32[1,2,1,3,2,8,512]{6,5,1,4,3,2,0:T(8,128)}, u32[]{:S(2)}) copy-start(f32[1,2,1,3,2,8,512]{6,5,1,4,3,2,0:T(8,128)} %get-tuple-element.103) | copy-start | bytes 589828
  1205.1 272.8 %copy-start.3 = (f32[1,2,1,3,2,8,512]{6,5,1,4,3,2,0:T(8,128)S(1)}, f32[1,2,1,3,2,8,512]{6,5,1,4,3,2,0:T(8,128)}, u32[]{:S(2)}) copy-start(f32[1,2,1,3,2,8,512]{6,5,1,4,3,2,0:T(8,128)} %get-tuple-element.181) | copy-start | bytes 589828
  (6 other events, 21.4 us)
Sparse Core Ops, SparseCore 0:
  1478.9 50.7 reduce-scatter.1
where the time goes:
time: 1540 us
  blocking collectives  1350 us (88%)
  waiting for transfers between devices  86.8 us (6%)
  starting transfers between devices  51.2 us (3%)
  other arithmetic  20.6 us (1%)
  between operations  16.9 us (1%)
    psum x2, blocking collectives, local(): lax.psum((cross_pair[0], cross_pair[1], energy), ('depth', 'lat'))  545 us
    psum x1, blocking collectives, local(): new_dot = lax.psum((next_pair[0], next_pair[1]), ('depth', 'lat'))  276 us
    psum x1, blocking collectives, local(): curve_sum = lax.psum((curve_pair[0], curve_pair[1]), ('depth', 'lat'))  271 us
    psum x1, blocking collectives, local(): shadow_dot = lax.psum((start_pair[0], start_pair[1]), ('depth', 'lat'))  259 us
    reduce_scatter x1, waiting for transfers between devices, local(): gradient = lax.psum_scatter(term, 'tx', scatter_dimension=2, tiled=True)  50.1 us
  transfers between devices with their start and end apart: 21, of which 19 were waited for; matrix products, arithmetic and copies ran while one was open for 1% of the time, Pallas kernels for 0%

commit v1 on v0

v1 whole, which is shorter than its diff:
```python
import functools

import jax
import jax.numpy as jnp
from jax import lax
from jax.experimental import pallas as pl
from jax.experimental.pallas import tpu as pltpu
from jax.sharding import PartitionSpec as P

SOURCE = 20.0
KINDS = 2
BASIS = 5
ROWS = 8
LANES = 128
GRID_AXES = ("depth", "lat")
PAIRS = [(i, j) for i in range(BASIS) for j in range(i, BASIS)]
ENTRIES = [(i, j, part) for i, j in PAIRS for part in range(1 if i == j else 2)]
MIB = 1 << 20


def in_vmem():
    return pl.BlockSpec(memory_space=pltpu.VMEM)


def in_smem():
    return pl.BlockSpec(memory_space=pltpu.SMEM)


def slot(part, component, layer):
    return (part * 3 + component) * 2 + layer


def pack_kernel(pieces, guess_ref, cond_ref, out_ref):
    lane = lax.broadcasted_iota(jnp.int32, (ROWS, LANES), 1)
    blank = jnp.zeros((ROWS, LANES), jnp.float32)
    for kind in range(KINDS):
        for piece in range(pieces):
            to = kind * pieces + piece
            edges = [blank, blank]
            for item in range(14):

                def tile(number):
                    if number < 0 or number >= pieces:
                        return blank
                    cols = slice(number * LANES, (number + 1) * LANES)
                    if item < 12:
                        return guess_ref[kind * 12 + item, :, cols]
                    return cond_ref[item - 12, :, cols]

                out_ref[to, item] = tile(piece)
                ends = jnp.where(lane >= LANES // 2, tile(piece - 1), tile(piece + 1))
                place = item % 8
                moved = pltpu.roll(ends, (16 * place + 8) % LANES, 1)
                edges[item // 8] = jnp.where(lane // 16 == place, moved, edges[item // 8])
            out_ref[to, 14] = edges[0]
            out_ref[to, 15] = edges[1]


def two_sum(a, b):
    total = a + b
    other = total - a
    return total, (a - (total - other)) + (b - other)


def basis_kernel(
    sizes, tx_ref, rx_ref, weight_ref, left_ref, mid_ref, right_ref, basis_ref, gram_ref,
    field, curl, cond, inside, acc,
):
    depths, lats, pieces = sizes
    layers = 2 * depths
    wide = 3 * ROWS
    span = 2 * LANES
    depth_index = lax.axis_index("depth")
    lat_index = lax.axis_index("lat")
    kind = depth_index // pieces
    piece = depth_index % pieces
    lane = lax.broadcasted_iota(jnp.int32, (ROWS, LANES), 1)
    blank = jnp.zeros((ROWS, LANES), jnp.float32)

    row_w = lax.broadcasted_iota(jnp.int32, (wide, span), 0)
    lane_w = lax.broadcasted_iota(jnp.int32, (wide, span), 1)
    x_at = lat_index * ROWS - ROWS + row_w
    y_at = piece * LANES + jnp.where(lane_w >= LANES + 64, lane_w - span, lane_w)
    good = (x_at >= 0) & (x_at < lats * ROWS) & (y_at >= 0) & (y_at < pieces * LANES)
    inside[...] = jnp.where(good, 1.0, 0.0)

    for number, ref in enumerate((left_ref, mid_ref, right_ref)):
        rows = slice(number * ROWS, (number + 1) * ROWS)

        def spread(source, carry, ref=ref, rows=rows):
            for item in range(14):
                place = item % 8
                edge = pltpu.roll(ref[source, 14 + item // 8], LANES - (16 * place + 8), 1)
                edge = jnp.where((lane < 8) | (lane >= LANES - 8), edge, blank)
                body = ref[source, item]
                z = 2 * source + item % 2
                if item < 12:
                    field[0, item // 2, z, rows, 0:LANES] = body
                    field[0, item // 2, z, rows, LANES:span] = edge
                else:
                    cond[z, rows, 0:LANES] = body
                    cond[z, rows, LANES:span] = edge
            return carry

        lax.fori_loop(0, depths, spread, 0)

    empty = jnp.zeros((wide, span), jnp.float32)
    for number in range(BASIS):
        for component in range(6):
            field[number, component, layers] = empty

    def ahead(values, axis):
        return pltpu.roll(values, values.shape[axis] - 1, axis) - values

    def behind(values, axis):
        return values - pltpu.roll(values, 1, axis)

    for step in range(BASIS):
        for component in range(4):
            curl[component] = empty

        def apply_layer(z, carry, step=step):
            keep = inside[...]
            sigma = cond[z]
            for part in range(2):
                uz = field[step, part * 3, z]
                ux = field[step, part * 3 + 1, z]
                uy = field[step, part * 3 + 2, z]
                dz_ux = field[step, part * 3 + 1, z + 1] - ux
                dz_uy = field[step, part * 3 + 2, z + 1] - uy
                hz = (ahead(uy, 0) - ahead(ux, 1)) * keep
                hx = (ahead(uz, 1) - dz_uy) * keep
                hy = (dz_ux - ahead(uz, 0)) * keep
                dz_hx = hx - curl[part * 2]
                dz_hy = hy - curl[part * 2 + 1]
                curl[part * 2] = hx
                curl[part * 2 + 1] = hy
                outs = (
                    behind(hy, 0) - behind(hx, 1),
                    behind(hz, 1) - dz_hy,
                    dz_hx - behind(hz, 0),
                )
                for component, value in enumerate(outs):
                    other = sigma * field[step, (1 - part) * 3 + component, z]
                    value = value - other if part == 0 else value + other
                    if step == 0:
                        value = -value
                    field[step + 1, part * 3 + component, z] = value * keep
            return carry

        lax.fori_loop(0, layers, apply_layer, 0)

        if step == 0:
            line = lax.broadcasted_iota(jnp.int32, (1, span), 1)

            def add_source(cell, real, imag):
                y = cell % (pieces * LANES)
                x = cell // (pieces * LANES) % (lats * ROWS)
                z = cell // (pieces * LANES * lats * ROWS)
                row = x - lat_index * ROWS + ROWS
                col = y - piece * LANES

                @pl.when((row >= 0) & (row < wide) & (col >= -8) & (col < LANES + 8))
                def _():
                    hit = line == jnp.where(col < 0, col + span, col)
                    at = pl.ds(row, 1)
                    field[1, 0, z, at] = field[1, 0, z, at] + jnp.where(hit, real, 0.0)
                    field[1, 3, z, at] = field[1, 3, z, at] + jnp.where(hit, imag, 0.0)

            @pl.when(kind == 0)
            def _():
                add_source(tx_ref[0], jnp.float32(0.0), jnp.float32(-SOURCE))

            @pl.when(kind == 1)
            def _():
                def each(r, carry):
                    add_source(rx_ref[0, r], weight_ref[0, 2 * r], weight_ref[0, 2 * r + 1])
                    return carry

                lax.fori_loop(0, rx_ref.shape[1], each, 0)

    for entry in range(2 * len(ENTRIES)):
        acc[entry] = blank
    own = slice(ROWS, 2 * ROWS)

    def gram_layer(source, carry):
        for layer in range(2):
            z = 2 * source + layer
            tiles = [[field[b + 1, c, z, own, 0:LANES] for c in range(6)] for b in range(BASIS)]
            for b in range(BASIS - 1):
                for c in range(6):
                    basis_ref[b, source, 2 * c + layer] = tiles[b][c]
            for entry, (i, j, part) in enumerate(ENTRIES):
                first, second = tiles[i], tiles[j]
                if part == 0:
                    terms = [first[c] * second[c] for c in range(6)]
                    value = (terms[0] + terms[3]) + (terms[1] + terms[4]) + (terms[2] + terms[5])
                else:
                    terms = [first[c] * second[c + 3] - first[c + 3] * second[c] for c in range(3)]
                    value = terms[0] + terms[1] + terms[2]
                total, error = two_sum(acc[2 * entry], value)
                acc[2 * entry] = total
                acc[2 * entry + 1] = acc[2 * entry + 1] + error
        return carry

    lax.fori_loop(0, depths, gram_layer, 0)

    def fold(high, low, shift, axis):
        total, error = two_sum(high, pltpu.roll(high, shift, axis))
        return total, low + pltpu.roll(low, shift, axis) + error

    sub = lax.broadcasted_iota(jnp.int32, (ROWS, LANES), 0)
    row = blank
    for start in range(0, len(ENTRIES), 8):
        highs, lows = blank, blank
        for entry in range(start, min(start + 8, len(ENTRIES))):
            high, low = acc[2 * entry], acc[2 * entry + 1]
            for shift in (4, 2, 1):
                high, low = fold(high, low, shift, 0)
            highs = jnp.where(sub == entry - start, high, highs)
            lows = jnp.where(sub == entry - start, low, lows)
        for shift in (64, 32, 16, 8, 4, 2, 1):
            highs, lows = fold(highs, lows, shift, 1)
        row = jnp.where(lane == sub + start, highs, row)
        row = jnp.where(lane == sub + start + 64, lows, row)
    for shift in (4, 2, 1):
        row = row + pltpu.roll(row, shift, 0)
    for number in range(depths * lats // ROWS):
        gram_ref[number * ROWS : (number + 1) * ROWS] = row


def quick(a, b):
    total = a + b
    return total, b - (total - a)


def split(a):
    big = a * 4097.0
    high = big - (big - a)
    return high, a - high


def two_product(a, b):
    value = a * b
    ah, al = split(a)
    bh, bl = split(b)
    return value, ((ah * bh - value) + ah * bl + al * bh) + al * bl


def add(a, b):
    total, error = two_sum(a[0], b[0])
    return quick(total, error + (a[1] + b[1]))


def neg(a):
    return (-a[0], -a[1])


def mul(a, b):
    value, error = two_product(a[0], b[0])
    return quick(value, error + (a[0] * b[1] + a[1] * b[0]))


def div(a, b):
    first = a[0] / b[0]
    zero = jnp.zeros_like(first)
    rest = add(a, neg(mul(b, (first, zero))))
    second = rest[0] / b[0]
    rest = add(rest, neg(mul(b, (second, zero))))
    third = rest[0] / b[0]
    return add(quick(first, second), (third, zero))


def c_add(a, b):
    return (add(a[0], b[0]), add(a[1], b[1]))


def c_neg(a):
    return (neg(a[0]), neg(a[1]))


def c_conj(a):
    return (a[0], neg(a[1]))


def c_mul(a, b):
    return (
        add(mul(a[0], b[0]), neg(mul(a[1], b[1]))),
        add(mul(a[0], b[1]), mul(a[1], b[0])),
    )


def c_div(a, b):
    top = c_mul(a, c_conj(b))
    bottom = add(mul(b[0], b[0]), mul(b[1], b[1]))
    return (div(top[0], bottom), div(top[1], bottom))


def c_over(a, real):
    return (div(a[0], real), div(a[1], real))


def total_of(values):
    result = values[0]
    for value in values[1:]:
        result = c_add(result, value)
    return result


def coefficients(gram):
    rho = gram[0, 0]
    alpha = c_div(rho, gram[0, 1])
    one_half = c_neg(alpha)

    def form(coeffs, left, right):
        rows = []
        for i, factor in enumerate(coeffs):
            inner = total_of(
                [
                    gram[i + left, j + right]
                    if other is None
                    else c_mul(gram[i + left, j + right], other)
                    for j, other in enumerate(coeffs)
                ]
            )
            rows.append(inner if factor is None else c_mul(c_conj(factor), inner))
        return total_of(rows)

    omega = c_over(form([None, one_half], 1, 0), form([None, one_half], 1, 1)[0])
    res1 = c_neg(c_add(alpha, omega))
    res2 = c_mul(alpha, omega)
    new_rho = total_of([gram[0, 0], c_mul(gram[0, 1], res1), c_mul(gram[0, 2], res2)])
    mix = c_mul(c_div(new_rho, rho), c_div(alpha, omega))
    dir0 = (add((jnp.ones_like(mix[0][0]), jnp.zeros_like(mix[0][0])), mix[0]), mix[1])
    dir1 = c_add(res1, c_neg(c_mul(mix, omega)))
    dir2 = res2
    along = total_of(
        [c_mul(gram[0, 1], dir0), c_mul(gram[0, 2], dir1), c_mul(gram[0, 3], dir2)]
    )
    alpha2 = c_div(new_rho, along)
    half1 = c_add(res1, c_neg(c_mul(alpha2, dir0)))
    half2 = c_add(res2, c_neg(c_mul(alpha2, dir1)))
    half3 = c_neg(c_mul(alpha2, dir2))
    half = [None, half1, half2, half3]
    omega2 = c_over(form(half, 1, 0), form(half, 1, 1)[0])
    out0 = total_of([alpha, omega, c_mul(alpha2, dir0), omega2])
    out1 = total_of([c_mul(omega, one_half), c_mul(alpha2, dir1), c_mul(omega2, half1)])
    out2 = c_add(c_mul(alpha2, dir2), c_mul(omega2, half2))
    out3 = c_mul(omega2, half3)
    return [(c[0][0], c[1][0]) for c in (out0, out1, out2, out3)]


def update_kernel(sizes, rows_ref, start_ref, basis_ref, out_ref):
    depths, lats, pieces = sizes
    kind = lax.axis_index("depth") // pieces
    count = pieces * lats
    sub = lax.broadcasted_iota(jnp.int32, (ROWS, LANES), 0)
    high = jnp.zeros((ROWS, LANES), jnp.float32)
    low = high
    for number in range(KINDS * count // ROWS):
        mine = (sub >= kind * count - number * ROWS) & (sub < (kind + 1) * count - number * ROWS)
        rows = jnp.where(mine, rows_ref[number * ROWS : (number + 1) * ROWS], 0.0)
        high, error = two_sum(high, rows)
        low = low + error
    for shift in (4, 2, 1):
        high, error = two_sum(high, pltpu.roll(high, shift, 0))
        low = low + pltpu.roll(low, shift, 0) + error
    high, low = quick(high, low + pltpu.roll(high, 64, 1))

    def entry(number):
        return (
            jnp.broadcast_to(high[:, number : number + 1], (ROWS, LANES)),
            jnp.broadcast_to(low[:, number : number + 1], (ROWS, LANES)),
        )

    zero = jnp.zeros((ROWS, LANES), jnp.float32)
    gram = {}
    at = 0
    for i, j in PAIRS:
        real = entry(at)
        at += 1
        if i == j:
            gram[i, i] = (real, (zero, zero))
        else:
            gram[i, j] = (real, entry(at))
            gram[j, i] = c_conj(gram[i, j])
            at += 1
    factors = coefficients(gram)

    def layer(source, carry):
        for component in range(3):
            for z in range(2):
                real = start_ref[source, slot(0, component, z)]
                imag = start_ref[source, slot(1, component, z)]
                for b, (fr, fi) in enumerate(factors):
                    br = basis_ref[b, source, slot(0, component, z)]
                    bi = basis_ref[b, source, slot(1, component, z)]
                    real = real + (fr * br - fi * bi)
                    imag = imag + (fr * bi + fi * br)
                out_ref[source, slot(0, component, z)] = real
                out_ref[source, slot(1, component, z)] = imag
        return carry

    lax.fori_loop(0, depths, layer, 0)


def output_kernel(pieces, in_ref, field_ref, term_ref):
    for piece in range(pieces):
        cols = slice(piece * LANES, (piece + 1) * LANES)
        for z in range(2):
            term = None
            for component in range(3):
                values = []
                for kind in range(KINDS):
                    for part in range(2):
                        value = in_ref[kind * pieces + piece, slot(part, component, z)]
                        field_ref[kind * 12 + slot(part, component, z), :, cols] = value
                        values.append(value)
                product = values[0] * values[2] - values[1] * values[3]
                term = product if term is None else term + product
            term_ref[piece, z] = term


def local(conductivity, field_guess, tx_cell, rx_cell, rx_weight):
    depths, lats = lax.axis_size("depth"), lax.axis_size("lat")
    pieces = depths // KINDS
    sizes = (depths, lats, pieces)
    width = conductivity.shape[2]
    layers = 2 * depths
    f32 = jnp.float32
    params = pltpu.CompilerParams

    packed = pl.pallas_call(
        functools.partial(pack_kernel, pieces),
        out_shape=jax.ShapeDtypeStruct((depths, 16, ROWS, LANES), f32),
        in_specs=[in_vmem()] * 2,
        out_specs=in_vmem(),
        compiler_params=params(vmem_limit_bytes=4 * MIB),
    )(field_guess.reshape(24, ROWS, width), conductivity)
    mid = lax.all_to_all(packed, "depth", 0, 0)
    left = lax.ppermute(mid, "lat", [(i, i + 1) for i in range(lats - 1)])
    right = lax.ppermute(mid, "lat", [(i + 1, i) for i in range(lats - 1)])

    basis, rows = pl.pallas_call(
        functools.partial(basis_kernel, sizes),
        out_shape=(
            jax.ShapeDtypeStruct((BASIS - 1, depths, 12, ROWS, LANES), f32),
            jax.ShapeDtypeStruct((depths * lats, LANES), f32),
        ),
        in_specs=[in_smem()] * 3 + [in_vmem()] * 3,
        out_specs=(in_vmem(), in_vmem()),
        scratch_shapes=[
            pltpu.VMEM((BASIS + 1, 6, layers + 1, 3 * ROWS, 2 * LANES), f32),
            pltpu.VMEM((4, 3 * ROWS, 2 * LANES), f32),
            pltpu.VMEM((layers, 3 * ROWS, 2 * LANES), f32),
            pltpu.VMEM((3 * ROWS, 2 * LANES), f32),
            pltpu.VMEM((2 * len(ENTRIES), ROWS, LANES), f32),
        ],
        compiler_params=params(vmem_limit_bytes=28 * MIB),
    )(tx_cell, rx_cell, rx_weight.reshape(1, -1), left, mid, right)

    rows = lax.all_to_all(rows, GRID_AXES, 0, 0)
    moved = pl.pallas_call(
        functools.partial(update_kernel, sizes),
        out_shape=jax.ShapeDtypeStruct((depths, 12, ROWS, LANES), f32),
        in_specs=[in_vmem()] * 3,
        out_specs=in_vmem(),
        compiler_params=params(vmem_limit_bytes=8 * MIB),
    )(rows, mid, basis)
    moved = lax.all_to_all(moved, "depth", 0, 0)
    fields, terms = pl.pallas_call(
        functools.partial(output_kernel, pieces),
        out_shape=(
            jax.ShapeDtypeStruct((24, ROWS, width), f32),
            jax.ShapeDtypeStruct((pieces, 2, ROWS, LANES), f32),
        ),
        in_specs=[in_vmem()],
        out_specs=(in_vmem(), in_vmem()),
        compiler_params=params(vmem_limit_bytes=4 * MIB),
    )(moved)
    gradient = jnp.sum(lax.all_to_all(terms, "tx", 0, 0), axis=0)
    return (fields.reshape(field_guess.shape), gradient)


def solution(mesh):
    return jax.shard_map(
        local,
        mesh=mesh,
        in_specs=(
            P("depth", "lat", None),
            P("tx", None, None, None, "depth", "lat", None),
            P("tx"),
            P("tx", None),
            P("tx", None, None),
        ),
        out_specs=(P("tx", None, None, None, "depth", "lat", None), P("depth", "lat", "tx")),
        check_vma=False,
    )
```

time: 1540 us -> 117 us (0.08)
  blocking collectives: 1350 us -> 78.5 us
  waiting for transfers between devices: 86.8 us -> 7.19 us
  starting transfers between devices: 51.2 us -> 4.32 us
  Pallas kernels: 0 us -> 21.5 us
  other arithmetic: 20.6 us -> 0.6 us
  between operations: 16.9 us -> 1.35 us
    psum x5 -> x0, blocking collectives: 1350 us -> none  [the longest x2 545 us: local(): lax.psum((cross_pair[0], cross_pair[1], energy), ('depth', 'lat'))]
    all_to_all x0 -> x4, blocking collectives: none -> 78.5 us  [the longest x1 24.4 us: local(): mid = lax.all_to_all(packed, 'depth', 0, 0)]
    reduce_scatter x1 -> x0, waiting for transfers between devices: 50.1 us -> none  [local(): gradient = lax.psum_scatter(term, 'tx', scatter_dimension=2, tiled=True)]
    ppermute x20 -> x2, starting transfers between devices: 51.1 us -> 4.32 us  [the longest x1 2.41 us: local(): left = lax.ppermute(mid, 'lat', [(i, i + 1) for i in range(lats - 1)])]
    ppermute x20 -> x2, waiting for transfers between devices: 36.6 us -> 7.19 us  [the longest x1 3.82 us: local(): left = lax.ppermute(mid, 'lat', [(i, i + 1) for i in range(lats - 1)])]
    pallas_call x0 -> x4, Pallas kernels: none -> 21.5 us  [the longest x1 19.1 us: local(): pl.pallas_call(functools.partial(basis_kernel, sizes), out_shape=(jax.Sha...]
  transfers between devices with their start and end apart: 21 -> 2, of which waited for: 19 -> 2; matrix products, arithmetic and copies ran while one was open for 1% -> 0% of each run, Pallas kernels for 0% -> 0%
where the time goes in v1:
time: 117 us; the launch traced here: 115 us
  blocking collectives  78.5 us (67%)
  Pallas kernels  21.5 us (18%)
  waiting for transfers between devices  7.19 us (6%)
  starting transfers between devices  4.32 us (4%)
  local copies, waits for them, and re-layouts  2 us (2%)
  between operations  1.35 us (1%)
    all_to_all x1, blocking collectives, local(): mid = lax.all_to_all(packed, 'depth', 0, 0)  24.4 us
    pallas_call x1, Pallas kernels, local(): pl.pallas_call(functools.partial(basis_kernel, sizes), out_shape=(jax.Sha...  19.1 us
    all_to_all x1, blocking collectives, local(): rows = lax.all_to_all(rows, GRID_AXES, 0, 0)  18.7 us
    all_to_all x1, blocking collectives, local(): gradient = jnp.sum(lax.all_to_all(terms, 'tx', 0, 0), axis=0)  17.9 us
    all_to_all x1, blocking collectives, local(): moved = lax.all_to_all(moved, 'depth', 0, 0)  17.4 us
    ppermute x1, waiting for transfers between devices, local(): left = lax.ppermute(mid, 'lat', [(i, i + 1) for i in range(lats - 1)])  3.82 us
    ppermute x1, waiting for transfers between devices, local(): right = lax.ppermute(mid, 'lat', [(i + 1, i) for i in range(lats - 1)])  3.37 us
    ppermute x1, starting transfers between devices, local(): left = lax.ppermute(mid, 'lat', [(i, i + 1) for i in range(lats - 1)])  2.41 us
  transfers between devices with their start and end apart: 2, of which 2 were waited for; matrix products, arithmetic and copies ran while one was open for 0% of the time, Pallas kernels for 0%

profile of v1, /device:TPU:6, one launch (start us, length us, event | category | flops | bytes accessed | tf_op | source)
XLA Modules:
  0.0 115.5 jit_solution(9145934284827988537)
XLA Ops:
  0.6 0.0 copy-start.3
  0.6 0.0 copy-start.2
  0.7 0.0 copy-start
  0.7 1.0 copy-done
  1.7 0.0 copy-start.1
  1.7 0.8 copy-done.1
  2.4 0.2 shard_map.68
  2.6 24.4 %all_to_all.26.mid_ref.start_ref = f32[8,16,8,128]{3,2,1,0:T(8,128)S(1)} all-to-all(f32[8,16,8,128]{3,2,1,0:T(8,128)S(1)} %shard_map.68), channel_id=1, replica_groups=mesh['depth'=8,'lat'=16,'tx'=4] {'depth'}, dimensions={0} | all-to-all | bytes 1048576 | tf_op jit(solution)/shard_map/all_to_all | solution.py:440
  27.0 1.9 %collective-permute-start.1 = (f32[8,16,8,128]{3,2,1,0:T(8,128)S(1)}, f32[8,16,8,128]{3,2,1,0:T(8,128)S(1)}, u32[]{:S(2)}, u32[]{:S(2)}) collective-permute-start(f32[8,16,8,128]{3,2,1,0:T(8,128)S(1)} %all_to_all.26.mid_ref.start_ref), channel_id=1, source_target_pairs={{4,0},{8,4},{12,8},{16,12},{20,16},{24,20},{28,24},{32,28},{36,32}... | collective-permute-start | bytes 1572872 | tf_op jit(solution)/shard_map/ppermute | solution.py:442
  28.9 2.4 %collective-permute-start = (f32[8,16,8,128]{3,2,1,0:T(8,128)S(1)}, f32[8,16,8,128]{3,2,1,0:T(8,128)S(1)}, u32[]{:S(2)}, u32[]{:S(2)}) collective-permute-start(f32[8,16,8,128]{3,2,1,0:T(8,128)S(1)} %all_to_all.26.mid_ref.start_ref), channel_id=1, source_target_pairs={{0,4},{4,8},{8,12},{12,16},{16,20},{20,24},{24,28},{28,32},{32,36}... | collective-permute-start | bytes 1572872 | tf_op jit(solution)/shard_map/ppermute | solution.py:441
  32.0 0.0 copy-done.3
  32.0 0.1 copy.9
  32.1 0.1 reshape.15.weight_ref
  32.2 3.4 %collective-permute-done.1.right_ref = f32[8,16,8,128]{3,2,1,0:T(8,128)S(1)} collective-permute-done((f32[8,16,8,128]{3,2,1,0:T(8,128)S(1)}, f32[8,16,8,128]{3,2,1,0:T(8,128)S(1)}, u32[]{:S(2)}, u32[]{:S(2)}) %collective-permute-start.1) | collective-permute-done | bytes 524320 | tf_op jit(solution)/shard_map/ppermute | solution.py:442
  35.6 3.8 %collective-permute-done.left_ref = f32[8,16,8,128]{3,2,1,0:T(8,128)S(1)} collective-permute-done((f32[8,16,8,128]{3,2,1,0:T(8,128)S(1)}, f32[8,16,8,128]{3,2,1,0:T(8,128)S(1)}, u32[]{:S(2)}, u32[]{:S(2)}) %collective-permute-start) | collective-permute-done | bytes 524320 | tf_op jit(solution)/shard_map/ppermute | solution.py:441
  39.4 0.0 copy-done.2
  39.4 19.1 %shard_map.69 = (f32[4,8,12,8,128]{4,3,2,1,0:T(8,128)S(1)}, f32[128,128]{1,0:T(8,128)S(1)}) custom-call(s32[1]{0:T(128)S(6)} %copy.11.tx_ref, s32[1,64]{1,0:T(1,128)S(1)} %copy-done.2, f32[1,128]{1,0:T(1,128)S(1)} %reshape.15.weight_ref, f32[8,16,8,128]{3,2,1,0:T(8,128)S(1)} %collective-permute-done.left_ref, ...), custom_call_target="tpu_custom_call" | custom-call | tf_op jit(solution)/shard_map/pallas_call | solution.py:444
  58.5 18.7 %all_to_all.27 = f32[128,1,128]{2,1,0:T(1,128)S(1)} all-to-all(f32[128,1,128]{2,1,0:T(1,128)S(1)} %bitcast.8), channel_id=1, replica_groups=mesh['depth'=8,'lat'=16,'tx'=4] {'depth','lat'}, dimensions={0} | all-to-all | bytes 131072 | tf_op jit(solution)/shard_map/all_to_all | solution.py:462
  77.2 1.5 %shard_map.70 = f32[8,12,8,128]{3,2,1,0:T(8,128)S(1)} custom-call(f32[128,128]{1,0:T(8,128)S(1)} %bitcast.7, f32[8,16,8,128]{3,2,1,0:T(8,128)S(1)} %all_to_all.26.mid_ref.start_ref, f32[4,8,12,8,128]{4,3,2,1,0:T(8,128)S(1)} %get-tuple-element.7.basis_ref), custom_call_target="tpu_custom_call" | custom-call | tf_op jit(solution)/shard_map/pallas_call | solution.py:463
  78.7 17.4 %all_to_all.28.in_ref = f32[8,12,8,128]{3,2,1,0:T(8,128)S(1)} all-to-all(f32[8,12,8,128]{3,2,1,0:T(8,128)S(1)} %shard_map.70), channel_id=1, replica_groups=mesh['depth'=8,'lat'=16,'tx'=4] {'depth'}, dimensions={0} | all-to-all | bytes 786432 | tf_op jit(solution)/shard_map/all_to_all | solution.py:470
  96.1 0.8 shard_map.71
  96.9 17.9 %all_to_all.29 = f32[4,2,8,128]{3,2,1,0:T(8,128)S(1)} all-to-all(f32[4,2,8,128]{3,2,1,0:T(8,128)S(1)} %get-tuple-element.9), channel_id=1, replica_groups=mesh['depth'=8,'lat'=16,'tx'=4] {'tx'}, dimensions={0} | all-to-all | bytes 65536 | tf_op jit(solution)/shard_map/all_to_all | solution.py:481
  114.9 0.6 reduce_sum.9
Async XLA Ops:
  0.6 31.3 %copy-start.3 = (f32[1,64,2]{1,2,0:T(2,128)S(1)}, f32[1,64,2]{1,2,0:T(2,128)}, u32[]{:S(2)}) copy-start(f32[1,64,2]{1,2,0:T(2,128)} %param.9) | copy-start | bytes 1540
  0.6 38.8 %copy-start.2 = (s32[1,64]{1,0:T(1,128)S(1)}, s32[1,64]{1,0:T(1,128)}, u32[]{:S(2)}) copy-start(s32[1,64]{1,0:T(1,128)} %rx_ref.1) | copy-start | bytes 772
  0.7 1.0 copy-start
  1.7 0.8 copy-start.1
  27.0 8.6 %collective-permute-start.1 = (f32[8,16,8,128]{3,2,1,0:T(8,128)S(1)}, f32[8,16,8,128]{3,2,1,0:T(8,128)S(1)}, u32[]{:S(2)}, u32[]{:S(2)}) collective-permute-start(f32[8,16,8,128]{3,2,1,0:T(8,128)S(1)} %all_to_all.26.mid_ref.start_ref), channel_id=1, source_target_pairs={{4,0},{8,4},{12,8},{16,12},{20,16},{24,20},{28,24},{32,28},{36,32}... | collective-permute-start | bytes 1572872 | tf_op jit(solution)/shard_map/ppermute | solution.py:442
  28.9 10.5 %collective-permute-start = (f32[8,16,8,128]{3,2,1,0:T(8,128)S(1)}, f32[8,16,8,128]{3,2,1,0:T(8,128)S(1)}, u32[]{:S(2)}, u32[]{:S(2)}) collective-permute-start(f32[8,16,8,128]{3,2,1,0:T(8,128)S(1)} %all_to_all.26.mid_ref.start_ref), channel_id=1, source_target_pairs={{0,4},{4,8},{8,12},{12,16},{16,20},{20,24},{24,28},{28,32},{32,36}... | collective-permute-start | bytes 1572872 | tf_op jit(solution)/shard_map/ppermute | solution.py:441

commit v2 on v1

--- a/solution.py
+++ b/solution.py
@@ -5,6 +5,7 @@
 from jax import lax
 from jax.experimental import pallas as pl
 from jax.experimental.pallas import tpu as pltpu
+from jax.sharding import Mesh
 from jax.sharding import PartitionSpec as P
 
 SOURCE = 20.0
@@ -12,7 +13,7 @@
 BASIS = 5
 ROWS = 8
 LANES = 128
-GRID_AXES = ("depth", "lat")
+DEPTH = ("kind", "piece")
 PAIRS = [(i, j) for i in range(BASIS) for j in range(i, BASIS)]
 ENTRIES = [(i, j, part) for i, j in PAIRS for part in range(1 if i == j else 2)]
 MIB = 1 << 20
@@ -62,50 +63,63 @@
     return total, (a - (total - other)) + (b - other)
 
 
+def basis_scratch(depths):
+    layers = 2 * depths
+    f32 = jnp.float32
+    return [
+        pltpu.VMEM((BASIS, 6, layers + 1, 2 * ROWS, 2 * LANES), f32),
+        pltpu.VMEM((7, layers, 3 * ROWS, LANES), f32),
+        pltpu.VMEM((4, 3 * ROWS, 2 * LANES), f32),
+        pltpu.VMEM((4, 2 * ROWS, 2 * LANES), f32),
+        pltpu.VMEM((layers, 2 * ROWS, 2 * LANES), f32),
+        pltpu.VMEM((3 * ROWS, 2 * LANES), f32),
+        pltpu.VMEM((2 * ROWS, 2 * LANES), f32),
+        pltpu.VMEM((2 * len(ENTRIES), ROWS, LANES), f32),
+    ]
+
+
 def basis_kernel(
     sizes, tx_ref, rx_ref, weight_ref, left_ref, mid_ref, right_ref, basis_ref, gram_ref,
-    field, curl, cond, inside, acc,
+    field, edges, curl_start, curl, cond, inside_start, inside, acc,
 ):
     depths, lats, pieces = sizes
     layers = 2 * depths
-    wide = 3 * ROWS
     span = 2 * LANES
-    depth_index = lax.axis_index("depth")
+    width = pieces * LANES
     lat_index = lax.axis_index("lat")
-    kind = depth_index // pieces
-    piece = depth_index % pieces
+    kind = lax.axis_index("kind")
+    piece = lax.axis_index("piece")
     lane = lax.broadcasted_iota(jnp.int32, (ROWS, LANES), 1)
     blank = jnp.zeros((ROWS, LANES), jnp.float32)
 
-    row_w = lax.broadcasted_iota(jnp.int32, (wide, span), 0)
-    lane_w = lax.broadcasted_iota(jnp.int32, (wide, span), 1)
-    x_at = lat_index * ROWS - ROWS + row_w
-    y_at = piece * LANES + jnp.where(lane_w >= LANES + 64, lane_w - span, lane_w)
-    good = (x_at >= 0) & (x_at < lats * ROWS) & (y_at >= 0) & (y_at < pieces * LANES)
-    inside[...] = jnp.where(good, 1.0, 0.0)
-
-    for number, ref in enumerate((left_ref, mid_ref, right_ref)):
-        rows = slice(number * ROWS, (number + 1) * ROWS)
-
-        def spread(source, carry, ref=ref, rows=rows):
+    def within(rows, row):
+        lane_w = lax.broadcasted_iota(jnp.int32, (rows, span), 1)
+        x_at = lat_index * ROWS + row
+        y_at = piece * LANES + jnp.where(lane_w >= LANES + 64, lane_w - span, lane_w)
+        good = (x_at >= 0) & (x_at < lats * ROWS) & (y_at >= 0) & (y_at < width)
+        return jnp.where(good, 1.0, 0.0)
+
+    row_s = lax.broadcasted_iota(jnp.int32, (3 * ROWS, span), 0)
+    inside_start[...] = within(3 * ROWS, row_s - ROWS)
+    row_b = lax.broadcasted_iota(jnp.int32, (2 * ROWS, span), 0)
+    inside[...] = within(2 * ROWS, jnp.where(row_b >= 12, row_b - 16, row_b))
+
+    received = (left_ref, mid_ref, right_ref)
+
+    def spread(source, carry):
+        for number, ref in enumerate(received):
+            packs = [ref[source, 14], ref[source, 15]]
             for item in range(14):
-                place = item % 8
-                edge = pltpu.roll(ref[source, 14 + item // 8], LANES - (16 * place + 8), 1)
+                edge = pltpu.roll(packs[item // 8], LANES - (16 * (item % 8) + 8), 1)
                 edge = jnp.where((lane < 8) | (lane >= LANES - 8), edge, blank)
-                body = ref[source, item]
-                z = 2 * source + item % 2
-                if item < 12:
-                    field[0, item // 2, z, rows, 0:LANES] = body
-                    field[0, item // 2, z, rows, LANES:span] = edge
-                else:
-                    cond[z, rows, 0:LANES] = body
-                    cond[z, rows, LANES:span] = edge
-            return carry
-
-        lax.fori_loop(0, depths, spread, 0)
-
-    empty = jnp.zeros((wide, span), jnp.float32)
-    for number in range(BASIS):
+                at = slice(number * ROWS, (number + 1) * ROWS)
+                edges[item // 2, 2 * source + item % 2, at] = edge
+        return carry
+
+    lax.fori_loop(0, depths, spread, 0, unroll=2)
+
+    empty = jnp.zeros((2 * ROWS, span), jnp.float32)
+    for number in range(BASIS - 1):
         for component in range(6):
             field[number, component, layers] = empty
 
@@ -115,78 +129,133 @@
     def behind(values, axis):
         return values - pltpu.roll(values, 1, axis)
 
-    for step in range(BASIS):
-        for component in range(4):
-            curl[component] = empty
-
-        def apply_layer(z, carry, step=step):
+    def curl_ahead(here, above, keep):
+        uz, ux, uy = here
+        hz = (ahead(uy, 0) - ahead(ux, 1)) * keep
+        hx = (ahead(uz, 1) - (above[1] - uy)) * keep
+        hy = ((above[0] - ux) - ahead(uz, 0)) * keep
+        return hz, hx, hy
+
+    def curl_behind(h, below):
+        hz, hx, hy = h
+        return (
+            behind(hy, 0) - behind(hx, 1),
+            behind(hz, 1) - (hy - below[1]),
+            (hx - below[0]) - behind(hz, 0),
+        )
+
+    def start_tile(number, z, source, layer):
+        body = jnp.concatenate([ref[source, 2 * number + layer] for ref in received], axis=0)
+        return jnp.concatenate([body, edges[number, z]], axis=1)
+
+    def merge(values):
+        sub = lax.broadcasted_iota(jnp.int32, (ROWS, span), 0)
+        sides = jnp.where(sub < 4, values[2 * ROWS :], values[:ROWS])
+        return jnp.concatenate([values[ROWS : 2 * ROWS], sides], axis=0)
+
+    for number in range(4):
+        curl_start[number] = jnp.zeros((3 * ROWS, span), jnp.float32)
+
+    def start_layers(source, carry):
+        keep = inside_start[...]
+        below = [[curl_start[0], curl_start[1]], [curl_start[2], curl_start[3]]]
+        for layer in range(2):
+            z = 2 * source + layer
+            tiles = [start_tile(c, z, source, layer) for c in range(6)]
+            sigma = start_tile(6, z, source, layer)
+            cond[z] = merge(sigma)
+            for part in range(2):
+                here = tiles[3 * part : 3 * part + 3]
+                if layer == 0:
+                    above = [start_tile(3 * part + c, z + 1, source, 1) for c in (1, 2)]
+                else:
+                    last = source == depths - 1
+                    after = jnp.minimum(source + 1, depths - 1)
+                    above = [
+                        jnp.where(last, 0.0, start_tile(3 * part + c, 2 * after, after, 0))
+                        for c in (1, 2)
+                    ]
+                h = curl_ahead(here, above, keep)
+                outs = curl_behind(h, below[part])
+                below[part] = [h[1], h[2]]
+                for component, value in enumerate(outs):
+                    other = sigma * tiles[3 * (1 - part) + component]
+                    value = other - value if part == 0 else -value - other
+                    field[0, 3 * part + component, z] = merge(value) * inside[...]
+        for number in range(4):
+            curl_start[number] = below[number // 2][number % 2]
+        return carry
+
+    lax.fori_loop(0, depths, start_layers, 0)
+
+    line = lax.broadcasted_iota(jnp.int32, (1, span), 1)
+
+    def add_source(cell, real, imag):
+        col = (cell & (width - 1)) - piece * LANES
+        rest = lax.shift_right_logical(cell, width.bit_length() - 1)
+        row = (rest & (lats * ROWS - 1)) - lat_index * ROWS
+        z = lax.shift_right_logical(rest, (lats * ROWS).bit_length() - 1)
+
+        @pl.when((row >= -4) & (row < 12) & (col >= -8) & (col < LANES + 8))
+        def _():
+            hit = line == (col & (span - 1))
+            at = pl.ds(row & (2 * ROWS - 1), 1)
+            field[0, 0, z, at] = field[0, 0, z, at] + jnp.where(hit, real, 0.0)
+            field[0, 3, z, at] = field[0, 3, z, at] + jnp.where(hit, imag, 0.0)
+
+    @pl.when(kind == 0)
+    def _():
+        add_source(tx_ref[0], jnp.float32(0.0), jnp.float32(-SOURCE))
+
+    @pl.when(kind == 1)
+    def _():
+        def each(r, carry):
+            add_source(rx_ref[0, r], weight_ref[0, 2 * r], weight_ref[0, 2 * r + 1])
+            return carry
+
+        lax.fori_loop(0, rx_ref.shape[1], each, 0)
+
+    for step in range(BASIS - 1):
+        for number in range(4):
+            curl[number] = empty
+
+        def apply_layers(source, carry, step=step):
             keep = inside[...]
-            sigma = cond[z]
-            for part in range(2):
-                uz = field[step, part * 3, z]
-                ux = field[step, part * 3 + 1, z]
-                uy = field[step, part * 3 + 2, z]
-                dz_ux = field[step, part * 3 + 1, z + 1] - ux
-                dz_uy = field[step, part * 3 + 2, z + 1] - uy
-                hz = (ahead(uy, 0) - ahead(ux, 1)) * keep
-                hx = (ahead(uz, 1) - dz_uy) * keep
-                hy = (dz_ux - ahead(uz, 0)) * keep
-                dz_hx = hx - curl[part * 2]
-                dz_hy = hy - curl[part * 2 + 1]
-                curl[part * 2] = hx
-                curl[part * 2 + 1] = hy
-                outs = (
-                    behind(hy, 0) - behind(hx, 1),
-                    behind(hz, 1) - dz_hy,
-                    dz_hx - behind(hz, 0),
-                )
-                for component, value in enumerate(outs):
-                    other = sigma * field[step, (1 - part) * 3 + component, z]
-                    value = value - other if part == 0 else value + other
-                    if step == 0:
-                        value = -value
-                    field[step + 1, part * 3 + component, z] = value * keep
+            below = [[curl[0], curl[1]], [curl[2], curl[3]]]
+            for layer in range(2):
+                z = 2 * source + layer
+                sigma = cond[z]
+                for part in range(2):
+                    here = [field[step, 3 * part + c, z] for c in range(3)]
+                    above = [field[step, 3 * part + c, z + 1] for c in (1, 2)]
+                    h = curl_ahead(here, above, keep)
+                    outs = curl_behind(h, below[part])
+                    below[part] = [h[1], h[2]]
+                    for component, value in enumerate(outs):
+                        if step == BASIS - 2:
+                            mine = (slice(0, ROWS), slice(0, LANES))
+                        else:
+                            mine = (slice(None), slice(None))
+                        near = field[(step, 3 * (1 - part) + component, z) + mine]
+                        other = sigma[mine] * near
+                        value = value[mine]
+                        value = value - other if part == 0 else value + other
+                        if step < BASIS - 2:
+                            value = value * keep
+                        field[(step + 1, 3 * part + component, z) + mine] = value
+            for number in range(4):
+                curl[number] = below[number // 2][number % 2]
             return carry
 
-        lax.fori_loop(0, layers, apply_layer, 0)
-
-        if step == 0:
-            line = lax.broadcasted_iota(jnp.int32, (1, span), 1)
-
-            def add_source(cell, real, imag):
-                y = cell % (pieces * LANES)
-                x = cell // (pieces * LANES) % (lats * ROWS)
-                z = cell // (pieces * LANES * lats * ROWS)
-                row = x - lat_index * ROWS + ROWS
-                col = y - piece * LANES
-
-                @pl.when((row >= 0) & (row < wide) & (col >= -8) & (col < LANES + 8))
-                def _():
-                    hit = line == jnp.where(col < 0, col + span, col)
-                    at = pl.ds(row, 1)
-                    field[1, 0, z, at] = field[1, 0, z, at] + jnp.where(hit, real, 0.0)
-                    field[1, 3, z, at] = field[1, 3, z, at] + jnp.where(hit, imag, 0.0)
-
-            @pl.when(kind == 0)
-            def _():
-                add_source(tx_ref[0], jnp.float32(0.0), jnp.float32(-SOURCE))
-
-            @pl.when(kind == 1)
-            def _():
-                def each(r, carry):
-                    add_source(rx_ref[0, r], weight_ref[0, 2 * r], weight_ref[0, 2 * r + 1])
-                    return carry
-
-                lax.fori_loop(0, rx_ref.shape[1], each, 0)
+        lax.fori_loop(0, depths, apply_layers, 0, unroll=2)
 
     for entry in range(2 * len(ENTRIES)):
         acc[entry] = blank
-    own = slice(ROWS, 2 * ROWS)
 
     def gram_layer(source, carry):
         for layer in range(2):
             z = 2 * source + layer
-            tiles = [[field[b + 1, c, z, own, 0:LANES] for c in range(6)] for b in range(BASIS)]
+            tiles = [[field[b, c, z, 0:ROWS, 0:LANES] for c in range(6)] for b in range(BASIS)]
             for b in range(BASIS - 1):
                 for c in range(6):
                     basis_ref[b, source, 2 * c + layer] = tiles[b][c]
@@ -203,7 +272,7 @@
                 acc[2 * entry + 1] = acc[2 * entry + 1] + error
         return carry
 
-    lax.fori_loop(0, depths, gram_layer, 0)
+    lax.fori_loop(0, depths, gram_layer, 0, unroll=2)
 
     def fold(high, low, shift, axis):
         total, error = two_sum(high, pltpu.roll(high, shift, axis))
@@ -225,7 +294,7 @@
         row = jnp.where(lane == sub + start + 64, lows, row)
     for shift in (4, 2, 1):
         row = row + pltpu.roll(row, shift, 0)
-    for number in range(depths * lats // ROWS):
+    for number in range(pieces * lats // ROWS):
         gram_ref[number * ROWS : (number + 1) * ROWS] = row
 
 
@@ -352,15 +421,10 @@
 
 def update_kernel(sizes, rows_ref, start_ref, basis_ref, out_ref):
     depths, lats, pieces = sizes
-    kind = lax.axis_index("depth") // pieces
-    count = pieces * lats
-    sub = lax.broadcasted_iota(jnp.int32, (ROWS, LANES), 0)
     high = jnp.zeros((ROWS, LANES), jnp.float32)
     low = high
-    for number in range(KINDS * count // ROWS):
-        mine = (sub >= kind * count - number * ROWS) & (sub < (kind + 1) * count - number * ROWS)
-        rows = jnp.where(mine, rows_ref[number * ROWS : (number + 1) * ROWS], 0.0)
-        high, error = two_sum(high, rows)
+    for number in range(pieces * lats // ROWS):
+        high, error = two_sum(high, rows_ref[number * ROWS : (number + 1) * ROWS])
         low = low + error
     for shift in (4, 2, 1):
         high, error = two_sum(high, pltpu.roll(high, shift, 0))
@@ -422,8 +486,8 @@
 
 
 def local(conductivity, field_guess, tx_cell, rx_cell, rx_weight):
-    depths, lats = lax.axis_size("depth"), lax.axis_size("lat")
-    pieces = depths // KINDS
+    pieces, lats = lax.axis_size("piece"), lax.axis_size("lat")
+    depths = KINDS * pieces
     sizes = (depths, lats, pieces)
     width = conductivity.shape[2]
     layers = 2 * depths
@@ -437,7 +501,7 @@
         out_specs=in_vmem(),
         compiler_params=params(vmem_limit_bytes=4 * MIB),
     )(field_guess.reshape(24, ROWS, width), conductivity)
-    mid = lax.all_to_all(packed, "depth", 0, 0)
+    mid = lax.all_to_all(packed, DEPTH, 0, 0)
     left = lax.ppermute(mid, "lat", [(i, i + 1) for i in range(lats - 1)])
     right = lax.ppermute(mid, "lat", [(i + 1, i) for i in range(lats - 1)])
 
@@ -445,21 +509,15 @@
         functools.partial(basis_kernel, sizes),
         out_shape=(
             jax.ShapeDtypeStruct((BASIS - 1, depths, 12, ROWS, LANES), f32),
-            jax.ShapeDtypeStruct((depths * lats, LANES), f32),
+            jax.ShapeDtypeStruct((pieces * lats, LANES), f32),
         ),
         in_specs=[in_smem()] * 3 + [in_vmem()] * 3,
         out_specs=(in_vmem(), in_vmem()),
-        scratch_shapes=[
-            pltpu.VMEM((BASIS + 1, 6, layers + 1, 3 * ROWS, 2 * LANES), f32),
-            pltpu.VMEM((4, 3 * ROWS, 2 * LANES), f32),
-            pltpu.VMEM((layers, 3 * ROWS, 2 * LANES), f32),
-            pltpu.VMEM((3 * ROWS, 2 * LANES), f32),
-            pltpu.VMEM((2 * len(ENTRIES), ROWS, LANES), f32),
-        ],
+        scratch_shapes=basis_scratch(depths),
         compiler_params=params(vmem_limit_bytes=28 * MIB),
     )(tx_cell, rx_cell, rx_weight.reshape(1, -1), left, mid, right)
 
-    rows = lax.all_to_all(rows, GRID_AXES, 0, 0)
+    rows = lax.all_to_all(rows, ("piece", "lat"), 0, 0)
     moved = pl.pallas_call(
         functools.partial(update_kernel, sizes),
         out_shape=jax.ShapeDtypeStruct((depths, 12, ROWS, LANES), f32),
@@ -467,7 +525,7 @@
         out_specs=in_vmem(),
         compiler_params=params(vmem_limit_bytes=8 * MIB),
     )(rows, mid, basis)
-    moved = lax.all_to_all(moved, "depth", 0, 0)
+    moved = lax.all_to_all(moved, DEPTH, 0, 0)
     fields, terms = pl.pallas_call(
         functools.partial(output_kernel, pieces),
         out_shape=(
@@ -483,16 +541,21 @@
 
 
 def solution(mesh):
+    grid = mesh.devices
+    split = Mesh(
+        grid.reshape((KINDS, grid.shape[0] // KINDS) + grid.shape[1:]),
+        DEPTH + tuple(mesh.axis_names[1:]),
+    )
     return jax.shard_map(
         local,
-        mesh=mesh,
+        mesh=split,
         in_specs=(
-            P("depth", "lat", None),
-            P("tx", None, None, None, "depth", "lat", None),
+            P(DEPTH, "lat", None),
+            P("tx", None, None, None, DEPTH, "lat", None),
             P("tx"),
             P("tx", None),
             P("tx", None, None),
         ),
-        out_specs=(P("tx", None, None, None, "depth", "lat", None), P("depth", "lat", "tx")),
+        out_specs=(P("tx", None, None, None, DEPTH, "lat", None), P(DEPTH, "lat", "tx")),
         check_vma=False,
     )

time: 117 us -> 104 us (0.89)
  Pallas kernels: 21.5 us -> 11.3 us
  blocking collectives: 78.5 us -> 75.6 us
    pallas_call x1, Pallas kernels: 19.1 us -> 8.88 us  [local(): pl.pallas_call(functools.partial(basis_kernel, sizes), out_shape=(jax.Sha...]
    all_to_all x3, blocking collectives: 60.5 us -> 57.7 us  [the longest x1 24.4 us: local(): mid = lax.all_to_all(packed, DEPTH, 0, 0)]
where the time goes in v2:
time: 104 us; the launch traced here: 102 us
  blocking collectives  75.6 us (73%)
  Pallas kernels  11.3 us (11%)
  waiting for transfers between devices  7.19 us (7%)
  starting transfers between devices  4.32 us (4%)
  local copies, waits for them, and re-layouts  2 us (2%)
  between operations  1.34 us (1%)
    all_to_all x1, blocking collectives, local(): mid = lax.all_to_all(packed, DEPTH, 0, 0)  24.4 us
    all_to_all x1, blocking collectives, local(): moved = lax.all_to_all(moved, DEPTH, 0, 0)  19.5 us
    all_to_all x1, blocking collectives, local(): gradient = jnp.sum(lax.all_to_all(terms, 'tx', 0, 0), axis=0)  18 us
    all_to_all x1, blocking collectives, local(): rows = lax.all_to_all(rows, ('piece', 'lat'), 0, 0)  13.7 us
    pallas_call x1, Pallas kernels, local(): pl.pallas_call(functools.partial(basis_kernel, sizes), out_shape=(jax.Sha...  8.88 us
    ppermute x1, waiting for transfers between devices, local(): left = lax.ppermute(mid, 'lat', [(i, i + 1) for i in range(lats - 1)])  3.82 us
    ppermute x1, waiting for transfers between devices, local(): right = lax.ppermute(mid, 'lat', [(i + 1, i) for i in range(lats - 1)])  3.37 us
    ppermute x1, starting transfers between devices, local(): left = lax.ppermute(mid, 'lat', [(i, i + 1) for i in range(lats - 1)])  2.41 us
  transfers between devices with their start and end apart: 2, of which 2 were waited for; matrix products, arithmetic and copies ran while one was open for 0% of the time, Pallas kernels for 0%

profile of v2, /device:TPU:6, one launch (start us, length us, event | category | flops | bytes accessed | tf_op | source)
XLA Modules:
  0.0 102.4 jit_solution(7188266830752607427)
XLA Ops:
  0.6 0.0 copy-start.3
  0.6 0.0 copy-start.2
  0.7 0.0 copy-start
  0.7 1.0 copy-done
  1.7 0.0 copy-start.1
  1.7 0.8 copy-done.1
  2.4 0.2 shard_map.68
  2.6 24.4 %all_to_all.26.mid_ref.start_ref = f32[8,16,8,128]{3,2,1,0:T(8,128)S(1)} all-to-all(f32[8,16,8,128]{3,2,1,0:T(8,128)S(1)} %shard_map.68), channel_id=1, replica_groups=mesh['kind'=2,'piece'=4,'lat'=16,'tx'=4] {'kind','piece'}, dimensions={0} | all-to-all | bytes 1048576 | tf_op jit(solution)/shard_map/all_to_all | solution.py:504
  27.0 1.9 %collective-permute-start.1 = (f32[8,16,8,128]{3,2,1,0:T(8,128)S(1)}, f32[8,16,8,128]{3,2,1,0:T(8,128)S(1)}, u32[]{:S(2)}, u32[]{:S(2)}) collective-permute-start(f32[8,16,8,128]{3,2,1,0:T(8,128)S(1)} %all_to_all.26.mid_ref.start_ref), channel_id=1, source_target_pairs={{4,0},{8,4},{12,8},{16,12},{20,16},{24,20},{28,24},{32,28},{36,32}... | collective-permute-start | bytes 1572872 | tf_op jit(solution)/shard_map/ppermute | solution.py:506
  28.9 2.4 %collective-permute-start = (f32[8,16,8,128]{3,2,1,0:T(8,128)S(1)}, f32[8,16,8,128]{3,2,1,0:T(8,128)S(1)}, u32[]{:S(2)}, u32[]{:S(2)}) collective-permute-start(f32[8,16,8,128]{3,2,1,0:T(8,128)S(1)} %all_to_all.26.mid_ref.start_ref), channel_id=1, source_target_pairs={{0,4},{4,8},{8,12},{12,16},{16,20},{20,24},{24,28},{28,32},{32,36}... | collective-permute-start | bytes 1572872 | tf_op jit(solution)/shard_map/ppermute | solution.py:505
  32.0 0.0 copy-done.3
  32.0 0.1 copy.9
  32.1 0.1 reshape.15.weight_ref
  32.2 3.4 %collective-permute-done.1.right_ref = f32[8,16,8,128]{3,2,1,0:T(8,128)S(1)} collective-permute-done((f32[8,16,8,128]{3,2,1,0:T(8,128)S(1)}, f32[8,16,8,128]{3,2,1,0:T(8,128)S(1)}, u32[]{:S(2)}, u32[]{:S(2)}) %collective-permute-start.1) | collective-permute-done | bytes 524320 | tf_op jit(solution)/shard_map/ppermute | solution.py:506
  35.6 3.8 %collective-permute-done.left_ref = f32[8,16,8,128]{3,2,1,0:T(8,128)S(1)} collective-permute-done((f32[8,16,8,128]{3,2,1,0:T(8,128)S(1)}, f32[8,16,8,128]{3,2,1,0:T(8,128)S(1)}, u32[]{:S(2)}, u32[]{:S(2)}) %collective-permute-start) | collective-permute-done | bytes 524320 | tf_op jit(solution)/shard_map/ppermute | solution.py:505
  39.4 0.0 copy-done.2
  39.4 8.9 %shard_map.69 = (f32[4,8,12,8,128]{4,3,2,1,0:T(8,128)S(1)}, f32[64,128]{1,0:T(8,128)S(1)}) custom-call(s32[1]{0:T(128)S(6)} %copy.11.tx_ref, s32[1,64]{1,0:T(1,128)S(1)} %copy-done.2, f32[1,128]{1,0:T(1,128)S(1)} %reshape.15.weight_ref, f32[8,16,8,128]{3,2,1,0:T(8,128)S(1)} %collective-permute-done.left_ref, ...), custom_call_target="tpu_custom_call" | custom-call | tf_op jit(solution)/shard_map/pallas_call | solution.py:508
  48.3 13.7 %all_to_all.27 = f32[64,1,128]{2,1,0:T(1,128)S(1)} all-to-all(f32[64,1,128]{2,1,0:T(1,128)S(1)} %bitcast.8), channel_id=1, replica_groups=mesh['kind'=2,'piece'=4,'lat'=16,'tx'=4] {'piece','lat'}, dimensions={0} | all-to-all | bytes 65536 | tf_op jit(solution)/shard_map/all_to_all | solution.py:520
  62.0 1.5 %shard_map.70 = f32[8,12,8,128]{3,2,1,0:T(8,128)S(1)} custom-call(f32[64,128]{1,0:T(8,128)S(1)} %bitcast.7, f32[8,16,8,128]{3,2,1,0:T(8,128)S(1)} %all_to_all.26.mid_ref.start_ref, f32[4,8,12,8,128]{4,3,2,1,0:T(8,128)S(1)} %get-tuple-element.7.basis_ref), custom_call_target="tpu_custom_call" | custom-call | tf_op jit(solution)/shard_map/pallas_call | solution.py:521
  63.5 19.5 %all_to_all.28.in_ref = f32[8,12,8,128]{3,2,1,0:T(8,128)S(1)} all-to-all(f32[8,12,8,128]{3,2,1,0:T(8,128)S(1)} %shard_map.70), channel_id=1, replica_groups=mesh['kind'=2,'piece'=4,'lat'=16,'tx'=4] {'kind','piece'}, dimensions={0} | all-to-all | bytes 786432 | tf_op jit(solution)/shard_map/all_to_all | solution.py:528
  83.0 0.8 shard_map.71
  83.8 18.0 %all_to_all.29 = f32[4,2,8,128]{3,2,1,0:T(8,128)S(1)} all-to-all(f32[4,2,8,128]{3,2,1,0:T(8,128)S(1)} %get-tuple-element.9), channel_id=1, replica_groups=mesh['kind'=2,'piece'=4,'lat'=16,'tx'=4] {'tx'}, dimensions={0} | all-to-all | bytes 65536 | tf_op jit(solution)/shard_map/all_to_all | solution.py:539
  101.8 0.6 reduce_sum.9
Async XLA Ops:
  0.6 31.3 %copy-start.3 = (f32[1,64,2]{1,2,0:T(2,128)S(1)}, f32[1,64,2]{1,2,0:T(2,128)}, u32[]{:S(2)}) copy-start(f32[1,64,2]{1,2,0:T(2,128)} %param.9) | copy-start | bytes 1540
  0.6 38.8 %copy-start.2 = (s32[1,64]{1,0:T(1,128)S(1)}, s32[1,64]{1,0:T(1,128)}, u32[]{:S(2)}) copy-start(s32[1,64]{1,0:T(1,128)} %rx_ref.1) | copy-start | bytes 772
  0.7 1.0 copy-start
  1.7 0.8 copy-start.1
  27.0 8.6 %collective-permute-start.1 = (f32[8,16,8,128]{3,2,1,0:T(8,128)S(1)}, f32[8,16,8,128]{3,2,1,0:T(8,128)S(1)}, u32[]{:S(2)}, u32[]{:S(2)}) collective-permute-start(f32[8,16,8,128]{3,2,1,0:T(8,128)S(1)} %all_to_all.26.mid_ref.start_ref), channel_id=1, source_target_pairs={{4,0},{8,4},{12,8},{16,12},{20,16},{24,20},{28,24},{32,28},{36,32}... | collective-permute-start | bytes 1572872 | tf_op jit(solution)/shard_map/ppermute | solution.py:506
  28.9 10.5 %collective-permute-start = (f32[8,16,8,128]{3,2,1,0:T(8,128)S(1)}, f32[8,16,8,128]{3,2,1,0:T(8,128)S(1)}, u32[]{:S(2)}, u32[]{:S(2)}) collective-permute-start(f32[8,16,8,128]{3,2,1,0:T(8,128)S(1)} %all_to_all.26.mid_ref.start_ref), channel_id=1, source_target_pairs={{0,4},{4,8},{8,12},{12,16},{16,20},{20,24},{24,28},{28,32},{32,36}... | collective-permute-start | bytes 1572872 | tf_op jit(solution)/shard_map/ppermute | solution.py:505

commit v3 on v2

v3 whole, which is shorter than its diff:
```python
import functools

import jax
import jax.numpy as jnp
from jax import lax
from jax.experimental import pallas as pl
from jax.experimental.pallas import tpu as pltpu
from jax.sharding import Mesh
from jax.sharding import PartitionSpec as P

SOURCE = 20.0
KINDS = 2
BASIS = 5
ROWS = 8
LANES = 128
HALF = 64
OWN_ROWS = 2 * ROWS
BASIS_ROWS = OWN_ROWS + ROWS
START_ROWS = OWN_ROWS + 2 * ROWS
DEPTH = ("kind", "piece")
LAT = ("chip", "core")
SPREAD = ("core",) + DEPTH
PAIRS = [(i, j) for i in range(BASIS) for j in range(i, BASIS)]
ENTRIES = [(i, j, part) for i, j in PAIRS for part in range(1 if i == j else 2)]
MIB = 1 << 20


def in_vmem():
    return pl.BlockSpec(memory_space=pltpu.VMEM)


def in_smem():
    return pl.BlockSpec(memory_space=pltpu.SMEM)


def pack_kernel(pieces, guess_ref, cond_ref, out_ref):
    lane = lax.broadcasted_iota(jnp.int32, (ROWS, LANES), 1)
    low = lane < HALF
    blank = jnp.zeros((ROWS, LANES), jnp.float32)
    for kind in range(KINDS):
        planes = []
        for layer in range(2):
            group = []
            for ref, row in [(guess_ref, kind * 12 + n * 2 + layer) for n in range(6)] + [
                (cond_ref, layer)
            ]:
                straight = [ref[row, :, n * LANES : (n + 1) * LANES] for n in range(pieces)]
                group.append((straight, [pltpu.roll(v, HALF, 1) for v in straight]))
            planes.append(group)
        for piece in range(pieces):
            for core in range(2):
                to = (core * KINDS + kind) * pieces + piece
                for number in range(7):
                    first = planes[0][number][core]
                    second = planes[1][number][1 - core]
                    out_ref[to, number] = jnp.where(low, first[piece], second[piece])
                for layer in range(2):
                    edge = blank
                    for number in range(7):
                        straight, turned = planes[layer][number]
                        if core:
                            right = straight[piece + 1] if piece + 1 < pieces else blank
                            left = straight[piece]
                        else:
                            right = turned[piece]
                            left = turned[piece - 1] if piece > 0 else blank
                        ends = jnp.where(lane < 32, right, left)
                        at = 8 * number
                        ends = pltpu.roll(ends, at, 1) if at else ends
                        here = (lane // 8 == number) | (lane // 8 == number + 7)
                        edge = jnp.where(here, ends, edge)
                    out_ref[to, 7 + layer] = edge


def two_sum(a, b):
    total = a + b
    other = total - a
    return total, (a - (total - other)) + (b - other)


def basis_scratch(depths):
    layers = 2 * depths
    f32 = jnp.float32
    return [
        pltpu.VMEM((BASIS, 6, layers + 1, BASIS_ROWS, LANES), f32),
        pltpu.VMEM((7, layers + 1, START_ROWS, LANES), f32),
        pltpu.VMEM((4, START_ROWS, LANES), f32),
        pltpu.VMEM((4, BASIS_ROWS, LANES), f32),
        pltpu.VMEM((layers, BASIS_ROWS, LANES), f32),
        pltpu.VMEM((START_ROWS, LANES), f32),
        pltpu.VMEM((BASIS_ROWS, LANES), f32),
        pltpu.VMEM((2 * len(ENTRIES), ROWS, LANES), f32),
    ]


def basis_kernel(
    sizes, tx_ref, rx_ref, weight_ref, left_ref, mid_ref, right_ref, basis_ref, gram_ref,
    field, start, curl_start, curl, cond, inside_start, inside, acc,
):
    depths, chips, pieces = sizes
    layers = 2 * depths
    width = pieces * LANES
    x_size = chips * OWN_ROWS
    chip = lax.axis_index("chip")
    kind = lax.axis_index("kind")
    x_first = chip * OWN_ROWS
    y_first = (lax.axis_index("piece") * 2 + lax.axis_index("core")) * HALF
    lane = lax.broadcasted_iota(jnp.int32, (ROWS, LANES), 1)
    low = lane < HALF
    blank = jnp.zeros((ROWS, LANES), jnp.float32)

    def within(rows, row):
        lane_w = lax.broadcasted_iota(jnp.int32, (rows, LANES), 1)
        x_at = x_first + row
        y_at = y_first + jnp.where(lane_w >= 96, lane_w - LANES, lane_w)
        good = (x_at >= 0) & (x_at < x_size) & (y_at >= 0) & (y_at < width)
        return jnp.where(good, 1.0, 0.0)

    row_s = lax.broadcasted_iota(jnp.int32, (START_ROWS, LANES), 0)
    inside_start[...] = within(START_ROWS, row_s - ROWS)
    row_b = lax.broadcasted_iota(jnp.int32, (BASIS_ROWS, LANES), 0)
    inside[...] = within(BASIS_ROWS, jnp.where(row_b >= 20, row_b - BASIS_ROWS, row_b))

    received = ((left_ref, 0), (mid_ref, 0), (mid_ref, depths), (right_ref, 0))
    rim = (lane < HALF + 8) | (lane >= LANES - 8)

    def spread(source, carry):
        for number, (ref, first) in enumerate(received):
            at = slice(number * ROWS, (number + 1) * ROWS)
            packs = [ref[first + source, 7], ref[first + source, 8]]
            for item in range(7):
                both = ref[first + source, item]
                for layer in range(2):
                    edge = pltpu.roll(packs[layer], HALF - 8 * item, 1)
                    body = pltpu.roll(both, HALF, 1) if layer else both
                    tile = jnp.where(low, body, jnp.where(rim, edge, 0.0))
                    start[item, 2 * source + layer, at] = tile
        return carry

    lax.fori_loop(0, depths, spread, 0, unroll=2)

    empty_start = jnp.zeros((START_ROWS, LANES), jnp.float32)
    empty = jnp.zeros((BASIS_ROWS, LANES), jnp.float32)
    for component in range(6):
        start[component, layers] = empty_start
        for number in range(BASIS - 1):
            field[number, component, layers] = empty

    def ahead(values, axis):
        return pltpu.roll(values, values.shape[axis] - 1, axis) - values

    def behind(values, axis):
        return values - pltpu.roll(values, 1, axis)

    def curl_ahead(here, above, keep):
        uz, ux, uy = here
        hz = (ahead(uy, 0) - ahead(ux, 1)) * keep
        hx = (ahead(uz, 1) - (above[1] - uy)) * keep
        hy = ((above[0] - ux) - ahead(uz, 0)) * keep
        return hz, hx, hy

    def curl_behind(h, below):
        hz, hx, hy = h
        return (
            behind(hy, 0) - behind(hx, 1),
            behind(hz, 1) - (hy - below[1]),
            (hx - below[0]) - behind(hz, 0),
        )

    def merge(values):
        sides = jnp.where(
            lax.broadcasted_iota(jnp.int32, (ROWS, LANES), 0) < 4,
            values[START_ROWS - ROWS :],
            values[:ROWS],
        )
        return jnp.concatenate([values[ROWS : ROWS + OWN_ROWS], sides], axis=0)

    for number in range(4):
        curl_start[number] = empty_start

    def start_layers(source, carry):
        keep = inside_start[...]
        below = [[curl_start[0], curl_start[1]], [curl_start[2], curl_start[3]]]
        for layer in range(2):
            z = 2 * source + layer
            sigma = start[6, z]
            cond[z] = merge(sigma)
            for part in range(2):
                here = [start[3 * part + c, z] for c in range(3)]
                above = [start[3 * part + c, z + 1] for c in (1, 2)]
                h = curl_ahead(here, above, keep)
                outs = curl_behind(h, below[part])
                below[part] = [h[1], h[2]]
                for component, value in enumerate(outs):
                    other = sigma * start[3 * (1 - part) + component, z]
                    value = other - value if part == 0 else -value - other
                    field[0, 3 * part + component, z] = merge(value) * inside[...]
        for number in range(4):
            curl_start[number] = below[number // 2][number % 2]
        return carry

    lax.fori_loop(0, depths, start_layers, 0, unroll=2)

    line = lax.broadcasted_iota(jnp.int32, (1, LANES), 1)

    def place_of(cell):
        col = (cell & (width - 1)) - y_first
        rest = lax.shift_right_logical(cell, width.bit_length() - 1)
        row = (rest & (x_size - 1)) - x_first
        z = lax.shift_right_logical(rest, x_size.bit_length() - 1)
        return (row >= -4) & (row < OWN_ROWS + 4) & (col >= -8) & (col < HALF + 8), z, row, col

    def add_source(cell, real, imag):
        held, z, row, col = place_of(cell)

        @pl.when(held)
        def _():
            hit = line == (col & (LANES - 1))
            at = pl.ds(jnp.where(row < 0, row + BASIS_ROWS, row), 1)
            field[0, 0, z, at] = field[0, 0, z, at] + jnp.where(hit, real, 0.0)
            field[0, 3, z, at] = field[0, 3, z, at] + jnp.where(hit, imag, 0.0)

    @pl.when(kind == 0)
    def _():
        add_source(tx_ref[0], jnp.float32(0.0), jnp.float32(-SOURCE))

    @pl.when(kind == 1)
    def _():
        def each(group, carry):
            numbers = [8 * group + n for n in range(8)]
            some = place_of(rx_ref[0, numbers[0]])[0]
            for r in numbers[1:]:
                some = some | place_of(rx_ref[0, r])[0]

            @pl.when(some)
            def _():
                for r in numbers:
                    add_source(rx_ref[0, r], weight_ref[0, 2 * r], weight_ref[0, 2 * r + 1])

            return carry

        lax.fori_loop(0, rx_ref.shape[1] // 8, each, 0)

    for step in range(BASIS - 1):
        for number in range(4):
            curl[number] = empty

        def apply_layers(source, carry, step=step):
            keep = inside[...]
            below = [[curl[0], curl[1]], [curl[2], curl[3]]]
            mine = slice(0, OWN_ROWS) if step == BASIS - 2 else slice(0, BASIS_ROWS)
            for layer in range(2):
                z = 2 * source + layer
                sigma = cond[z, mine]
                for part in range(2):
                    here = [field[step, 3 * part + c, z] for c in range(3)]
                    above = [field[step, 3 * part + c, z + 1] for c in (1, 2)]
                    h = curl_ahead(here, above, keep)
                    outs = curl_behind(h, below[part])
                    below[part] = [h[1], h[2]]
                    for component, value in enumerate(outs):
                        value = value[mine]
                        other = sigma * field[step, 3 * (1 - part) + component, z, mine]
                        value = value - other if part == 0 else value + other
                        if step < BASIS - 2:
                            value = value * keep
                        field[step + 1, 3 * part + component, z, mine] = value
            for number in range(4):
                curl[number] = below[number // 2][number % 2]
            return carry

        lax.fori_loop(0, depths, apply_layers, 0, unroll=2)

    for entry in range(2 * len(ENTRIES)):
        acc[entry] = blank

    def gram_layers(source, carry):
        tiles = []
        for b in range(BASIS):
            group = []
            for component in range(6):
                for core in range(2):
                    at = slice(core * ROWS, (core + 1) * ROWS)
                    first = field[b, component, 2 * source, at]
                    second = field[b, component, 2 * source + 1, at]
                    group.append(jnp.where(low, first, pltpu.roll(second, HALF, 1)))
                    if b < BASIS - 1:
                        basis_ref[b, core * depths + source, component] = group[-1]
            tiles.append(group)
        for entry, (i, j, part) in enumerate(ENTRIES):
            first, second = tiles[i], tiles[j]
            if part:
                terms = [first[n] * second[n + 6] - first[n + 6] * second[n] for n in range(6)]
            else:
                terms = [first[n] * second[n] + first[n + 6] * second[n + 6] for n in range(6)]
            value = (terms[0] + terms[1]) + (terms[2] + terms[3]) + (terms[4] + terms[5])
            total, error = two_sum(acc[2 * entry], value)
            acc[2 * entry] = total
            acc[2 * entry + 1] = acc[2 * entry + 1] + error
        return carry

    lax.fori_loop(0, depths, gram_layers, 0)

    def fold(high, low, shift, axis):
        total, error = two_sum(high, pltpu.roll(high, shift, axis))
        return total, low + pltpu.roll(low, shift, axis) + error

    sub = lax.broadcasted_iota(jnp.int32, (ROWS, LANES), 0)
    row = blank
    for first in range(0, len(ENTRIES), 8):
        highs, lows = blank, blank
        for entry in range(first, min(first + 8, len(ENTRIES))):
            value, rest = acc[2 * entry], acc[2 * entry + 1]
            for shift in (4, 2, 1):
                value, rest = fold(value, rest, shift, 0)
            highs = jnp.where(sub == entry - first, value, highs)
            lows = jnp.where(sub == entry - first, rest, lows)
        for shift in (64, 32, 16, 8, 4, 2, 1):
            highs, lows = fold(highs, lows, shift, 1)
        row = jnp.where(lane == sub + first, highs, row)
        row = jnp.where(lane == sub + first + 64, lows, row)
    for shift in (4, 2, 1):
        row = row + pltpu.roll(row, shift, 0)
    for number in range(pieces * chips * 2 // ROWS):
        gram_ref[number * ROWS : (number + 1) * ROWS] = row


def quick(a, b):
    total = a + b
    return total, b - (total - a)


def split(a):
    big = a * 4097.0
    high = big - (big - a)
    return high, a - high


def two_product(a, b):
    value = a * b
    ah, al = split(a)
    bh, bl = split(b)
    return value, ((ah * bh - value) + ah * bl + al * bh) + al * bl


def add(a, b):
    total, error = two_sum(a[0], b[0])
    return quick(total, error + (a[1] + b[1]))


def neg(a):
    return (-a[0], -a[1])


def mul(a, b):
    value, error = two_product(a[0], b[0])
    return quick(value, error + (a[0] * b[1] + a[1] * b[0]))


def div(a, b):
    first = a[0] / b[0]
    zero = jnp.zeros_like(first)
    rest = add(a, neg(mul(b, (first, zero))))
    second = rest[0] / b[0]
    rest = add(rest, neg(mul(b, (second, zero))))
    third = rest[0] / b[0]
    return add(quick(first, second), (third, zero))


def c_add(a, b):
    return (add(a[0], b[0]), add(a[1], b[1]))


def c_neg(a):
    return (neg(a[0]), neg(a[1]))


def c_conj(a):
    return (a[0], neg(a[1]))


def c_mul(a, b):
    return (
        add(mul(a[0], b[0]), neg(mul(a[1], b[1]))),
        add(mul(a[0], b[1]), mul(a[1], b[0])),
    )


def c_div(a, b):
    top = c_mul(a, c_conj(b))
    bottom = add(mul(b[0], b[0]), mul(b[1], b[1]))
    return (div(top[0], bottom), div(top[1], bottom))


def c_over(a, real):
    return (div(a[0], real), div(a[1], real))


def total_of(values):
    result = values[0]
    for value in values[1:]:
        result = c_add(result, value)
    return result


def coefficients(gram):
    rho = gram[0, 0]
    alpha = c_div(rho, gram[0, 1])
    one_half = c_neg(alpha)

    def form(coeffs, left, right):
        rows = []
        for i, factor in enumerate(coeffs):
            inner = total_of(
                [
                    gram[i + left, j + right]
                    if other is None
                    else c_mul(gram[i + left, j + right], other)
                    for j, other in enumerate(coeffs)
                ]
            )
            rows.append(inner if factor is None else c_mul(c_conj(factor), inner))
        return total_of(rows)

    omega = c_over(form([None, one_half], 1, 0), form([None, one_half], 1, 1)[0])
    res1 = c_neg(c_add(alpha, omega))
    res2 = c_mul(alpha, omega)
    new_rho = total_of([gram[0, 0], c_mul(gram[0, 1], res1), c_mul(gram[0, 2], res2)])
    mix = c_mul(c_div(new_rho, rho), c_div(alpha, omega))
    dir0 = (add((jnp.ones_like(mix[0][0]), jnp.zeros_like(mix[0][0])), mix[0]), mix[1])
    dir1 = c_add(res1, c_neg(c_mul(mix, omega)))
    dir2 = res2
    along = total_of(
        [c_mul(gram[0, 1], dir0), c_mul(gram[0, 2], dir1), c_mul(gram[0, 3], dir2)]
    )
    alpha2 = c_div(new_rho, along)
    half1 = c_add(res1, c_neg(c_mul(alpha2, dir0)))
    half2 = c_add(res2, c_neg(c_mul(alpha2, dir1)))
    half3 = c_neg(c_mul(alpha2, dir2))
    half = [None, half1, half2, half3]
    omega2 = c_over(form(half, 1, 0), form(half, 1, 1)[0])
    out0 = total_of([alpha, omega, c_mul(alpha2, dir0), omega2])
    out1 = total_of([c_mul(omega, one_half), c_mul(alpha2, dir1), c_mul(omega2, half1)])
    out2 = c_add(c_mul(alpha2, dir2), c_mul(omega2, half2))
    out3 = c_mul(omega2, half3)
    return [(c[0][0], c[1][0]) for c in (out0, out1, out2, out3)]


def update_kernel(sizes, rows_ref, start_ref, basis_ref, out_ref):
    depths, chips, pieces = sizes
    high = jnp.zeros((ROWS, LANES), jnp.float32)
    low = high
    for number in range(pieces * chips * 2 // ROWS):
        high, error = two_sum(high, rows_ref[number * ROWS : (number + 1) * ROWS])
        low = low + error
    for shift in (4, 2, 1):
        high, error = two_sum(high, pltpu.roll(high, shift, 0))
        low = low + pltpu.roll(low, shift, 0) + error
    high, low = quick(high, low + pltpu.roll(high, 64, 1))

    def entry(number):
        return (
            jnp.broadcast_to(high[:, number : number + 1], (ROWS, LANES)),
            jnp.broadcast_to(low[:, number : number + 1], (ROWS, LANES)),
        )

    zero = jnp.zeros((ROWS, LANES), jnp.float32)
    gram = {}
    at = 0
    for i, j in PAIRS:
        real = entry(at)
        at += 1
        if i == j:
            gram[i, i] = (real, (zero, zero))
        else:
            gram[i, j] = (real, entry(at))
            gram[j, i] = c_conj(gram[i, j])
            at += 1
    factors = coefficients(gram)

    def layer(source, carry):
        for component in range(3):
            real = start_ref[source, component]
            imag = start_ref[source, component + 3]
            for b, (fr, fi) in enumerate(factors):
                br = basis_ref[b, source, component]
                bi = basis_ref[b, source, component + 3]
                real = real + (fr * br - fi * bi)
                imag = imag + (fr * bi + fi * br)
            out_ref[source, component] = real
            out_ref[source, component + 3] = imag
        return carry

    lax.fori_loop(0, 2 * depths, layer, 0, unroll=2)


def output_kernel(pieces, in_ref, field_ref, term_ref):
    low = lax.broadcasted_iota(jnp.int32, (ROWS, LANES), 1) < HALF
    for piece in range(pieces):
        cols = slice(piece * LANES, (piece + 1) * LANES)
        terms = [None, None]
        for component in range(3):
            values = [[], []]
            for kind in range(KINDS):
                for part in range(2):
                    number = 3 * part + component
                    first = in_ref[kind * pieces + piece, number]
                    second = in_ref[(KINDS + kind) * pieces + piece, number]
                    pair = (
                        jnp.where(low, first, pltpu.roll(second, HALF, 1)),
                        jnp.where(low, pltpu.roll(first, HALF, 1), second),
                    )
                    for z in range(2):
                        field_ref[kind * 12 + 2 * number + z, :, cols] = pair[z]
                        values[z].append(pair[z])
            for z in range(2):
                v = values[z]
                product = v[0] * v[2] - v[1] * v[3]
                terms[z] = product if terms[z] is None else terms[z] + product
        for z in range(2):
            term_ref[piece, z] = terms[z]


def local(conductivity, field_guess, tx_cell, rx_cell, rx_weight):
    pieces, chips = lax.axis_size("piece"), lax.axis_size("chip")
    depths = KINDS * pieces
    sizes = (depths, chips, pieces)
    width = conductivity.shape[2]
    f32 = jnp.float32
    params = pltpu.CompilerParams

    packed = pl.pallas_call(
        functools.partial(pack_kernel, pieces),
        out_shape=jax.ShapeDtypeStruct((2 * depths, 9, ROWS, LANES), f32),
        in_specs=[in_vmem()] * 2,
        out_specs=in_vmem(),
        compiler_params=params(vmem_limit_bytes=4 * MIB),
    )(field_guess.reshape(24, ROWS, width), conductivity)
    mid = lax.all_to_all(packed, SPREAD, 0, 0)
    left = lax.ppermute(mid[depths:], "chip", [(i, i + 1) for i in range(chips - 1)])
    right = lax.ppermute(mid[:depths], "chip", [(i + 1, i) for i in range(chips - 1)])

    basis, rows = pl.pallas_call(
        functools.partial(basis_kernel, sizes),
        out_shape=(
            jax.ShapeDtypeStruct((BASIS - 1, 2 * depths, 6, ROWS, LANES), f32),
            jax.ShapeDtypeStruct((pieces * chips * 2, LANES), f32),
        ),
        in_specs=[in_smem()] * 3 + [in_vmem()] * 3,
        out_specs=(in_vmem(), in_vmem()),
        scratch_shapes=basis_scratch(depths),
        compiler_params=params(vmem_limit_bytes=28 * MIB),
    )(tx_cell, rx_cell, rx_weight.reshape(1, -1), left, mid, right)

    rows = lax.all_to_all(rows, ("piece",) + LAT, 0, 0)
    moved = pl.pallas_call(
        functools.partial(update_kernel, sizes),
        out_shape=jax.ShapeDtypeStruct((2 * depths, 6, ROWS, LANES), f32),
        in_specs=[in_vmem()] * 3,
        out_specs=in_vmem(),
        compiler_params=params(vmem_limit_bytes=8 * MIB),
    )(rows, mid, basis)
    moved = lax.all_to_all(moved, SPREAD, 0, 0)
    fields, terms = pl.pallas_call(
        functools.partial(output_kernel, pieces),
        out_shape=(
            jax.ShapeDtypeStruct((24, ROWS, width), f32),
            jax.ShapeDtypeStruct((pieces, 2, ROWS, LANES), f32),
        ),
        in_specs=[in_vmem()],
        out_specs=(in_vmem(), in_vmem()),
        compiler_params=params(vmem_limit_bytes=4 * MIB),
    )(moved)
    gradient = jnp.sum(lax.all_to_all(terms, "tx", 0, 0), axis=0)
    return (fields.reshape(field_guess.shape), gradient)


def solution(mesh):
    grid = mesh.devices
    shape = (KINDS, grid.shape[0] // KINDS, grid.shape[1] // 2, 2, grid.shape[2])
    split = Mesh(grid.reshape(shape), DEPTH + LAT + ("tx",))
    return jax.shard_map(
        local,
        mesh=split,
        in_specs=(
            P(DEPTH, LAT, None),
            P("tx", None, None, None, DEPTH, LAT, None),
            P("tx"),
            P("tx", None),
            P("tx", None, None),
        ),
        out_specs=(P("tx", None, None, None, DEPTH, LAT, None), P(DEPTH, LAT, "tx")),
        check_vma=False,
    )
```

time: 104 us -> 107 us (1.029)
  the two profiles are of different devices: /device:TPU:6 before, /device:TPU:8 now
where the time goes in v3:
time: 107 us
  blocking collectives  81.2 us (76%)
  Pallas kernels  11 us (10%)
  starting transfers between devices  5.86 us (5%)
  waiting for transfers between devices  4.95 us (5%)
  local copies, waits for them, and re-layouts  2.03 us (2%)
  between operations  1.34 us (1%)
    all_to_all x1, blocking collectives, local(): mid = lax.all_to_all(packed, SPREAD, 0, 0)  26.4 us
    all_to_all x1, blocking collectives, local(): moved = lax.all_to_all(moved, SPREAD, 0, 0)  20.3 us
    all_to_all x1, blocking collectives, local(): gradient = jnp.sum(lax.all_to_all(terms, 'tx', 0, 0), axis=0)  17.8 us
    all_to_all x1, blocking collectives, local(): rows = lax.all_to_all(rows, ('piece',) + LAT, 0, 0)  16.6 us
    pallas_call x1, Pallas kernels, local(): pl.pallas_call(functools.partial(basis_kernel, sizes), out_shape=(jax.Sha...  8.17 us
    ppermute x1, starting transfers between devices, local(): lax.ppermute(mid[depths:], 'chip', [(i, i + 1) for i in range(chips - 1)])  4.56 us
    ppermute x1, waiting for transfers between devices, local(): lax.ppermute(mid[:depths], 'chip', [(i + 1, i) for i in range(chips - 1)])  3.77 us
  transfers between devices with their start and end apart: 2, of which 2 were waited for; matrix products, arithmetic and copies ran while one was open for 0% of the time, Pallas kernels for 0%

profile of v3, /device:TPU:8, one launch (start us, length us, event | category | flops | bytes accessed | tf_op | source)
XLA Modules:
  0.0 107.0 jit_solution(1151208769401530040)
XLA Ops:
  0.6 0.0 copy-start
  0.6 1.0 copy-done
  1.6 0.0 copy-start.1
  1.6 0.8 copy-done.1
  2.4 0.0 copy-start.3
  2.4 0.0 copy-start.2
  2.4 0.5 shard_map.68
  2.9 26.4 %all_to_all.26.mid_ref.start_ref = f32[16,9,8,128]{3,2,1,0:T(8,128)S(1)} all-to-all(f32[16,9,8,128]{3,2,1,0:T(8,128)S(1)} %shard_map.68), channel_id=1, replica_groups=mesh['kind'=2,'piece'=4,'chip'=8,'core'=2,'tx'=4] {'core','kind','piece'}, dimensions={0} | all-to-all | bytes 1179648 | tf_op jit(solution)/shard_map/all_to_all | solution.py:539
  29.4 1.3 %collective-permute-start.1 = (f32[8,9,8,128]{3,2,1,0:T(8,128)S(1)}, f32[8,9,8,128]{3,2,1,0:T(8,128)S(1)}, u32[]{:S(2)}, u32[]{:S(2)}) collective-permute-start(f32[8,9,8,128]{3,2,1,0:T(8,128)S(1)} %get-tuple-element.10), channel_id=1, source_target_pairs={{8,0},{16,8},{24,16},{32,24},{40,32},{48,40},{56,48},{9,1},{17,9},... | collective-permute-start | bytes 884744 | tf_op jit(solution)/shard_map/ppermute | solution.py:541
  30.7 4.6 %collective-permute-start = (f32[8,9,8,128]{3,2,1,0:T(8,128)S(1)}, f32[8,9,8,128]{3,2,1,0:T(8,128)S(1)}, u32[]{:S(2)}, u32[]{:S(2)}) collective-permute-start(f32[8,9,8,128]{3,2,1,0:T(8,128)S(1)} %get-tuple-element.11), channel_id=1, source_target_pairs={{0,8},{8,16},{16,24},{24,32},{32,40},{40,48},{48,56},{1,9},{9,17},... | collective-permute-start | bytes 884744 | tf_op jit(solution)/shard_map/ppermute | solution.py:540
  35.9 0.0 copy-done.3
  35.9 0.1 copy.9
  36.0 0.1 reshape.15.weight_ref
  36.1 3.8 %collective-permute-done.1.right_ref = f32[8,9,8,128]{3,2,1,0:T(8,128)S(1)} collective-permute-done((f32[8,9,8,128]{3,2,1,0:T(8,128)S(1)}, f32[8,9,8,128]{3,2,1,0:T(8,128)S(1)}, u32[]{:S(2)}, u32[]{:S(2)}) %collective-permute-start.1) | collective-permute-done | bytes 294944 | tf_op jit(solution)/shard_map/ppermute | solution.py:541
  39.9 1.2 %collective-permute-done.left_ref = f32[8,9,8,128]{3,2,1,0:T(8,128)S(1)} collective-permute-done((f32[8,9,8,128]{3,2,1,0:T(8,128)S(1)}, f32[8,9,8,128]{3,2,1,0:T(8,128)S(1)}, u32[]{:S(2)}, u32[]{:S(2)}) %collective-permute-start) | collective-permute-done | bytes 294944 | tf_op jit(solution)/shard_map/ppermute | solution.py:540
  41.1 0.0 copy-done.2
  41.1 8.2 %shard_map.69 = (f32[4,16,6,8,128]{4,3,2,1,0:T(8,128)S(1)}, f32[64,128]{1,0:T(8,128)S(1)}) custom-call(s32[1]{0:T(128)S(6)} %copy.11.tx_ref, s32[1,64]{1,0:T(1,128)S(1)} %copy-done.2, f32[1,128]{1,0:T(1,128)S(1)} %reshape.15.weight_ref, f32[8,9,8,128]{3,2,1,0:T(8,128)S(1)} %collective-permute-done.left_ref, ...), custom_call_target="tpu_custom_call" | custom-call | tf_op jit(solution)/shard_map/pallas_call | solution.py:543
  49.3 16.6 %all_to_all.27 = f32[64,1,128]{2,1,0:T(1,128)S(1)} all-to-all(f32[64,1,128]{2,1,0:T(1,128)S(1)} %bitcast.8), channel_id=1, replica_groups=mesh['kind'=2,'piece'=4,'chip'=8,'core'=2,'tx'=4] {'piece','chip','core'}, dimensions={0} | all-to-all | bytes 65536 | tf_op jit(solution)/shard_map/all_to_all | solution.py:555
  65.9 1.5 %shard_map.70 = f32[16,6,8,128]{3,2,1,0:T(8,128)S(1)} custom-call(f32[64,128]{1,0:T(8,128)S(1)} %bitcast.7, f32[16,9,8,128]{3,2,1,0:T(8,128)S(1)} %all_to_all.26.mid_ref.start_ref, f32[4,16,6,8,128]{4,3,2,1,0:T(8,128)S(1)} %get-tuple-element.7.basis_ref), custom_call_target="tpu_custom_call" | custom-call | tf_op jit(solution)/shard_map/pallas_call | solution.py:556
  67.3 20.3 %all_to_all.28.in_ref = f32[16,6,8,128]{3,2,1,0:T(8,128)S(1)} all-to-all(f32[16,6,8,128]{3,2,1,0:T(8,128)S(1)} %shard_map.70), channel_id=1, replica_groups=mesh['kind'=2,'piece'=4,'chip'=8,'core'=2,'tx'=4] {'core','kind','piece'}, dimensions={0} | all-to-all | bytes 786432 | tf_op jit(solution)/shard_map/all_to_all | solution.py:563
  87.6 0.9 shard_map.71
  88.5 17.8 %all_to_all.29 = f32[4,2,8,128]{3,2,1,0:T(8,128)S(1)} all-to-all(f32[4,2,8,128]{3,2,1,0:T(8,128)S(1)} %get-tuple-element.9), channel_id=1, replica_groups=mesh['kind'=2,'piece'=4,'chip'=8,'core'=2,'tx'=4] {'tx'}, dimensions={0} | all-to-all | bytes 65536 | tf_op jit(solution)/shard_map/all_to_all | solution.py:574
  106.4 0.6 reduce_sum.9
  (1 shorter events, 0.0 us)
Async XLA Ops:
  0.6 1.0 copy-start
  1.6 0.8 copy-start.1
  2.4 33.5 %copy-start.3 = (f32[1,64,2]{1,2,0:T(2,128)S(1)}, f32[1,64,2]{1,2,0:T(2,128)}, u32[]{:S(2)}) copy-start(f32[1,64,2]{1,2,0:T(2,128)} %param.9) | copy-start | bytes 1540
  2.4 38.7 %copy-start.2 = (s32[1,64]{1,0:T(1,128)S(1)}, s32[1,64]{1,0:T(1,128)}, u32[]{:S(2)}) copy-start(s32[1,64]{1,0:T(1,128)} %rx_ref.1) | copy-start | bytes 772
  29.4 10.5 %collective-permute-start.1 = (f32[8,9,8,128]{3,2,1,0:T(8,128)S(1)}, f32[8,9,8,128]{3,2,1,0:T(8,128)S(1)}, u32[]{:S(2)}, u32[]{:S(2)}) collective-permute-start(f32[8,9,8,128]{3,2,1,0:T(8,128)S(1)} %get-tuple-element.10), channel_id=1, source_target_pairs={{8,0},{16,8},{24,16},{32,24},{40,32},{48,40},{56,48},{9,1},{17,9},... | collective-permute-start | bytes 884744 | tf_op jit(solution)/shard_map/ppermute | solution.py:541
  30.7 10.4 %collective-permute-start = (f32[8,9,8,128]{3,2,1,0:T(8,128)S(1)}, f32[8,9,8,128]{3,2,1,0:T(8,128)S(1)}, u32[]{:S(2)}, u32[]{:S(2)}) collective-permute-start(f32[8,9,8,128]{3,2,1,0:T(8,128)S(1)} %get-tuple-element.11), channel_id=1, source_target_pairs={{0,8},{8,16},{16,24},{24,32},{32,40},{40,48},{48,56},{1,9},{9,17},... | collective-permute-start | bytes 884744 | tf_op jit(solution)/shard_map/ppermute | solution.py:540

commit v4 on v2

--- a/solution.py
+++ b/solution.py
@@ -79,7 +79,7 @@
 
 
 def basis_kernel(
-    sizes, tx_ref, rx_ref, weight_ref, left_ref, mid_ref, right_ref, basis_ref, gram_ref,
+    sizes, tx_ref, rx_ref, weight_ref, outer_ref, mid_ref, inner_ref, basis_ref, gram_ref,
     field, edges, curl_start, curl, cond, inside_start, inside, acc,
 ):
     depths, lats, pieces = sizes
@@ -104,11 +104,17 @@
     row_b = lax.broadcasted_iota(jnp.int32, (2 * ROWS, span), 0)
     inside[...] = within(2 * ROWS, jnp.where(row_b >= 12, row_b - 16, row_b))
 
-    received = (left_ref, mid_ref, right_ref)
+    first_core = lat_index % 2 == 0
+
+    def received(source, item):
+        outer, inner = outer_ref[source, item], inner_ref[source, item]
+        left = jnp.where(first_core, outer, inner)
+        right = jnp.where(first_core, inner, outer)
+        return left, mid_ref[source, item], right
+
 
     def spread(source, carry):
-        for number, ref in enumerate(received):
-            packs = [ref[source, 14], ref[source, 15]]
+        for number, packs in enumerate(zip(received(source, 14), received(source, 15))):
             for item in range(14):
                 edge = pltpu.roll(packs[item // 8], LANES - (16 * (item % 8) + 8), 1)
                 edge = jnp.where((lane < 8) | (lane >= LANES - 8), edge, blank)
@@ -145,7 +151,7 @@
         )
 
     def start_tile(number, z, source, layer):
-        body = jnp.concatenate([ref[source, 2 * number + layer] for ref in received], axis=0)
+        body = jnp.concatenate(received(source, 2 * number + layer), axis=0)
         return jnp.concatenate([body, edges[number, z]], axis=1)
 
     def merge(values):
@@ -190,13 +196,17 @@
 
     line = lax.broadcasted_iota(jnp.int32, (1, span), 1)
 
-    def add_source(cell, real, imag):
+    def place_of(cell):
         col = (cell & (width - 1)) - piece * LANES
         rest = lax.shift_right_logical(cell, width.bit_length() - 1)
         row = (rest & (lats * ROWS - 1)) - lat_index * ROWS
         z = lax.shift_right_logical(rest, (lats * ROWS).bit_length() - 1)
-
-        @pl.when((row >= -4) & (row < 12) & (col >= -8) & (col < LANES + 8))
+        return (row >= -4) & (row < 12) & (col >= -8) & (col < LANES + 8), z, row, col
+
+    def add_source(cell, real, imag):
+        held, z, row, col = place_of(cell)
+
+        @pl.when(held)
         def _():
             hit = line == (col & (span - 1))
             at = pl.ds(row & (2 * ROWS - 1), 1)
@@ -209,11 +219,20 @@
 
     @pl.when(kind == 1)
     def _():
-        def each(r, carry):
-            add_source(rx_ref[0, r], weight_ref[0, 2 * r], weight_ref[0, 2 * r + 1])
+        def each(group, carry):
+            numbers = [8 * group + n for n in range(8)]
+            some = place_of(rx_ref[0, numbers[0]])[0]
+            for r in numbers[1:]:
+                some = some | place_of(rx_ref[0, r])[0]
+
+            @pl.when(some)
+            def _():
+                for r in numbers:
+                    add_source(rx_ref[0, r], weight_ref[0, 2 * r], weight_ref[0, 2 * r + 1])
+
             return carry
 
-        lax.fori_loop(0, rx_ref.shape[1], each, 0)
+        lax.fori_loop(0, rx_ref.shape[1] // 8, each, 0)
 
     for step in range(BASIS - 1):
         for number in range(4):
@@ -252,27 +271,30 @@
     for entry in range(2 * len(ENTRIES)):
         acc[entry] = blank
 
-    def gram_layer(source, carry):
-        for layer in range(2):
-            z = 2 * source + layer
-            tiles = [[field[b, c, z, 0:ROWS, 0:LANES] for c in range(6)] for b in range(BASIS)]
-            for b in range(BASIS - 1):
-                for c in range(6):
-                    basis_ref[b, source, 2 * c + layer] = tiles[b][c]
-            for entry, (i, j, part) in enumerate(ENTRIES):
-                first, second = tiles[i], tiles[j]
-                if part == 0:
-                    terms = [first[c] * second[c] for c in range(6)]
-                    value = (terms[0] + terms[3]) + (terms[1] + terms[4]) + (terms[2] + terms[5])
-                else:
-                    terms = [first[c] * second[c + 3] - first[c + 3] * second[c] for c in range(3)]
-                    value = terms[0] + terms[1] + terms[2]
-                total, error = two_sum(acc[2 * entry], value)
-                acc[2 * entry] = total
-                acc[2 * entry + 1] = acc[2 * entry + 1] + error
+    def gram_layers(source, carry):
+        tiles = []
+        for b in range(BASIS):
+            group = []
+            for component in range(6):
+                for layer in range(2):
+                    tile = field[b, component, 2 * source + layer, 0:ROWS, 0:LANES]
+                    group.append(tile)
+                    if b < BASIS - 1:
+                        basis_ref[b, source, 2 * component + layer] = tile
+            tiles.append(group)
+        for entry, (i, j, part) in enumerate(ENTRIES):
+            first, second = tiles[i], tiles[j]
+            if part:
+                terms = [first[n] * second[n + 6] - first[n + 6] * second[n] for n in range(6)]
+            else:
+                terms = [first[n] * second[n] + first[n + 6] * second[n + 6] for n in range(6)]
+            value = (terms[0] + terms[1]) + (terms[2] + terms[3]) + (terms[4] + terms[5])
+            total, error = two_sum(acc[2 * entry], value)
+            acc[2 * entry] = total
+            acc[2 * entry + 1] = acc[2 * entry + 1] + error
         return carry
 
-    lax.fori_loop(0, depths, gram_layer, 0, unroll=2)
+    lax.fori_loop(0, depths, gram_layers, 0)
 
     def fold(high, low, shift, axis):
         total, error = two_sum(high, pltpu.roll(high, shift, axis))
@@ -502,8 +524,9 @@
         compiler_params=params(vmem_limit_bytes=4 * MIB),
     )(field_guess.reshape(24, ROWS, width), conductivity)
     mid = lax.all_to_all(packed, DEPTH, 0, 0)
-    left = lax.ppermute(mid, "lat", [(i, i + 1) for i in range(lats - 1)])
-    right = lax.ppermute(mid, "lat", [(i + 1, i) for i in range(lats - 1)])
+    border = [(i, i + 1) for i in range(1, lats - 1, 2)]
+    outer = lax.ppermute(mid, "lat", border + [(b, a) for a, b in border])
+    inner = lax.ppermute(mid, "lat", [(i, i ^ 1) for i in range(lats)])
 
     basis, rows = pl.pallas_call(
         functools.partial(basis_kernel, sizes),
@@ -515,7 +538,7 @@
         out_specs=(in_vmem(), in_vmem()),
         scratch_shapes=basis_scratch(depths),
         compiler_params=params(vmem_limit_bytes=28 * MIB),
-    )(tx_cell, rx_cell, rx_weight.reshape(1, -1), left, mid, right)
+    )(tx_cell, rx_cell, rx_weight.reshape(1, -1), outer, mid, inner)
 
     rows = lax.all_to_all(rows, ("piece", "lat"), 0, 0)
     moved = pl.pallas_call(

time: 104 us -> 103 us (level)
  transfers between devices with their start and end apart: 2 -> 2, of which waited for: 2 -> 1; matrix products, arithmetic and copies ran while one was open for 0% -> 0% of each run, Pallas kernels for 0% -> 0%
where the time goes in v4:
time: 103 us; the launch traced here: 101 us
  blocking collectives  74.7 us (73%)
  Pallas kernels  11.2 us (11%)
  waiting for transfers between devices  6.75 us (7%)
  starting transfers between devices  4.75 us (5%)
  local copies, waits for them, and re-layouts  2 us (2%)
  between operations  1.35 us (1%)
    all_to_all x1, blocking collectives, local(): mid = lax.all_to_all(packed, DEPTH, 0, 0)  24.4 us
    all_to_all x1, blocking collectives, local(): moved = lax.all_to_all(moved, DEPTH, 0, 0)  18.5 us
    all_to_all x1, blocking collectives, local(): gradient = jnp.sum(lax.all_to_all(terms, 'tx', 0, 0), axis=0)  17.9 us
    all_to_all x1, blocking collectives, local(): rows = lax.all_to_all(rows, ('piece', 'lat'), 0, 0)  13.9 us
    pallas_call x1, Pallas kernels, local(): pl.pallas_call(functools.partial(basis_kernel, sizes), out_shape=(jax.Sha...  8.81 us
    ppermute x1, waiting for transfers between devices, local(): outer = lax.ppermute(mid, 'lat', border + [(b, a) for a, b in border])  6.75 us
    ppermute x1, starting transfers between devices, local(): outer = lax.ppermute(mid, 'lat', border + [(b, a) for a, b in border])  2.84 us
  transfers between devices with their start and end apart: 2, of which 1 were waited for; matrix products, arithmetic and copies ran while one was open for 0% of the time, Pallas kernels for 0%

profile of v4, /device:TPU:6, one launch (start us, length us, event | category | flops | bytes accessed | tf_op | source)
XLA Modules:
  0.0 101.4 jit_solution(6307519169590732824)
XLA Ops:
  0.6 0.0 copy-start.3
  0.6 0.0 copy-start.2
  0.7 0.0 copy-start
  0.7 1.0 copy-done
  1.7 0.0 copy-start.1
  1.7 0.8 copy-done.1
  2.4 0.2 shard_map.68
  2.6 24.4 %all_to_all.26.mid_ref.start_ref = f32[8,16,8,128]{3,2,1,0:T(8,128)S(1)} all-to-all(f32[8,16,8,128]{3,2,1,0:T(8,128)S(1)} %shard_map.68), channel_id=1, replica_groups=mesh['kind'=2,'piece'=4,'lat'=16,'tx'=4] {'kind','piece'}, dimensions={0} | all-to-all | bytes 1048576 | tf_op jit(solution)/shard_map/all_to_all | solution.py:526
  27.0 1.9 %collective-permute-start.1 = (f32[8,16,8,128]{3,2,1,0:T(8,128)S(1)}, f32[8,16,8,128]{3,2,1,0:T(8,128)S(1)}, u32[]{:S(2)}, u32[]{:S(2)}) collective-permute-start(f32[8,16,8,128]{3,2,1,0:T(8,128)S(1)} %all_to_all.26.mid_ref.start_ref), channel_id=1, source_target_pairs={{0,4},{4,0},{8,12},{12,8},{16,20},{20,16},{24,28},{28,24},{32,36},... | collective-permute-start | bytes 1572872 | tf_op jit(solution)/shard_map/ppermute | solution.py:529
  28.9 2.8 %collective-permute-start = (f32[8,16,8,128]{3,2,1,0:T(8,128)S(1)}, f32[8,16,8,128]{3,2,1,0:T(8,128)S(1)}, u32[]{:S(2)}, u32[]{:S(2)}) collective-permute-start(f32[8,16,8,128]{3,2,1,0:T(8,128)S(1)} %all_to_all.26.mid_ref.start_ref), channel_id=1, source_target_pairs={{4,8},{12,16},{20,24},{28,32},{36,40},{44,48},{52,56},{8,4},{16,12... | collective-permute-start | bytes 1572872 | tf_op jit(solution)/shard_map/ppermute | solution.py:528
  32.4 0.0 copy-done.3
  32.4 0.1 copy.9
  32.5 0.1 reshape.15.weight_ref
  32.7 0.0 collective-permute-done.1.inner_ref
  32.7 6.7 %collective-permute-done.outer_ref = f32[8,16,8,128]{3,2,1,0:T(8,128)S(1)} collective-permute-done((f32[8,16,8,128]{3,2,1,0:T(8,128)S(1)}, f32[8,16,8,128]{3,2,1,0:T(8,128)S(1)}, u32[]{:S(2)}, u32[]{:S(2)}) %collective-permute-start) | collective-permute-done | bytes 524320 | tf_op jit(solution)/shard_map/ppermute | solution.py:528
  39.4 0.0 copy-done.2
  39.4 8.8 %shard_map.69 = (f32[4,8,12,8,128]{4,3,2,1,0:T(8,128)S(1)}, f32[64,128]{1,0:T(8,128)S(1)}) custom-call(s32[1]{0:T(128)S(6)} %copy.11.tx_ref, s32[1,64]{1,0:T(1,128)S(1)} %copy-done.2, f32[1,128]{1,0:T(1,128)S(1)} %reshape.15.weight_ref, f32[8,16,8,128]{3,2,1,0:T(8,128)S(1)} %collective-permute-done.outer_ref, ...), custom_call_target="tpu_custom_call" | custom-call | tf_op jit(solution)/shard_map/pallas_call | solution.py:531
  48.2 13.9 %all_to_all.27 = f32[64,1,128]{2,1,0:T(1,128)S(1)} all-to-all(f32[64,1,128]{2,1,0:T(1,128)S(1)} %bitcast.8), channel_id=1, replica_groups=mesh['kind'=2,'piece'=4,'lat'=16,'tx'=4] {'piece','lat'}, dimensions={0} | all-to-all | bytes 65536 | tf_op jit(solution)/shard_map/all_to_all | solution.py:543
  62.1 1.5 %shard_map.70 = f32[8,12,8,128]{3,2,1,0:T(8,128)S(1)} custom-call(f32[64,128]{1,0:T(8,128)S(1)} %bitcast.7, f32[8,16,8,128]{3,2,1,0:T(8,128)S(1)} %all_to_all.26.mid_ref.start_ref, f32[4,8,12,8,128]{4,3,2,1,0:T(8,128)S(1)} %get-tuple-element.7.basis_ref), custom_call_target="tpu_custom_call" | custom-call | tf_op jit(solution)/shard_map/pallas_call | solution.py:544
  63.6 18.5 %all_to_all.28.in_ref = f32[8,12,8,128]{3,2,1,0:T(8,128)S(1)} all-to-all(f32[8,12,8,128]{3,2,1,0:T(8,128)S(1)} %shard_map.70), channel_id=1, replica_groups=mesh['kind'=2,'piece'=4,'lat'=16,'tx'=4] {'kind','piece'}, dimensions={0} | all-to-all | bytes 786432 | tf_op jit(solution)/shard_map/all_to_all | solution.py:551
  82.1 0.8 shard_map.71
  82.9 17.9 %all_to_all.29 = f32[4,2,8,128]{3,2,1,0:T(8,128)S(1)} all-to-all(f32[4,2,8,128]{3,2,1,0:T(8,128)S(1)} %get-tuple-element.9), channel_id=1, replica_groups=mesh['kind'=2,'piece'=4,'lat'=16,'tx'=4] {'tx'}, dimensions={0} | all-to-all | bytes 65536 | tf_op jit(solution)/shard_map/all_to_all | solution.py:562
  100.8 0.6 reduce_sum.9
Async XLA Ops:
  0.6 31.8 %copy-start.3 = (f32[1,64,2]{1,2,0:T(2,128)S(1)}, f32[1,64,2]{1,2,0:T(2,128)}, u32[]{:S(2)}) copy-start(f32[1,64,2]{1,2,0:T(2,128)} %param.9) | copy-start | bytes 1540
  0.6 38.8 %copy-start.2 = (s32[1,64]{1,0:T(1,128)S(1)}, s32[1,64]{1,0:T(1,128)}, u32[]{:S(2)}) copy-start(s32[1,64]{1,0:T(1,128)} %rx_ref.1) | copy-start | bytes 772
  0.7 1.0 copy-start
  1.7 0.8 copy-start.1
  27.0 5.7 %collective-permute-start.1 = (f32[8,16,8,128]{3,2,1,0:T(8,128)S(1)}, f32[8,16,8,128]{3,2,1,0:T(8,128)S(1)}, u32[]{:S(2)}, u32[]{:S(2)}) collective-permute-start(f32[8,16,8,128]{3,2,1,0:T(8,128)S(1)} %all_to_all.26.mid_ref.start_ref), channel_id=1, source_target_pairs={{0,4},{4,0},{8,12},{12,8},{16,20},{20,16},{24,28},{28,24},{32,36},... | collective-permute-start | bytes 1572872 | tf_op jit(solution)/shard_map/ppermute | solution.py:529
  28.9 10.5 %collective-permute-start = (f32[8,16,8,128]{3,2,1,0:T(8,128)S(1)}, f32[8,16,8,128]{3,2,1,0:T(8,128)S(1)}, u32[]{:S(2)}, u32[]{:S(2)}) collective-permute-start(f32[8,16,8,128]{3,2,1,0:T(8,128)S(1)} %all_to_all.26.mid_ref.start_ref), channel_id=1, source_target_pairs={{4,8},{12,16},{20,24},{28,32},{36,40},{44,48},{52,56},{8,4},{16,12... | collective-permute-start | bytes 1572872 | tf_op jit(solution)/shard_map/ppermute | solution.py:528

commit v5 on v4

--- a/solution.py
+++ b/solution.py
@@ -79,7 +79,7 @@
 
 
 def basis_kernel(
-    sizes, tx_ref, rx_ref, weight_ref, outer_ref, mid_ref, inner_ref, basis_ref, gram_ref,
+    sizes, tx_ref, rx_ref, weight_ref, inner_ref, mid_ref, outer_ref, basis_ref, gram_ref,
     field, edges, curl_start, curl, cond, inside_start, inside, acc,
 ):
     depths, lats, pieces = sizes
@@ -525,8 +525,8 @@
     )(field_guess.reshape(24, ROWS, width), conductivity)
     mid = lax.all_to_all(packed, DEPTH, 0, 0)
     border = [(i, i + 1) for i in range(1, lats - 1, 2)]
+    inner = lax.ppermute(mid, "lat", [(i, i ^ 1) for i in range(lats)])
     outer = lax.ppermute(mid, "lat", border + [(b, a) for a, b in border])
-    inner = lax.ppermute(mid, "lat", [(i, i ^ 1) for i in range(lats)])
 
     basis, rows = pl.pallas_call(
         functools.partial(basis_kernel, sizes),
@@ -538,7 +538,7 @@
         out_specs=(in_vmem(), in_vmem()),
         scratch_shapes=basis_scratch(depths),
         compiler_params=params(vmem_limit_bytes=28 * MIB),
-    )(tx_cell, rx_cell, rx_weight.reshape(1, -1), outer, mid, inner)
+    )(tx_cell, rx_cell, rx_weight.reshape(1, -1), inner, mid, outer)
 
     rows = lax.all_to_all(rows, ("piece", "lat"), 0, 0)
     moved = pl.pallas_call(

time: 103 us -> 99.7 us (0.968)
  waiting for transfers between devices: 6.75 us -> 3.37 us
  starting transfers between devices: 4.75 us -> 6.21 us
    ppermute x1, waiting for transfers between devices: 6.75 us -> 3.37 us  [local(): outer = lax.ppermute(mid, 'lat', border + [(b, a) for a, b in border])]
    ppermute x1, starting transfers between devices: 1.91 us -> 4.3 us  [local(): inner = lax.ppermute(mid, 'lat', [(i, i ^ 1) for i in range(lats)])]
where the time goes in v5:
time: 99.7 us; the launch traced here: 98.4 us
  blocking collectives  73.7 us (74%)
  Pallas kernels  11.2 us (11%)
  starting transfers between devices  6.21 us (6%)
  waiting for transfers between devices  3.37 us (3%)
  local copies, waits for them, and re-layouts  2 us (2%)
  between operations  1.34 us (1%)
    all_to_all x1, blocking collectives, local(): mid = lax.all_to_all(packed, DEPTH, 0, 0)  24.4 us
    all_to_all x1, blocking collectives, local(): moved = lax.all_to_all(moved, DEPTH, 0, 0)  18.4 us
    all_to_all x1, blocking collectives, local(): gradient = jnp.sum(lax.all_to_all(terms, 'tx', 0, 0), axis=0)  17.1 us
    all_to_all x1, blocking collectives, local(): rows = lax.all_to_all(rows, ('piece', 'lat'), 0, 0)  13.7 us
    pallas_call x1, Pallas kernels, local(): pl.pallas_call(functools.partial(basis_kernel, sizes), out_shape=(jax.Sha...  8.81 us
    ppermute x1, starting transfers between devices, local(): inner = lax.ppermute(mid, 'lat', [(i, i ^ 1) for i in range(lats)])  4.3 us
    ppermute x1, waiting for transfers between devices, local(): outer = lax.ppermute(mid, 'lat', border + [(b, a) for a, b in border])  3.37 us
  transfers between devices with their start and end apart: 2, of which 1 were waited for; matrix products, arithmetic and copies ran while one was open for 0% of the time, Pallas kernels for 0%

profile of v5, /device:TPU:6, one launch (start us, length us, event | category | flops | bytes accessed | tf_op | source)
XLA Modules:
  0.0 98.4 jit_solution(16211945134347321144)
XLA Ops:
  0.6 0.0 copy-start.3
  0.6 0.0 copy-start.2
  0.7 0.0 copy-start
  0.7 1.0 %copy-done = f32[1,2,2,3,2,8,512]{6,5,4,3,2,1,0:T(8,128)S(1)} copy-done((f32[1,2,2,3,2,8,512]{6,5,4,3,2,1,0:T(8,128)S(1)}, f32[1,2,2,3,2,8,512]{6,5,4,3,2,1,0:T(8,128)}, u32[]{:S(2)}) %copy-start) | copy-done | bytes 393240
  1.7 0.0 copy-start.1
  1.7 0.8 copy-done.1
  2.4 0.2 shard_map.68
  2.6 24.4 %all_to_all.26.mid_ref.start_ref = f32[8,16,8,128]{3,2,1,0:T(8,128)S(1)} all-to-all(f32[8,16,8,128]{3,2,1,0:T(8,128)S(1)} %shard_map.68), channel_id=1, replica_groups=mesh['kind'=2,'piece'=4,'lat'=16,'tx'=4] {'kind','piece'}, dimensions={0} | all-to-all | bytes 1048576 | tf_op jit(solution)/shard_map/all_to_all | solution.py:526
  27.0 1.9 %collective-permute-start.1 = (f32[8,16,8,128]{3,2,1,0:T(8,128)S(1)}, f32[8,16,8,128]{3,2,1,0:T(8,128)S(1)}, u32[]{:S(2)}, u32[]{:S(2)}) collective-permute-start(f32[8,16,8,128]{3,2,1,0:T(8,128)S(1)} %all_to_all.26.mid_ref.start_ref), channel_id=1, source_target_pairs={{4,8},{12,16},{20,24},{28,32},{36,40},{44,48},{52,56},{8,4},{16,12... | collective-permute-start | bytes 1572872 | tf_op jit(solution)/shard_map/ppermute | solution.py:529
  28.9 4.3 %collective-permute-start = (f32[8,16,8,128]{3,2,1,0:T(8,128)S(1)}, f32[8,16,8,128]{3,2,1,0:T(8,128)S(1)}, u32[]{:S(2)}, u32[]{:S(2)}) collective-permute-start(f32[8,16,8,128]{3,2,1,0:T(8,128)S(1)} %all_to_all.26.mid_ref.start_ref), channel_id=1, source_target_pairs={{0,4},{4,0},{8,12},{12,8},{16,20},{20,16},{24,28},{28,24},{32,36},... | collective-permute-start | bytes 1572872 | tf_op jit(solution)/shard_map/ppermute | solution.py:528
  33.9 0.0 copy-done.3
  33.9 0.1 copy.9
  34.0 0.1 reshape.15.weight_ref
  34.1 3.4 %collective-permute-done.1.outer_ref = f32[8,16,8,128]{3,2,1,0:T(8,128)S(1)} collective-permute-done((f32[8,16,8,128]{3,2,1,0:T(8,128)S(1)}, f32[8,16,8,128]{3,2,1,0:T(8,128)S(1)}, u32[]{:S(2)}, u32[]{:S(2)}) %collective-permute-start.1) | collective-permute-done | bytes 524320 | tf_op jit(solution)/shard_map/ppermute | solution.py:529
  37.5 0.0 collective-permute-done.inner_ref
  37.5 0.0 copy-done.2
  37.5 8.8 %shard_map.69 = (f32[4,8,12,8,128]{4,3,2,1,0:T(8,128)S(1)}, f32[64,128]{1,0:T(8,128)S(1)}) custom-call(s32[1]{0:T(128)S(6)} %copy.11.tx_ref, s32[1,64]{1,0:T(1,128)S(1)} %copy-done.2, f32[1,128]{1,0:T(1,128)S(1)} %reshape.15.weight_ref, f32[8,16,8,128]{3,2,1,0:T(8,128)S(1)} %collective-permute-done.inner_ref, ...), custom_call_target="tpu_custom_call" | custom-call | tf_op jit(solution)/shard_map/pallas_call | solution.py:531
  46.3 13.7 %all_to_all.27 = f32[64,1,128]{2,1,0:T(1,128)S(1)} all-to-all(f32[64,1,128]{2,1,0:T(1,128)S(1)} %bitcast.8), channel_id=1, replica_groups=mesh['kind'=2,'piece'=4,'lat'=16,'tx'=4] {'piece','lat'}, dimensions={0} | all-to-all | bytes 65536 | tf_op jit(solution)/shard_map/all_to_all | solution.py:543
  60.0 1.5 %shard_map.70 = f32[8,12,8,128]{3,2,1,0:T(8,128)S(1)} custom-call(f32[64,128]{1,0:T(8,128)S(1)} %bitcast.7, f32[8,16,8,128]{3,2,1,0:T(8,128)S(1)} %all_to_all.26.mid_ref.start_ref, f32[4,8,12,8,128]{4,3,2,1,0:T(8,128)S(1)} %get-tuple-element.7.basis_ref), custom_call_target="tpu_custom_call" | custom-call | tf_op jit(solution)/shard_map/pallas_call | solution.py:544
  61.5 18.4 %all_to_all.28.in_ref = f32[8,12,8,128]{3,2,1,0:T(8,128)S(1)} all-to-all(f32[8,12,8,128]{3,2,1,0:T(8,128)S(1)} %shard_map.70), channel_id=1, replica_groups=mesh['kind'=2,'piece'=4,'lat'=16,'tx'=4] {'kind','piece'}, dimensions={0} | all-to-all | bytes 786432 | tf_op jit(solution)/shard_map/all_to_all | solution.py:551
  79.9 0.8 shard_map.71
  80.7 17.1 %all_to_all.29 = f32[4,2,8,128]{3,2,1,0:T(8,128)S(1)} all-to-all(f32[4,2,8,128]{3,2,1,0:T(8,128)S(1)} %get-tuple-element.9), channel_id=1, replica_groups=mesh['kind'=2,'piece'=4,'lat'=16,'tx'=4] {'tx'}, dimensions={0} | all-to-all | bytes 65536 | tf_op jit(solution)/shard_map/all_to_all | solution.py:562
  97.8 0.6 reduce_sum.9
Async XLA Ops:
  0.6 33.2 %copy-start.3 = (f32[1,64,2]{1,2,0:T(2,128)S(1)}, f32[1,64,2]{1,2,0:T(2,128)}, u32[]{:S(2)}) copy-start(f32[1,64,2]{1,2,0:T(2,128)} %param.9) | copy-start | bytes 1540
  0.6 36.9 %copy-start.2 = (s32[1,64]{1,0:T(1,128)S(1)}, s32[1,64]{1,0:T(1,128)}, u32[]{:S(2)}) copy-start(s32[1,64]{1,0:T(1,128)} %rx_ref.1) | copy-start | bytes 772
  0.7 1.0 %copy-start = (f32[1,2,2,3,2,8,512]{6,5,4,3,2,1,0:T(8,128)S(1)}, f32[1,2,2,3,2,8,512]{6,5,4,3,2,1,0:T(8,128)}, u32[]{:S(2)}) copy-start(f32[1,2,2,3,2,8,512]{6,5,4,3,2,1,0:T(8,128)} %param.6) | copy-start | bytes 1179652
  1.7 0.8 copy-start.1
  27.0 10.5 %collective-permute-start.1 = (f32[8,16,8,128]{3,2,1,0:T(8,128)S(1)}, f32[8,16,8,128]{3,2,1,0:T(8,128)S(1)}, u32[]{:S(2)}, u32[]{:S(2)}) collective-permute-start(f32[8,16,8,128]{3,2,1,0:T(8,128)S(1)} %all_to_all.26.mid_ref.start_ref), channel_id=1, source_target_pairs={{4,8},{12,16},{20,24},{28,32},{36,40},{44,48},{52,56},{8,4},{16,12... | collective-permute-start | bytes 1572872 | tf_op jit(solution)/shard_map/ppermute | solution.py:529
  28.9 8.6 %collective-permute-start = (f32[8,16,8,128]{3,2,1,0:T(8,128)S(1)}, f32[8,16,8,128]{3,2,1,0:T(8,128)S(1)}, u32[]{:S(2)}, u32[]{:S(2)}) collective-permute-start(f32[8,16,8,128]{3,2,1,0:T(8,128)S(1)} %all_to_all.26.mid_ref.start_ref), channel_id=1, source_target_pairs={{0,4},{4,0},{8,12},{12,8},{16,20},{20,16},{24,28},{28,24},{32,36},... | collective-permute-start | bytes 1572872 | tf_op jit(solution)/shard_map/ppermute | solution.py:528

commit v6 on v5

--- a/solution.py
+++ b/solution.py
@@ -63,12 +63,80 @@
     return total, (a - (total - other)) + (b - other)
 
 
+def edge_columns(ref, source, item, lane):
+    edge = pltpu.roll(ref[source, 14 + item // 8], LANES - (16 * (item % 8) + 8), 1)
+    return jnp.where((lane < 8) | (lane >= LANES - 8), edge, 0.0)
+
+
+def early_kernel(sizes, tx_ref, rx_ref, weight_ref, mid_ref, edge_ref, source_ref):
+    depths, lats, pieces = sizes
+    span = 2 * LANES
+    width = pieces * LANES
+    lat_index = lax.axis_index("lat")
+    kind = lax.axis_index("kind")
+    piece = lax.axis_index("piece")
+    lane = lax.broadcasted_iota(jnp.int32, (ROWS, LANES), 1)
+
+    def spread(source, carry):
+        for number, ref in enumerate((mid_ref,)):
+            rows = slice(number * ROWS, (number + 1) * ROWS)
+            for item in range(14):
+                edge = edge_columns(ref, source, item, lane)
+                edge_ref[item // 2, 2 * source + item % 2, rows] = edge
+        return carry
+
+    lax.fori_loop(0, depths, spread, 0, unroll=2)
+
+    for z in range(2 * depths):
+        for part in range(2):
+            source_ref[part, z] = jnp.zeros((2 * ROWS, span), jnp.float32)
+    line = lax.broadcasted_iota(jnp.int32, (1, span), 1)
+
+    def place_of(cell):
+        col = (cell & (width - 1)) - piece * LANES
+        rest = lax.shift_right_logical(cell, width.bit_length() - 1)
+        row = (rest & (lats * ROWS - 1)) - lat_index * ROWS
+        z = lax.shift_right_logical(rest, (lats * ROWS).bit_length() - 1)
+        return (row >= -4) & (row < 12) & (col >= -8) & (col < LANES + 8), z, row, col
+
+    def add_source(cell, real, imag):
+        held, z, row, col = place_of(cell)
+
+        @pl.when(held)
+        def _():
+            hit = line == (col & (span - 1))
+            at = pl.ds(row & (2 * ROWS - 1), 1)
+            source_ref[0, z, at] = source_ref[0, z, at] + jnp.where(hit, real, 0.0)
+            source_ref[1, z, at] = source_ref[1, z, at] + jnp.where(hit, imag, 0.0)
+
+    @pl.when(kind == 0)
+    def _():
+        add_source(tx_ref[0], jnp.float32(0.0), jnp.float32(-SOURCE))
+
+    @pl.when(kind == 1)
+    def _():
+        def each(group, carry):
+            numbers = [8 * group + n for n in range(8)]
+            some = place_of(rx_ref[0, numbers[0]])[0]
+            for r in numbers[1:]:
+                some = some | place_of(rx_ref[0, r])[0]
+
+            @pl.when(some)
+            def _():
+                for r in numbers:
+                    add_source(rx_ref[0, r], weight_ref[0, 2 * r], weight_ref[0, 2 * r + 1])
+
+            return carry
+
+        lax.fori_loop(0, rx_ref.shape[1] // 8, each, 0)
+
+
 def basis_scratch(depths):
     layers = 2 * depths
     f32 = jnp.float32
     return [
         pltpu.VMEM((BASIS, 6, layers + 1, 2 * ROWS, 2 * LANES), f32),
-        pltpu.VMEM((7, layers, 3 * ROWS, LANES), f32),
+        pltpu.VMEM((7, layers, 2 * ROWS, LANES), f32),
         pltpu.VMEM((4, 3 * ROWS, 2 * LANES), f32),
         pltpu.VMEM((4, 2 * ROWS, 2 * LANES), f32),
         pltpu.VMEM((layers, 2 * ROWS, 2 * LANES), f32),
@@ -79,7 +147,7 @@
 
 
 def basis_kernel(
-    sizes, tx_ref, rx_ref, weight_ref, inner_ref, mid_ref, outer_ref, basis_ref, gram_ref,
+    sizes, edge_ref, source_ref, inner_ref, mid_ref, outer_ref, basis_ref, gram_ref,
     field, edges, curl_start, curl, cond, inside_start, inside, acc,
 ):
     depths, lats, pieces = sizes
@@ -114,12 +182,12 @@
 
 
     def spread(source, carry):
-        for number, packs in enumerate(zip(received(source, 14), received(source, 15))):
-            for item in range(14):
-                edge = pltpu.roll(packs[item // 8], LANES - (16 * (item % 8) + 8), 1)
-                edge = jnp.where((lane < 8) | (lane >= LANES - 8), edge, blank)
-                at = slice(number * ROWS, (number + 1) * ROWS)
-                edges[item // 2, 2 * source + item % 2, at] = edge
+        for item in range(14):
+            at = (item // 2, 2 * source + item % 2)
+            outer = edge_columns(outer_ref, source, item, lane)
+            inner = edge_columns(inner_ref, source, item, lane)
+            edges[at + (slice(0, ROWS),)] = jnp.where(first_core, outer, inner)
+            edges[at + (slice(ROWS, 2 * ROWS),)] = jnp.where(first_core, inner, outer)
         return carry
 
     lax.fori_loop(0, depths, spread, 0, unroll=2)
@@ -152,7 +220,9 @@
 
     def start_tile(number, z, source, layer):
         body = jnp.concatenate(received(source, 2 * number + layer), axis=0)
-        return jnp.concatenate([body, edges[number, z]], axis=1)
+        left, right = edges[number, z, :ROWS], edges[number, z, ROWS:]
+        edge = jnp.concatenate([left, edge_ref[number, z, 0:ROWS], right], axis=0)
+        return jnp.concatenate([body, edge], axis=1)
 
     def merge(values):
         sub = lax.broadcasted_iota(jnp.int32, (ROWS, span), 0)
@@ -187,52 +257,15 @@
                 for component, value in enumerate(outs):
                     other = sigma * tiles[3 * (1 - part) + component]
                     value = other - value if part == 0 else -value - other
-                    field[0, 3 * part + component, z] = merge(value) * inside[...]
+                    value = merge(value) * inside[...]
+                    if component == 0:
+                        value = value + source_ref[part, z]
+                    field[0, 3 * part + component, z] = value
         for number in range(4):
             curl_start[number] = below[number // 2][number % 2]
         return carry
 
     lax.fori_loop(0, depths, start_layers, 0)
-
-    line = lax.broadcasted_iota(jnp.int32, (1, span), 1)
-
-    def place_of(cell):
-        col = (cell & (width - 1)) - piece * LANES
-        rest = lax.shift_right_logical(cell, width.bit_length() - 1)
-        row = (rest & (lats * ROWS - 1)) - lat_index * ROWS
-        z = lax.shift_right_logical(rest, (lats * ROWS).bit_length() - 1)
-        return (row >= -4) & (row < 12) & (col >= -8) & (col < LANES + 8), z, row, col
-
-    def add_source(cell, real, imag):
-        held, z, row, col = place_of(cell)
-
-        @pl.when(held)
-        def _():
-            hit = line == (col & (span - 1))
-            at = pl.ds(row & (2 * ROWS - 1), 1)
-            field[0, 0, z, at] = field[0, 0, z, at] + jnp.where(hit, real, 0.0)
-            field[0, 3, z, at] = field[0, 3, z, at] + jnp.where(hit, imag, 0.0)
-
-    @pl.when(kind == 0)
-    def _():
-        add_source(tx_ref[0], jnp.float32(0.0), jnp.float32(-SOURCE))
-
-    @pl.when(kind == 1)
-    def _():
-        def each(group, carry):
-            numbers = [8 * group + n for n in range(8)]
-            some = place_of(rx_ref[0, numbers[0]])[0]
-            for r in numbers[1:]:
-                some = some | place_of(rx_ref[0, r])[0]
-
-            @pl.when(some)
-            def _():
-                for r in numbers:
-                    add_source(rx_ref[0, r], weight_ref[0, 2 * r], weight_ref[0, 2 * r + 1])
-
-            return carry
-
-        lax.fori_loop(0, rx_ref.shape[1] // 8, each, 0)
 
     for step in range(BASIS - 1):
         for number in range(4):
@@ -528,17 +561,27 @@
     inner = lax.ppermute(mid, "lat", [(i, i ^ 1) for i in range(lats)])
     outer = lax.ppermute(mid, "lat", border + [(b, a) for a, b in border])
 
+    edges, sources = pl.pallas_call(
+        functools.partial(early_kernel, sizes),
+        out_shape=(
+            jax.ShapeDtypeStruct((7, 2 * depths, ROWS, LANES), f32),
+            jax.ShapeDtypeStruct((2, 2 * depths, 2 * ROWS, 2 * LANES), f32),
+        ),
+        in_specs=[in_smem()] * 3 + [in_vmem()],
+        out_specs=(in_vmem(), in_vmem()),
+        compiler_params=params(vmem_limit_bytes=8 * MIB),
+    )(tx_cell, rx_cell, rx_weight.reshape(1, -1), mid)
     basis, rows = pl.pallas_call(
         functools.partial(basis_kernel, sizes),
         out_shape=(
             jax.ShapeDtypeStruct((BASIS - 1, depths, 12, ROWS, LANES), f32),
             jax.ShapeDtypeStruct((pieces * lats, LANES), f32),
         ),
-        in_specs=[in_smem()] * 3 + [in_vmem()] * 3,
+        in_specs=[in_vmem()] * 5,
         out_specs=(in_vmem(), in_vmem()),
         scratch_shapes=basis_scratch(depths),
         compiler_params=params(vmem_limit_bytes=28 * MIB),
-    )(tx_cell, rx_cell, rx_weight.reshape(1, -1), inner, mid, outer)
+    )(edges, sources, inner, mid, outer)
 
     rows = lax.all_to_all(rows, ("piece", "lat"), 0, 0)
     moved = pl.pallas_call(

time: 99.7 us -> 98.4 us (0.987)
  transfers between devices with their start and end apart: 2 -> 2, of which waited for: 1 -> 1; matrix products, arithmetic and copies ran while one was open for 0% -> 0% of each run, Pallas kernels for 0% -> 1%
where the time goes in v6:
time: 98.4 us; the launch traced here: 97.2 us
  blocking collectives  73.1 us (74%)
  Pallas kernels  11.6 us (12%)
  starting transfers between devices  6.21 us (6%)
  waiting for transfers between devices  2.39 us (2%)
  local copies, waits for them, and re-layouts  2 us (2%)
  between operations  1.36 us (1%)
    all_to_all x1, blocking collectives, local(): mid = lax.all_to_all(packed, DEPTH, 0, 0)  24.4 us
    all_to_all x1, blocking collectives, local(): moved = lax.all_to_all(moved, DEPTH, 0, 0)  17.9 us
    all_to_all x1, blocking collectives, local(): gradient = jnp.sum(lax.all_to_all(terms, 'tx', 0, 0), axis=0)  17.1 us
    all_to_all x1, blocking collectives, local(): rows = lax.all_to_all(rows, ('piece', 'lat'), 0, 0)  13.7 us
    pallas_call x1, Pallas kernels, local(): pl.pallas_call(functools.partial(basis_kernel, sizes), out_shape=(jax.Sha...  8.18 us
    ppermute x1, starting transfers between devices, local(): inner = lax.ppermute(mid, 'lat', [(i, i ^ 1) for i in range(lats)])  4.3 us
    ppermute x1, waiting for transfers between devices, local(): outer = lax.ppermute(mid, 'lat', border + [(b, a) for a, b in border])  2.39 us
  transfers between devices with their start and end apart: 2, of which 1 were waited for; matrix products, arithmetic and copies ran while one was open for 0% of the time, Pallas kernels for 1%

profile of v6, /device:TPU:6, one launch (start us, length us, event | category | flops | bytes accessed | tf_op | source)
XLA Modules:
  0.0 97.2 jit_solution(14353374968107925270)
XLA Ops:
  0.6 0.0 copy-start.3
  0.6 0.0 copy-start.2
  0.7 0.0 copy-start
  0.7 1.0 %copy-done = f32[1,2,2,3,2,8,512]{6,5,4,3,2,1,0:T(8,128)S(1)} copy-done((f32[1,2,2,3,2,8,512]{6,5,4,3,2,1,0:T(8,128)S(1)}, f32[1,2,2,3,2,8,512]{6,5,4,3,2,1,0:T(8,128)}, u32[]{:S(2)}) %copy-start) | copy-done | bytes 393240
  1.7 0.0 copy-start.1
  1.7 0.8 copy-done.1
  2.4 0.2 shard_map.68
  2.6 24.4 %all_to_all.26.mid_ref.start_ref = f32[8,16,8,128]{3,2,1,0:T(8,128)S(1)} all-to-all(f32[8,16,8,128]{3,2,1,0:T(8,128)S(1)} %shard_map.68), channel_id=1, replica_groups=mesh['kind'=2,'piece'=4,'lat'=16,'tx'=4] {'kind','piece'}, dimensions={0} | all-to-all | bytes 1048576 | tf_op jit(solution)/shard_map/all_to_all | solution.py:559
  27.0 1.9 %collective-permute-start.1 = (f32[8,16,8,128]{3,2,1,0:T(8,128)S(1)}, f32[8,16,8,128]{3,2,1,0:T(8,128)S(1)}, u32[]{:S(2)}, u32[]{:S(2)}) collective-permute-start(f32[8,16,8,128]{3,2,1,0:T(8,128)S(1)} %all_to_all.26.mid_ref.start_ref), channel_id=1, source_target_pairs={{4,8},{12,16},{20,24},{28,32},{36,40},{44,48},{52,56},{8,4},{16,12... | collective-permute-start | bytes 1572872 | tf_op jit(solution)/shard_map/ppermute | solution.py:562
  28.9 4.3 %collective-permute-start = (f32[8,16,8,128]{3,2,1,0:T(8,128)S(1)}, f32[8,16,8,128]{3,2,1,0:T(8,128)S(1)}, u32[]{:S(2)}, u32[]{:S(2)}) collective-permute-start(f32[8,16,8,128]{3,2,1,0:T(8,128)S(1)} %all_to_all.26.mid_ref.start_ref), channel_id=1, source_target_pairs={{0,4},{4,0},{8,12},{12,8},{16,20},{20,16},{24,28},{28,24},{32,36},... | collective-permute-start | bytes 1572872 | tf_op jit(solution)/shard_map/ppermute | solution.py:561
  33.9 0.0 copy-done.3
  33.9 0.1 copy.9
  34.0 0.1 reshape.15.weight_ref
  34.1 0.0 copy-done.2
  34.1 1.0 shard_map.69
  35.1 2.4 %collective-permute-done.1.outer_ref = f32[8,16,8,128]{3,2,1,0:T(8,128)S(1)} collective-permute-done((f32[8,16,8,128]{3,2,1,0:T(8,128)S(1)}, f32[8,16,8,128]{3,2,1,0:T(8,128)S(1)}, u32[]{:S(2)}, u32[]{:S(2)}) %collective-permute-start.1) | collective-permute-done | bytes 524320 | tf_op jit(solution)/shard_map/ppermute | solution.py:562
  37.5 0.0 collective-permute-done.inner_ref
  37.5 8.2 %shard_map.70 = (f32[4,8,12,8,128]{4,3,2,1,0:T(8,128)S(1)}, f32[64,128]{1,0:T(8,128)S(1)}) custom-call(f32[7,16,8,128]{3,2,1,0:T(8,128)S(1)} %get-tuple-element.8.edge_ref, f32[2,16,16,256]{3,2,1,0:T(8,128)S(1)} %get-tuple-element.9.source_ref, f32[8,16,8,128]{3,2,1,0:T(8,128)S(1)} %collective-permute-done.inner_ref, ...), custom_call_target="tpu_custom_call" | custom-call | tf_op jit(solution)/shard_map/pallas_call | solution.py:574
  45.7 13.7 %all_to_all.27 = f32[64,1,128]{2,1,0:T(1,128)S(1)} all-to-all(f32[64,1,128]{2,1,0:T(1,128)S(1)} %bitcast.8), channel_id=1, replica_groups=mesh['kind'=2,'piece'=4,'lat'=16,'tx'=4] {'piece','lat'}, dimensions={0} | all-to-all | bytes 65536 | tf_op jit(solution)/shard_map/all_to_all | solution.py:586
  59.4 1.5 %shard_map.71 = f32[8,12,8,128]{3,2,1,0:T(8,128)S(1)} custom-call(f32[64,128]{1,0:T(8,128)S(1)} %bitcast.7, f32[8,16,8,128]{3,2,1,0:T(8,128)S(1)} %all_to_all.26.mid_ref.start_ref, f32[4,8,12,8,128]{4,3,2,1,0:T(8,128)S(1)} %get-tuple-element.11.basis_ref), custom_call_target="tpu_custom_call" | custom-call | tf_op jit(solution)/shard_map/pallas_call | solution.py:587
  60.9 17.9 %all_to_all.28.in_ref = f32[8,12,8,128]{3,2,1,0:T(8,128)S(1)} all-to-all(f32[8,12,8,128]{3,2,1,0:T(8,128)S(1)} %shard_map.71), channel_id=1, replica_groups=mesh['kind'=2,'piece'=4,'lat'=16,'tx'=4] {'kind','piece'}, dimensions={0} | all-to-all | bytes 786432 | tf_op jit(solution)/shard_map/all_to_all | solution.py:594
  78.8 0.8 shard_map.72
  79.6 17.1 %all_to_all.29 = f32[4,2,8,128]{3,2,1,0:T(8,128)S(1)} all-to-all(f32[4,2,8,128]{3,2,1,0:T(8,128)S(1)} %get-tuple-element.13), channel_id=1, replica_groups=mesh['kind'=2,'piece'=4,'lat'=16,'tx'=4] {'tx'}, dimensions={0} | all-to-all | bytes 65536 | tf_op jit(solution)/shard_map/all_to_all | solution.py:605
  96.6 0.6 reduce_sum.9
Async XLA Ops:
  0.6 33.2 %copy-start.3 = (f32[1,64,2]{1,2,0:T(2,128)S(1)}, f32[1,64,2]{1,2,0:T(2,128)}, u32[]{:S(2)}) copy-start(f32[1,64,2]{1,2,0:T(2,128)} %param.9) | copy-start | bytes 1540
  0.6 33.5 %copy-start.2 = (s32[1,64]{1,0:T(1,128)S(1)}, s32[1,64]{1,0:T(1,128)}, u32[]{:S(2)}) copy-start(s32[1,64]{1,0:T(1,128)} %rx_ref.1) | copy-start | bytes 772
  0.7 1.0 %copy-start = (f32[1,2,2,3,2,8,512]{6,5,4,3,2,1,0:T(8,128)S(1)}, f32[1,2,2,3,2,8,512]{6,5,4,3,2,1,0:T(8,128)}, u32[]{:S(2)}) copy-start(f32[1,2,2,3,2,8,512]{6,5,4,3,2,1,0:T(8,128)} %param.6) | copy-start | bytes 1179652
  1.7 0.8 copy-start.1
  27.0 10.5 %collective-permute-start.1 = (f32[8,16,8,128]{3,2,1,0:T(8,128)S(1)}, f32[8,16,8,128]{3,2,1,0:T(8,128)S(1)}, u32[]{:S(2)}, u32[]{:S(2)}) collective-permute-start(f32[8,16,8,128]{3,2,1,0:T(8,128)S(1)} %all_to_all.26.mid_ref.start_ref), channel_id=1, source_target_pairs={{4,8},{12,16},{20,24},{28,32},{36,40},{44,48},{52,56},{8,4},{16,12... | collective-permute-start | bytes 1572872 | tf_op jit(solution)/shard_map/ppermute | solution.py:562
  28.9 8.6 %collective-permute-start = (f32[8,16,8,128]{3,2,1,0:T(8,128)S(1)}, f32[8,16,8,128]{3,2,1,0:T(8,128)S(1)}, u32[]{:S(2)}, u32[]{:S(2)}) collective-permute-start(f32[8,16,8,128]{3,2,1,0:T(8,128)S(1)} %all_to_all.26.mid_ref.start_ref), channel_id=1, source_target_pairs={{0,4},{4,0},{8,12},{12,8},{16,20},{20,16},{24,28},{28,24},{32,36},... | collective-permute-start | bytes 1572872 | tf_op jit(solution)/shard_map/ppermute | solution.py:561

commit v7 on v6

--- a/solution.py
+++ b/solution.py
@@ -17,6 +17,9 @@
 PAIRS = [(i, j) for i in range(BASIS) for j in range(i, BASIS)]
 ENTRIES = [(i, j, part) for i, j in PAIRS for part in range(1 if i == j else 2)]
 MIB = 1 << 20
+TILES = 16
+NEAR = 5
+NEAR_TILES = TILES * NEAR // ROWS
 
 
 def in_vmem():
@@ -63,8 +66,37 @@
     return total, (a - (total - other)) + (b - other)
 
 
-def edge_columns(ref, source, item, lane):
-    edge = pltpu.roll(ref[source, 14 + item // 8], LANES - (16 * (item % 8) + 8), 1)
+def gather(read, moves, sub):
+    found = {}
+    for tile, row, to in moves:
+        found.setdefault((tile, (to - row) % ROWS), []).append(to)
+    result = jnp.zeros((ROWS, LANES), jnp.float32)
+    for (tile, shift), rows in found.items():
+        value = pltpu.roll(read(tile), shift, 0) if shift else read(tile)
+        result = jnp.where((sub >= min(rows)) & (sub <= max(rows)), value, result)
+    return result
+
+
+def border_kernel(depths, mid_ref, outer_ref, inner_ref):
+    sub = lax.broadcasted_iota(jnp.int32, (ROWS, LANES), 0)
+    first_core = lax.axis_index("lat") % 2 == 0
+
+    def each(source, carry):
+        for number in range(NEAR_TILES):
+            ends = []
+            for first in (0, ROWS - NEAR):
+                places = [divmod(number * ROWS + to, NEAR) for to in range(ROWS)]
+                moves = [(tile, first + row, to) for to, (tile, row) in enumerate(places)]
+                ends.append(gather(lambda n: mid_ref[source, n], moves, sub))
+            outer_ref[source, number] = jnp.where(first_core, ends[0], ends[1])
+            inner_ref[source, number] = jnp.where(first_core, ends[1], ends[0])
+        return carry
+
+    lax.fori_loop(0, depths, each, 0, unroll=2)
+
+
+def edge_columns(packs, item, lane):
+    edge = pltpu.roll(packs[item // 8], LANES - (16 * (item % 8) + 8), 1)
     return jnp.where((lane < 8) | (lane >= LANES - 8), edge, 0.0)
 
 
@@ -78,11 +110,9 @@
     lane = lax.broadcasted_iota(jnp.int32, (ROWS, LANES), 1)
 
     def spread(source, carry):
-        for number, ref in enumerate((mid_ref,)):
-            rows = slice(number * ROWS, (number + 1) * ROWS)
-            for item in range(14):
-                edge = edge_columns(ref, source, item, lane)
-                edge_ref[item // 2, 2 * source + item % 2, rows] = edge
+        packs = [mid_ref[source, 14], mid_ref[source, 15]]
+        for item in range(14):
+            edge_ref[item // 2, 2 * source + item % 2] = edge_columns(packs, item, lane)
         return carry
 
     lax.fori_loop(0, depths, spread, 0, unroll=2)
@@ -136,7 +166,7 @@
     f32 = jnp.float32
     return [
         pltpu.VMEM((BASIS, 6, layers + 1, 2 * ROWS, 2 * LANES), f32),
-        pltpu.VMEM((7, layers, 2 * ROWS, LANES), f32),
+        pltpu.VMEM((7, layers, 2 * ROWS, 2 * LANES), f32),
         pltpu.VMEM((4, 3 * ROWS, 2 * LANES), f32),
         pltpu.VMEM((4, 2 * ROWS, 2 * LANES), f32),
         pltpu.VMEM((layers, 2 * ROWS, 2 * LANES), f32),
@@ -147,8 +177,8 @@
 
 
 def basis_kernel(
-    sizes, edge_ref, source_ref, inner_ref, mid_ref, outer_ref, basis_ref, gram_ref,
-    field, edges, curl_start, curl, cond, inside_start, inside, acc,
+    sizes, edge_ref, source_ref, outer_ref, mid_ref, inner_ref, basis_ref, gram_ref,
+    field, sides, curl_start, curl, cond, inside_start, inside, acc,
 ):
     depths, lats, pieces = sizes
     layers = 2 * depths
@@ -174,20 +204,25 @@
 
     first_core = lat_index % 2 == 0
 
-    def received(source, item):
-        outer, inner = outer_ref[source, item], inner_ref[source, item]
-        left = jnp.where(first_core, outer, inner)
-        right = jnp.where(first_core, inner, outer)
-        return left, mid_ref[source, item], right
-
+    sub = lax.broadcasted_iota(jnp.int32, (ROWS, LANES), 0)
 
     def spread(source, carry):
-        for item in range(14):
-            at = (item // 2, 2 * source + item % 2)
-            outer = edge_columns(outer_ref, source, item, lane)
-            inner = edge_columns(inner_ref, source, item, lane)
-            edges[at + (slice(0, ROWS),)] = jnp.where(first_core, outer, inner)
-            edges[at + (slice(ROWS, 2 * ROWS),)] = jnp.where(first_core, inner, outer)
+        tiles = [], []
+        for number in range(NEAR_TILES):
+            outer, inner = outer_ref[source, number], inner_ref[source, number]
+            tiles[0].append(jnp.where(first_core, outer, inner))
+            tiles[1].append(jnp.where(first_core, inner, outer))
+        for number, first in enumerate((ROWS - NEAR, 0)):
+            found = []
+            for item in range(TILES):
+                places = [divmod(item * NEAR + row, ROWS) for row in range(NEAR)]
+                moves = [(tile, at, first + row) for row, (tile, at) in enumerate(places)]
+                found.append(gather(lambda n: tiles[number][n], moves, sub))
+            for item in range(14):
+                rows = slice(number * ROWS, (number + 1) * ROWS)
+                at = (item // 2, 2 * source + item % 2, rows)
+                sides[at + (slice(0, LANES),)] = found[item]
+                sides[at + (slice(LANES, span),)] = edge_columns(found[14:], item, lane)
         return carry
 
     lax.fori_loop(0, depths, spread, 0, unroll=2)
@@ -219,10 +254,9 @@
         )
 
     def start_tile(number, z, source, layer):
-        body = jnp.concatenate(received(source, 2 * number + layer), axis=0)
-        left, right = edges[number, z, :ROWS], edges[number, z, ROWS:]
-        edge = jnp.concatenate([left, edge_ref[number, z, 0:ROWS], right], axis=0)
-        return jnp.concatenate([body, edge], axis=1)
+        own = jnp.concatenate([mid_ref[source, 2 * number + layer], edge_ref[number, z]], axis=1)
+        left, right = sides[number, z, :ROWS], sides[number, z, ROWS:]
+        return jnp.concatenate([left, own, right], axis=0)
 
     def merge(values):
         sub = lax.broadcasted_iota(jnp.int32, (ROWS, span), 0)
@@ -558,8 +592,16 @@
     )(field_guess.reshape(24, ROWS, width), conductivity)
     mid = lax.all_to_all(packed, DEPTH, 0, 0)
     border = [(i, i + 1) for i in range(1, lats - 1, 2)]
-    inner = lax.ppermute(mid, "lat", [(i, i ^ 1) for i in range(lats)])
-    outer = lax.ppermute(mid, "lat", border + [(b, a) for a, b in border])
+    near_outer, near_inner = pl.pallas_call(
+        functools.partial(border_kernel, depths),
+        out_shape=(jax.ShapeDtypeStruct((depths, NEAR_TILES, ROWS, LANES), f32),) * 2,
+        in_specs=[in_vmem()],
+        out_specs=(in_vmem(), in_vmem()),
+        compiler_params=params(vmem_limit_bytes=4 * MIB),
+    )(mid)
+    border = [(i, i + 1) for i in range(1, lats - 1, 2)]
+    inner = lax.ppermute(near_inner, "lat", [(i, i ^ 1) for i in range(lats)])
+    outer = lax.ppermute(near_outer, "lat", border + [(b, a) for a, b in border])
 
     edges, sources = pl.pallas_call(
         functools.partial(early_kernel, sizes),
@@ -581,7 +623,7 @@
         out_specs=(in_vmem(), in_vmem()),
         scratch_shapes=basis_scratch(depths),
         compiler_params=params(vmem_limit_bytes=28 * MIB),
-    )(edges, sources, inner, mid, outer)
+    )(edges, sources, outer, mid, inner)
 
     rows = lax.all_to_all(rows, ("piece", "lat"), 0, 0)
     moved = pl.pallas_call(

time: 98.4 us -> 96.4 us (0.980)
  waiting for transfers between devices: 2.39 us -> 0.29 us
    ppermute x2, waiting for transfers between devices: 2.39 us -> 0.29 us  [the longest x1 0.28 us: local(): lax.ppermute(near_outer, 'lat', border + [(b, a) for a, b in border])]
where the time goes in v7:
time: 96.4 us; the launch traced here: 95.2 us
  blocking collectives  73.1 us (76%)
  Pallas kernels  11.6 us (12%)
  starting transfers between devices  6.22 us (6%)
  local copies, waits for them, and re-layouts  2 us (2%)
  between operations  1.36 us (1%)
    all_to_all x1, blocking collectives, local(): mid = lax.all_to_all(packed, DEPTH, 0, 0)  24.4 us
    all_to_all x1, blocking collectives, local(): moved = lax.all_to_all(moved, DEPTH, 0, 0)  17.9 us
    all_to_all x1, blocking collectives, local(): gradient = jnp.sum(lax.all_to_all(terms, 'tx', 0, 0), axis=0)  17.1 us
    all_to_all x1, blocking collectives, local(): rows = lax.all_to_all(rows, ('piece', 'lat'), 0, 0)  13.7 us
    pallas_call x1, Pallas kernels, local(): pl.pallas_call(functools.partial(basis_kernel, sizes), out_shape=(jax.Sha...  8.1 us
    ppermute x1, starting transfers between devices, local(): inner = lax.ppermute(near_inner, 'lat', [(i, i ^ 1) for i in range(lats)])  4.3 us
  transfers between devices with their start and end apart: 2, of which 1 were waited for; matrix products, arithmetic and copies ran while one was open for 0% of the time, Pallas kernels for 1%

profile of v7, /device:TPU:6, one launch (start us, length us, event | category | flops | bytes accessed | tf_op | source)
XLA Modules:
  0.0 95.2 jit_solution(14299550816825621609)
XLA Ops:
  0.6 0.0 copy-start.3
  0.6 0.0 copy-start.2
  0.7 0.0 copy-start
  0.7 1.0 %copy-done = f32[1,2,2,3,2,8,512]{6,5,4,3,2,1,0:T(8,128)S(1)} copy-done((f32[1,2,2,3,2,8,512]{6,5,4,3,2,1,0:T(8,128)S(1)}, f32[1,2,2,3,2,8,512]{6,5,4,3,2,1,0:T(8,128)}, u32[]{:S(2)}) %copy-start) | copy-done | bytes 393240
  1.7 0.8 copy-done.1
  2.4 0.2 shard_map.68
  2.6 24.4 %all_to_all.26.mid_ref.start_ref = f32[8,16,8,128]{3,2,1,0:T(8,128)S(1)} all-to-all(f32[8,16,8,128]{3,2,1,0:T(8,128)S(1)} %shard_map.68), channel_id=1, replica_groups=mesh['kind'=2,'piece'=4,'lat'=16,'tx'=4] {'kind','piece'}, dimensions={0} | all-to-all | bytes 1048576 | tf_op jit(solution)/shard_map/all_to_all | solution.py:593
  27.0 0.1 shard_map.70
  27.1 1.9 %collective-permute-start = (f32[8,10,8,128]{3,2,1,0:T(8,128)S(1)}, f32[8,10,8,128]{3,2,1,0:T(8,128)S(1)}, u32[]{:S(2)}, u32[]{:S(2)}) collective-permute-start(f32[8,10,8,128]{3,2,1,0:T(8,128)S(1)} %get-tuple-element.12), channel_id=1, source_target_pairs={{4,8},{12,16},{20,24},{28,32},{36,40},{44,48},{52,56},{8,4},{16,12... | collective-permute-start | bytes 983048 | tf_op jit(solution)/shard_map/ppermute | solution.py:604
  29.0 4.3 %collective-permute-start.1 = (f32[8,10,8,128]{3,2,1,0:T(8,128)S(1)}, f32[8,10,8,128]{3,2,1,0:T(8,128)S(1)}, u32[]{:S(2)}, u32[]{:S(2)}) collective-permute-start(f32[8,10,8,128]{3,2,1,0:T(8,128)S(1)} %get-tuple-element.13), channel_id=1, source_target_pairs={{0,4},{4,0},{8,12},{12,8},{16,20},{20,16},{24,28},{28,24},{32,36},... | collective-permute-start | bytes 983048 | tf_op jit(solution)/shard_map/ppermute | solution.py:603
  34.0 0.0 copy-done.3
  34.0 0.1 copy.9
  34.1 0.1 reshape.15.weight_ref
  34.2 0.0 copy-done.2
  34.3 1.0 %shard_map.69 = (f32[7,16,8,128]{3,2,1,0:T(8,128)S(1)}, f32[2,16,16,256]{3,2,1,0:T(8,128)S(1)}) custom-call(s32[1]{0:T(128)S(6)} %copy.11.tx_ref, s32[1,64]{1,0:T(1,128)S(1)} %copy-done.2, f32[1,128]{1,0:T(1,128)S(1)} %reshape.15.weight_ref, f32[8,16,8,128]{3,2,1,0:T(8,128)S(1)} %all_to_all.26.mid_ref.start_ref), custom_call_target="tpu_custom_call" | custom-call | tf_op jit(solution)/shard_map/pallas_call | solution.py:606
  35.2 0.3 collective-permute-done.outer_ref
  35.5 0.0 collective-permute-done.1.inner_ref
  35.5 8.1 %shard_map.71 = (f32[4,8,12,8,128]{4,3,2,1,0:T(8,128)S(1)}, f32[64,128]{1,0:T(8,128)S(1)}) custom-call(f32[7,16,8,128]{3,2,1,0:T(8,128)S(1)} %get-tuple-element.10.edge_ref, f32[2,16,16,256]{3,2,1,0:T(8,128)S(1)} %get-tuple-element.11.source_ref, f32[8,10,8,128]{3,2,1,0:T(8,128)S(1)} %collective-permute-done.outer_ref, ...), custom_call_target="tpu_custom_call" | custom-call | tf_op jit(solution)/shard_map/pallas_call | solution.py:616
  43.6 13.7 %all_to_all.27 = f32[64,1,128]{2,1,0:T(1,128)S(1)} all-to-all(f32[64,1,128]{2,1,0:T(1,128)S(1)} %bitcast.8), channel_id=1, replica_groups=mesh['kind'=2,'piece'=4,'lat'=16,'tx'=4] {'piece','lat'}, dimensions={0} | all-to-all | bytes 65536 | tf_op jit(solution)/shard_map/all_to_all | solution.py:628
  57.4 1.5 %shard_map.72 = f32[8,12,8,128]{3,2,1,0:T(8,128)S(1)} custom-call(f32[64,128]{1,0:T(8,128)S(1)} %bitcast.7, f32[8,16,8,128]{3,2,1,0:T(8,128)S(1)} %all_to_all.26.mid_ref.start_ref, f32[4,8,12,8,128]{4,3,2,1,0:T(8,128)S(1)} %get-tuple-element.15.basis_ref), custom_call_target="tpu_custom_call" | custom-call | tf_op jit(solution)/shard_map/pallas_call | solution.py:629
  58.8 17.9 %all_to_all.28.in_ref = f32[8,12,8,128]{3,2,1,0:T(8,128)S(1)} all-to-all(f32[8,12,8,128]{3,2,1,0:T(8,128)S(1)} %shard_map.72), channel_id=1, replica_groups=mesh['kind'=2,'piece'=4,'lat'=16,'tx'=4] {'kind','piece'}, dimensions={0} | all-to-all | bytes 786432 | tf_op jit(solution)/shard_map/all_to_all | solution.py:636
  76.7 0.8 shard_map.73
  77.5 17.1 %all_to_all.29 = f32[4,2,8,128]{3,2,1,0:T(8,128)S(1)} all-to-all(f32[4,2,8,128]{3,2,1,0:T(8,128)S(1)} %get-tuple-element.17), channel_id=1, replica_groups=mesh['kind'=2,'piece'=4,'lat'=16,'tx'=4] {'tx'}, dimensions={0} | all-to-all | bytes 65536 | tf_op jit(solution)/shard_map/all_to_all | solution.py:647
  94.6 0.6 reduce_sum.9
  (1 shorter events, 0.0 us)
Async XLA Ops:
  0.6 33.4 %copy-start.3 = (f32[1,64,2]{1,2,0:T(2,128)S(1)}, f32[1,64,2]{1,2,0:T(2,128)}, u32[]{:S(2)}) copy-start(f32[1,64,2]{1,2,0:T(2,128)} %param.9) | copy-start | bytes 1540
  0.6 33.6 %copy-start.2 = (s32[1,64]{1,0:T(1,128)S(1)}, s32[1,64]{1,0:T(1,128)}, u32[]{:S(2)}) copy-start(s32[1,64]{1,0:T(1,128)} %rx_ref.1) | copy-start | bytes 772
  0.7 1.0 %copy-start = (f32[1,2,2,3,2,8,512]{6,5,4,3,2,1,0:T(8,128)S(1)}, f32[1,2,2,3,2,8,512]{6,5,4,3,2,1,0:T(8,128)}, u32[]{:S(2)}) copy-start(f32[1,2,2,3,2,8,512]{6,5,4,3,2,1,0:T(8,128)} %param.6) | copy-start | bytes 1179652
  1.7 0.8 copy-start.1
  27.1 8.4 %collective-permute-start = (f32[8,10,8,128]{3,2,1,0:T(8,128)S(1)}, f32[8,10,8,128]{3,2,1,0:T(8,128)S(1)}, u32[]{:S(2)}, u32[]{:S(2)}) collective-permute-start(f32[8,10,8,128]{3,2,1,0:T(8,128)S(1)} %get-tuple-element.12), channel_id=1, source_target_pairs={{4,8},{12,16},{20,24},{28,32},{36,40},{44,48},{52,56},{8,4},{16,12... | collective-permute-start | bytes 983048 | tf_op jit(solution)/shard_map/ppermute | solution.py:604
  29.0 6.5 %collective-permute-start.1 = (f32[8,10,8,128]{3,2,1,0:T(8,128)S(1)}, f32[8,10,8,128]{3,2,1,0:T(8,128)S(1)}, u32[]{:S(2)}, u32[]{:S(2)}) collective-permute-start(f32[8,10,8,128]{3,2,1,0:T(8,128)S(1)} %get-tuple-element.13), channel_id=1, source_target_pairs={{0,4},{4,0},{8,12},{12,8},{16,20},{20,16},{24,28},{28,24},{32,36},... | collective-permute-start | bytes 983048 | tf_op jit(solution)/shard_map/ppermute | solution.py:603

commit v8 on v7

--- a/solution.py
+++ b/solution.py
@@ -225,7 +225,7 @@
                 sides[at + (slice(LANES, span),)] = edge_columns(found[14:], item, lane)
         return carry
 
-    lax.fori_loop(0, depths, spread, 0, unroll=2)
+    lax.fori_loop(0, depths, spread, 0, unroll=4)
 
     empty = jnp.zeros((2 * ROWS, span), jnp.float32)
     for number in range(BASIS - 1):
@@ -361,7 +361,7 @@
             acc[2 * entry + 1] = acc[2 * entry + 1] + error
         return carry
 
-    lax.fori_loop(0, depths, gram_layers, 0)
+    lax.fori_loop(0, depths, gram_layers, 0, unroll=2)
 
     def fold(high, low, shift, axis):
         total, error = two_sum(high, pltpu.roll(high, shift, axis))
@@ -488,7 +488,7 @@
     res1 = c_neg(c_add(alpha, omega))
     res2 = c_mul(alpha, omega)
     new_rho = total_of([gram[0, 0], c_mul(gram[0, 1], res1), c_mul(gram[0, 2], res2)])
-    mix = c_mul(c_div(new_rho, rho), c_div(alpha, omega))
+    mix = c_mul(c_over(new_rho, rho[0]), c_div(alpha, omega))
     dir0 = (add((jnp.ones_like(mix[0][0]), jnp.zeros_like(mix[0][0])), mix[0]), mix[1])
     dir1 = c_add(res1, c_neg(c_mul(mix, omega)))
     dir2 = res2
@@ -554,7 +554,7 @@
                 out_ref[source, slot(1, component, z)] = imag
         return carry
 
-    lax.fori_loop(0, depths, layer, 0)
+    lax.fori_loop(0, depths, layer, 0, unroll=2)
 
 
 def output_kernel(pieces, in_ref, field_ref, term_ref):

time: 96.4 us -> 96.2 us (level)
  no operation moved by 1% of the time
where the time goes in v8:
time: 96.2 us; the launch traced here: 95 us
  blocking collectives  73.1 us (76%)
  Pallas kernels  11.4 us (12%)
  starting transfers between devices  6.22 us (6%)
  local copies, waits for them, and re-layouts  2 us (2%)
  between operations  1.36 us (1%)
    all_to_all x1, blocking collectives, local(): mid = lax.all_to_all(packed, DEPTH, 0, 0)  24.4 us
    all_to_all x1, blocking collectives, local(): moved = lax.all_to_all(moved, DEPTH, 0, 0)  17.9 us
    all_to_all x1, blocking collectives, local(): gradient = jnp.sum(lax.all_to_all(terms, 'tx', 0, 0), axis=0)  17.1 us
    all_to_all x1, blocking collectives, local(): rows = lax.all_to_all(rows, ('piece', 'lat'), 0, 0)  13.7 us
    pallas_call x1, Pallas kernels, local(): pl.pallas_call(functools.partial(basis_kernel, sizes), out_shape=(jax.Sha...  7.93 us
    ppermute x1, starting transfers between devices, local(): inner = lax.ppermute(near_inner, 'lat', [(i, i ^ 1) for i in range(lats)])  4.3 us
  transfers between devices with their start and end apart: 2, of which 1 were waited for; matrix products, arithmetic and copies ran while one was open for 0% of the time, Pallas kernels for 1%

profile of v8, /device:TPU:6, one launch (start us, length us, event | category | flops | bytes accessed | tf_op | source)
XLA Modules:
  0.0 95.0 jit_solution(4403838729041118923)
XLA Ops:
  0.6 0.0 copy-start.3
  0.6 0.0 copy-start.2
  0.7 0.0 copy-start
  0.7 1.0 %copy-done = f32[1,2,2,3,2,8,512]{6,5,4,3,2,1,0:T(8,128)S(1)} copy-done((f32[1,2,2,3,2,8,512]{6,5,4,3,2,1,0:T(8,128)S(1)}, f32[1,2,2,3,2,8,512]{6,5,4,3,2,1,0:T(8,128)}, u32[]{:S(2)}) %copy-start) | copy-done | bytes 393240
  1.7 0.8 copy-done.1
  2.4 0.2 shard_map.68
  2.6 24.4 %all_to_all.26.mid_ref.start_ref = f32[8,16,8,128]{3,2,1,0:T(8,128)S(1)} all-to-all(f32[8,16,8,128]{3,2,1,0:T(8,128)S(1)} %shard_map.68), channel_id=1, replica_groups=mesh['kind'=2,'piece'=4,'lat'=16,'tx'=4] {'kind','piece'}, dimensions={0} | all-to-all | bytes 1048576 | tf_op jit(solution)/shard_map/all_to_all | solution.py:593
  27.0 0.1 shard_map.70
  27.1 1.9 %collective-permute-start = (f32[8,10,8,128]{3,2,1,0:T(8,128)S(1)}, f32[8,10,8,128]{3,2,1,0:T(8,128)S(1)}, u32[]{:S(2)}, u32[]{:S(2)}) collective-permute-start(f32[8,10,8,128]{3,2,1,0:T(8,128)S(1)} %get-tuple-element.12), channel_id=1, source_target_pairs={{4,8},{12,16},{20,24},{28,32},{36,40},{44,48},{52,56},{8,4},{16,12... | collective-permute-start | bytes 983048 | tf_op jit(solution)/shard_map/ppermute | solution.py:604
  29.0 4.3 %collective-permute-start.1 = (f32[8,10,8,128]{3,2,1,0:T(8,128)S(1)}, f32[8,10,8,128]{3,2,1,0:T(8,128)S(1)}, u32[]{:S(2)}, u32[]{:S(2)}) collective-permute-start(f32[8,10,8,128]{3,2,1,0:T(8,128)S(1)} %get-tuple-element.13), channel_id=1, source_target_pairs={{0,4},{4,0},{8,12},{12,8},{16,20},{20,16},{24,28},{28,24},{32,36},... | collective-permute-start | bytes 983048 | tf_op jit(solution)/shard_map/ppermute | solution.py:603
  34.0 0.0 copy-done.3
  34.0 0.1 copy.9
  34.1 0.1 reshape.15.weight_ref
  34.2 0.0 copy-done.2
  34.3 1.0 %shard_map.69 = (f32[7,16,8,128]{3,2,1,0:T(8,128)S(1)}, f32[2,16,16,256]{3,2,1,0:T(8,128)S(1)}) custom-call(s32[1]{0:T(128)S(6)} %copy.11.tx_ref, s32[1,64]{1,0:T(1,128)S(1)} %copy-done.2, f32[1,128]{1,0:T(1,128)S(1)} %reshape.15.weight_ref, f32[8,16,8,128]{3,2,1,0:T(8,128)S(1)} %all_to_all.26.mid_ref.start_ref), custom_call_target="tpu_custom_call" | custom-call | tf_op jit(solution)/shard_map/pallas_call | solution.py:606
  35.2 0.3 collective-permute-done.outer_ref
  35.5 0.0 collective-permute-done.1.inner_ref
  35.5 7.9 %shard_map.71 = (f32[4,8,12,8,128]{4,3,2,1,0:T(8,128)S(1)}, f32[64,128]{1,0:T(8,128)S(1)}) custom-call(f32[7,16,8,128]{3,2,1,0:T(8,128)S(1)} %get-tuple-element.10.edge_ref, f32[2,16,16,256]{3,2,1,0:T(8,128)S(1)} %get-tuple-element.11.source_ref, f32[8,10,8,128]{3,2,1,0:T(8,128)S(1)} %collective-permute-done.outer_ref, ...), custom_call_target="tpu_custom_call" | custom-call | tf_op jit(solution)/shard_map/pallas_call | solution.py:616
  43.4 13.7 %all_to_all.27 = f32[64,1,128]{2,1,0:T(1,128)S(1)} all-to-all(f32[64,1,128]{2,1,0:T(1,128)S(1)} %bitcast.8), channel_id=1, replica_groups=mesh['kind'=2,'piece'=4,'lat'=16,'tx'=4] {'piece','lat'}, dimensions={0} | all-to-all | bytes 65536 | tf_op jit(solution)/shard_map/all_to_all | solution.py:628
  57.2 1.4 %shard_map.72 = f32[8,12,8,128]{3,2,1,0:T(8,128)S(1)} custom-call(f32[64,128]{1,0:T(8,128)S(1)} %bitcast.7, f32[8,16,8,128]{3,2,1,0:T(8,128)S(1)} %all_to_all.26.mid_ref.start_ref, f32[4,8,12,8,128]{4,3,2,1,0:T(8,128)S(1)} %get-tuple-element.15.basis_ref), custom_call_target="tpu_custom_call" | custom-call | tf_op jit(solution)/shard_map/pallas_call | solution.py:629
  58.6 17.9 %all_to_all.28.in_ref = f32[8,12,8,128]{3,2,1,0:T(8,128)S(1)} all-to-all(f32[8,12,8,128]{3,2,1,0:T(8,128)S(1)} %shard_map.72), channel_id=1, replica_groups=mesh['kind'=2,'piece'=4,'lat'=16,'tx'=4] {'kind','piece'}, dimensions={0} | all-to-all | bytes 786432 | tf_op jit(solution)/shard_map/all_to_all | solution.py:636
  76.5 0.8 shard_map.73
  77.3 17.1 %all_to_all.29 = f32[4,2,8,128]{3,2,1,0:T(8,128)S(1)} all-to-all(f32[4,2,8,128]{3,2,1,0:T(8,128)S(1)} %get-tuple-element.17), channel_id=1, replica_groups=mesh['kind'=2,'piece'=4,'lat'=16,'tx'=4] {'tx'}, dimensions={0} | all-to-all | bytes 65536 | tf_op jit(solution)/shard_map/all_to_all | solution.py:647
  94.4 0.6 reduce_sum.9
  (1 shorter events, 0.0 us)
Async XLA Ops:
  0.6 33.4 %copy-start.3 = (f32[1,64,2]{1,2,0:T(2,128)S(1)}, f32[1,64,2]{1,2,0:T(2,128)}, u32[]{:S(2)}) copy-start(f32[1,64,2]{1,2,0:T(2,128)} %param.9) | copy-start | bytes 1540
  0.6 33.6 %copy-start.2 = (s32[1,64]{1,0:T(1,128)S(1)}, s32[1,64]{1,0:T(1,128)}, u32[]{:S(2)}) copy-start(s32[1,64]{1,0:T(1,128)} %rx_ref.1) | copy-start | bytes 772
  0.7 1.0 %copy-start = (f32[1,2,2,3,2,8,512]{6,5,4,3,2,1,0:T(8,128)S(1)}, f32[1,2,2,3,2,8,512]{6,5,4,3,2,1,0:T(8,128)}, u32[]{:S(2)}) copy-start(f32[1,2,2,3,2,8,512]{6,5,4,3,2,1,0:T(8,128)} %param.6) | copy-start | bytes 1179652
  1.7 0.8 copy-start.1
  27.1 8.4 %collective-permute-start = (f32[8,10,8,128]{3,2,1,0:T(8,128)S(1)}, f32[8,10,8,128]{3,2,1,0:T(8,128)S(1)}, u32[]{:S(2)}, u32[]{:S(2)}) collective-permute-start(f32[8,10,8,128]{3,2,1,0:T(8,128)S(1)} %get-tuple-element.12), channel_id=1, source_target_pairs={{4,8},{12,16},{20,24},{28,32},{36,40},{44,48},{52,56},{8,4},{16,12... | collective-permute-start | bytes 983048 | tf_op jit(solution)/shard_map/ppermute | solution.py:604
  29.0 6.5 %collective-permute-start.1 = (f32[8,10,8,128]{3,2,1,0:T(8,128)S(1)}, f32[8,10,8,128]{3,2,1,0:T(8,128)S(1)}, u32[]{:S(2)}, u32[]{:S(2)}) collective-permute-start(f32[8,10,8,128]{3,2,1,0:T(8,128)S(1)} %get-tuple-element.13), channel_id=1, source_target_pairs={{0,4},{4,0},{8,12},{12,8},{16,20},{20,16},{24,28},{28,24},{32,36},... | collective-permute-start | bytes 983048 | tf_op jit(solution)/shard_map/ppermute | solution.py:603

commit v9 on v8

--- a/solution.py
+++ b/solution.py
@@ -34,10 +34,21 @@
     return (part * 3 + component) * 2 + layer
 
 
-def pack_kernel(pieces, guess_ref, cond_ref, out_ref):
+def pack_kernel(pieces, guess_hbm, cond_hbm, out_ref, guess_ref, cond_ref, arrived):
+    copies = [
+        pltpu.make_async_copy(
+            guess_hbm.at[pl.ds(kind * 12, 12)], guess_ref.at[pl.ds(kind * 12, 12)], arrived.at[kind]
+        )
+        for kind in range(KINDS)
+    ]
+    copies.append(pltpu.make_async_copy(cond_hbm, cond_ref, arrived.at[KINDS]))
+    for copy in copies:
+        copy.start()
+    copies[KINDS].wait()
     lane = lax.broadcasted_iota(jnp.int32, (ROWS, LANES), 1)
     blank = jnp.zeros((ROWS, LANES), jnp.float32)
     for kind in range(KINDS):
+        copies[kind].wait()
         for piece in range(pieces):
             to = kind * pieces + piece
             edges = [blank, blank]
@@ -586,9 +597,13 @@
     packed = pl.pallas_call(
         functools.partial(pack_kernel, pieces),
         out_shape=jax.ShapeDtypeStruct((depths, 16, ROWS, LANES), f32),
-        in_specs=[in_vmem()] * 2,
+        in_specs=[pl.BlockSpec(memory_space=pl.ANY)] * 2,
         out_specs=in_vmem(),
-        compiler_params=params(vmem_limit_bytes=4 * MIB),
+        scratch_shapes=[
+            pltpu.VMEM((24, ROWS, width), f32),
+            pltpu.VMEM(conductivity.shape, f32),
+            pltpu.SemaphoreType.DMA((KINDS + 1,)),
+        ],
     )(field_guess.reshape(24, ROWS, width), conductivity)
     mid = lax.all_to_all(packed, DEPTH, 0, 0)
     border = [(i, i + 1) for i in range(1, lats - 1, 2)]

time: 96.2 us -> 96.5 us (level)
  Pallas kernels: 11.4 us -> 13.3 us
  local copies, waits for them, and re-layouts: 2 us -> 0.24 us
    pallas_call x1, Pallas kernels: 0.18 us -> 2.03 us  [local(): pl.pallas_call(functools.partial(pack_kernel, pieces), out_shape=jax.Shap...]
    unnamed x9 -> x5, local copies, waits for them, and re-layouts: 1.86 us -> 0.1 us
where the time goes in v9:
time: 96.5 us; the launch traced here: 95.3 us
  blocking collectives  73.3 us (76%)
  Pallas kernels  13.3 us (14%)
  starting transfers between devices  6.22 us (6%)
  between operations  1.36 us (1%)
    all_to_all x1, blocking collectives, local(): mid = lax.all_to_all(packed, DEPTH, 0, 0)  24.6 us
    all_to_all x1, blocking collectives, local(): moved = lax.all_to_all(moved, DEPTH, 0, 0)  17.9 us
    all_to_all x1, blocking collectives, local(): gradient = jnp.sum(lax.all_to_all(terms, 'tx', 0, 0), axis=0)  17.1 us
    all_to_all x1, blocking collectives, local(): rows = lax.all_to_all(rows, ('piece', 'lat'), 0, 0)  13.7 us
    pallas_call x1, Pallas kernels, local(): pl.pallas_call(functools.partial(basis_kernel, sizes), out_shape=(jax.Sha...  7.93 us
    ppermute x1, starting transfers between devices, local(): inner = lax.ppermute(near_inner, 'lat', [(i, i ^ 1) for i in range(lats)])  4.3 us
    pallas_call x1, Pallas kernels, local(): pl.pallas_call(functools.partial(pack_kernel, pieces), out_shape=jax.Shap...  2.03 us
  transfers between devices with their start and end apart: 2, of which 1 were waited for; matrix products, arithmetic and copies ran while one was open for 0% of the time, Pallas kernels for 1%

profile of v9, /device:TPU:6, one launch (start us, length us, event | category | flops | bytes accessed | tf_op | source)
XLA Modules:
  0.0 95.3 jit_solution(4313454912173834225)
XLA Ops:
  0.6 0.0 copy-start.1
  0.6 0.0 copy-start
  0.7 2.0 %shard_map.68 = f32[8,16,8,128]{3,2,1,0:T(8,128)} custom-call(f32[24,8,512]{2,1,0:T(8,128)} %bitcast.8, f32[2,8,512]{2,1,0:T(8,128)} %cond_hbm.1), custom_call_target="tpu_custom_call" | custom-call | tf_op jit(solution)/shard_map/pallas_call | solution.py:597
  2.7 24.6 %all_to_all.26.mid_ref.start_ref = f32[8,16,8,128]{3,2,1,0:T(8,128)S(1)} all-to-all(f32[8,16,8,128]{3,2,1,0:T(8,128)} %shard_map.68), channel_id=1, replica_groups=mesh['kind'=2,'piece'=4,'lat'=16,'tx'=4] {'kind','piece'}, dimensions={0} | all-to-all | bytes 1048576 | tf_op jit(solution)/shard_map/all_to_all | solution.py:608
  27.3 0.1 shard_map.70
  27.4 1.9 %collective-permute-start = (f32[8,10,8,128]{3,2,1,0:T(8,128)S(1)}, f32[8,10,8,128]{3,2,1,0:T(8,128)S(1)}, u32[]{:S(2)}, u32[]{:S(2)}) collective-permute-start(f32[8,10,8,128]{3,2,1,0:T(8,128)S(1)} %get-tuple-element.12), channel_id=1, source_target_pairs={{4,8},{12,16},{20,24},{28,32},{36,40},{44,48},{52,56},{8,4},{16,12... | collective-permute-start | bytes 983048 | tf_op jit(solution)/shard_map/ppermute | solution.py:619
  29.3 4.3 %collective-permute-start.1 = (f32[8,10,8,128]{3,2,1,0:T(8,128)S(1)}, f32[8,10,8,128]{3,2,1,0:T(8,128)S(1)}, u32[]{:S(2)}, u32[]{:S(2)}) collective-permute-start(f32[8,10,8,128]{3,2,1,0:T(8,128)S(1)} %get-tuple-element.13), channel_id=1, source_target_pairs={{0,4},{4,0},{8,12},{12,8},{16,20},{20,16},{24,28},{28,24},{32,36},... | collective-permute-start | bytes 983048 | tf_op jit(solution)/shard_map/ppermute | solution.py:618
  34.3 0.0 copy-done.1
  34.3 0.1 copy.9
  34.4 0.1 reshape.15.weight_ref
  34.5 0.0 copy-done
  34.6 1.0 %shard_map.69 = (f32[7,16,8,128]{3,2,1,0:T(8,128)S(1)}, f32[2,16,16,256]{3,2,1,0:T(8,128)S(1)}) custom-call(s32[1]{0:T(128)S(6)} %copy.11.tx_ref, s32[1,64]{1,0:T(1,128)S(1)} %copy-done, f32[1,128]{1,0:T(1,128)S(1)} %reshape.15.weight_ref, f32[8,16,8,128]{3,2,1,0:T(8,128)S(1)} %all_to_all.26.mid_ref.start_ref), custom_call_target="tpu_custom_call" | custom-call | tf_op jit(solution)/shard_map/pallas_call | solution.py:621
  35.5 0.3 collective-permute-done.outer_ref
  35.8 0.0 collective-permute-done.1.inner_ref
  35.8 7.9 %shard_map.71 = (f32[4,8,12,8,128]{4,3,2,1,0:T(8,128)S(1)}, f32[64,128]{1,0:T(8,128)S(1)}) custom-call(f32[7,16,8,128]{3,2,1,0:T(8,128)S(1)} %get-tuple-element.10.edge_ref, f32[2,16,16,256]{3,2,1,0:T(8,128)S(1)} %get-tuple-element.11.source_ref, f32[8,10,8,128]{3,2,1,0:T(8,128)S(1)} %collective-permute-done.outer_ref, ...), custom_call_target="tpu_custom_call" | custom-call | tf_op jit(solution)/shard_map/pallas_call | solution.py:631
  43.7 13.7 %all_to_all.27 = f32[64,1,128]{2,1,0:T(1,128)S(1)} all-to-all(f32[64,1,128]{2,1,0:T(1,128)S(1)} %bitcast.7), channel_id=1, replica_groups=mesh['kind'=2,'piece'=4,'lat'=16,'tx'=4] {'piece','lat'}, dimensions={0} | all-to-all | bytes 65536 | tf_op jit(solution)/shard_map/all_to_all | solution.py:643
  57.5 1.4 %shard_map.72 = f32[8,12,8,128]{3,2,1,0:T(8,128)S(1)} custom-call(f32[64,128]{1,0:T(8,128)S(1)} %bitcast.6, f32[8,16,8,128]{3,2,1,0:T(8,128)S(1)} %all_to_all.26.mid_ref.start_ref, f32[4,8,12,8,128]{4,3,2,1,0:T(8,128)S(1)} %get-tuple-element.15.basis_ref), custom_call_target="tpu_custom_call" | custom-call | tf_op jit(solution)/shard_map/pallas_call | solution.py:644
  58.9 17.9 %all_to_all.28.in_ref = f32[8,12,8,128]{3,2,1,0:T(8,128)S(1)} all-to-all(f32[8,12,8,128]{3,2,1,0:T(8,128)S(1)} %shard_map.72), channel_id=1, replica_groups=mesh['kind'=2,'piece'=4,'lat'=16,'tx'=4] {'kind','piece'}, dimensions={0} | all-to-all | bytes 786432 | tf_op jit(solution)/shard_map/all_to_all | solution.py:651
  76.8 0.8 shard_map.73
  77.6 17.1 %all_to_all.29 = f32[4,2,8,128]{3,2,1,0:T(8,128)S(1)} all-to-all(f32[4,2,8,128]{3,2,1,0:T(8,128)S(1)} %get-tuple-element.17), channel_id=1, replica_groups=mesh['kind'=2,'piece'=4,'lat'=16,'tx'=4] {'tx'}, dimensions={0} | all-to-all | bytes 65536 | tf_op jit(solution)/shard_map/all_to_all | solution.py:662
  94.7 0.6 reduce_sum.9
Async XLA Ops:
  0.6 33.7 %copy-start.1 = (f32[1,64,2]{1,2,0:T(2,128)S(1)}, f32[1,64,2]{1,2,0:T(2,128)}, u32[]{:S(2)}) copy-start(f32[1,64,2]{1,2,0:T(2,128)} %param.9) | copy-start | bytes 1540
  0.6 33.9 %copy-start = (s32[1,64]{1,0:T(1,128)S(1)}, s32[1,64]{1,0:T(1,128)}, u32[]{:S(2)}) copy-start(s32[1,64]{1,0:T(1,128)} %rx_ref.1) | copy-start | bytes 772
  27.4 8.4 %collective-permute-start = (f32[8,10,8,128]{3,2,1,0:T(8,128)S(1)}, f32[8,10,8,128]{3,2,1,0:T(8,128)S(1)}, u32[]{:S(2)}, u32[]{:S(2)}) collective-permute-start(f32[8,10,8,128]{3,2,1,0:T(8,128)S(1)} %get-tuple-element.12), channel_id=1, source_target_pairs={{4,8},{12,16},{20,24},{28,32},{36,40},{44,48},{52,56},{8,4},{16,12... | collective-permute-start | bytes 983048 | tf_op jit(solution)/shard_map/ppermute | solution.py:619
  29.3 6.5 %collective-permute-start.1 = (f32[8,10,8,128]{3,2,1,0:T(8,128)S(1)}, f32[8,10,8,128]{3,2,1,0:T(8,128)S(1)}, u32[]{:S(2)}, u32[]{:S(2)}) collective-permute-start(f32[8,10,8,128]{3,2,1,0:T(8,128)S(1)} %get-tuple-element.13), channel_id=1, source_target_pairs={{0,4},{4,0},{8,12},{12,8},{16,20},{20,16},{24,28},{28,24},{32,36},... | collective-permute-start | bytes 983048 | tf_op jit(solution)/shard_map/ppermute | solution.py:618
